TPU v7x, 32 devices: a whole 2x2x4 slice. The times are simulated.
32 devices in a mesh: dp: 16 (over z, x, core), pipe: 2 (over y).
Axes of the slice: x: 2, y: 2, z: 4, core: 2. Of those that a mesh axis runs over, the one named last changes fastest.
Arguments:
- block_input: bfloat16 [2, 4096, 1536], P('pipe', 'dp'), may hold values from -100 to 100
- saved_qkv: bfloat16 [2, 4096, 4608], P('pipe', 'dp'), may hold values from -10 to 10
- cotangent: bfloat16 [2, 4096, 1536], P('pipe', 'dp'), may hold values from -6 to 6
- mod_table: float32 [2, 3, 1536], P('pipe'), may hold values from -3 to 3
- clip_condition: float32 [2, 128, 4608], P('pipe', 'dp'), may hold values from -3 to 3
- clip_frames: int32 [2, 128], P('pipe', 'dp'), may hold values from 0 to 8, as said below
- frame_tokens: int32 [2, 128], P('pipe', 'dp'), may hold values from 2 to 64, as said below
- tile_layout: int32 [2, 32, 2], P('pipe', 'dp'), may hold values from 0 to 1, as said below
- frozen_qkv: bfloat16 [2, 1536, 4608], P('pipe', 'dp'), may hold values from -0.15625 to 0.15625
- frozen_out: bfloat16 [2, 1536, 1536], P('pipe', 'dp'), may hold values from -0.15625 to 0.15625
- adapters: bfloat16 [2, 9216, 128], P('pipe'), may hold values from -0.15625 to 0.15625
Outputs:
- upstream: bfloat16 [2, 4096, 1536], P('pipe', 'dp')
- d_table: float32 [2, 3, 1536], P('pipe')
- d_adapters: float32 [2, 9216, 128], P('pipe', 'dp')
Inputs may be any that keep to these rules, and one draw needn't show every extreme that they name: `clip_frames`: clips are packed in slot order; a slot with 0 frames holds no clip and so does every later slot of that device; the clips of one device hold at most 256 tokens. `frame_tokens`: even. `tile_layout`: every diagonal tile is live.
All inputs are finite; a program needn't handle non-finite values.
Results may differ from a plain program's by a relative error of at most 0.0065.
Values may be sent and summed in bfloat16 or wider, within the bound.
No kernel may reach another device: no remote copies, remote signals or barrier semaphores. Data moves between devices by JAX's collectives and lax.ppermute only.
A program may use at most 128 MiB of HBM per device.

v0:
```python
import jax
import jax.numpy as jnp
from jax import lax
from jax.sharding import PartitionSpec as P

HEAD = 128
TILE = 128


EPSILON = 1e-06
HIGH = lax.Precision.HIGHEST


def passed_along(block, axis, distance):
    devices = range(lax.axis_size(axis))
    route = [((i - distance) % len(devices), i) for i in devices]
    return lax.ppermute(block, axis, route)


def contract_last(left, right):
    return lax.dot_general(
        left, right, (((1,), (1,)), ((), ())), preferred_element_type=jnp.float32
    )


def contract_first(left, right):
    return lax.dot_general(
        left, right, (((0,), (0,)), ((), ())), preferred_element_type=jnp.float32
    )


def on_device(
    block_input,
    saved_qkv,
    cotangent,
    mod_table,
    clip_condition,
    clip_frames,
    frame_tokens,
    tile_layout,
    frozen_qkv,
    frozen_out,
    adapters,
):
    tokens_here = block_input[0]
    rows, width = tokens_here.shape
    saved = saved_qkv[0]
    inner = saved.shape[1] // 3
    heads = inner // HEAD
    slots = clip_frames.shape[1]
    tiles = tile_layout.shape[1]
    adapter_rows = adapters[0]
    down_qkv = adapter_rows[:width]
    up_qkv = adapter_rows[width : width + 3 * inner]
    down_out = adapter_rows[width + 3 * inner : width + 4 * inner]
    up_out = adapter_rows[width + 4 * inner :]
    clip_ends = jnp.cumsum(clip_frames[0] * frame_tokens[0])
    position = jnp.arange(rows, dtype=jnp.int32)
    clip_of = jnp.sum((position[:, None] >= clip_ends[None, :]).astype(jnp.int32), axis=1)
    onehot_clip = (clip_of[:, None] == jnp.arange(slots, dtype=jnp.int32)[None, :]).astype(
        jnp.float32
    )
    modulation = mod_table[0].reshape(1, 3 * width) + jnp.dot(
        onehot_clip, clip_condition[0], precision=HIGH
    )
    shift_rows = modulation[:, :width]
    scale_rows = modulation[:, width : 2 * width]
    gate_rows = modulation[:, 2 * width :]
    inputs_f = tokens_here.astype(jnp.float32)
    centered = inputs_f - jnp.mean(inputs_f, axis=1, keepdims=True)
    inverse = lax.rsqrt(jnp.mean(centered * centered, axis=1, keepdims=True) + EPSILON)
    normed = centered * inverse
    modded = (normed * (1.0 + scale_rows) + shift_rows).astype(jnp.bfloat16)
    tile_onehot = (
        (position // TILE)[:, None] == jnp.arange(tiles, dtype=jnp.int32)[None, :]
    ).astype(jnp.float32)
    live_rows = jnp.dot(tile_onehot, tile_layout[0].astype(jnp.float32), precision=HIGH)
    live_pairs = jnp.dot(live_rows, tile_onehot.T, precision=HIGH) > 0.5
    allowed = live_pairs & (clip_of[:, None] == clip_of[None, :])
    queries = saved[:, :inner].reshape(rows, heads, HEAD)
    key_rows = saved[:, inner : 2 * inner].reshape(rows, heads, HEAD)
    value_rows = saved[:, 2 * inner :].reshape(rows, heads, HEAD)
    factor = HEAD ** (-0.5)
    scores = (
        jnp.einsum("qhd,khd->hqk", queries, key_rows, preferred_element_type=jnp.float32) * factor
    )
    scores = jnp.where(allowed[None], scores, -jnp.inf)
    probs = jax.nn.softmax(scores, axis=2)
    probs_b = probs.astype(jnp.bfloat16)
    attention = (
        jnp.einsum("hqk,khd->qhd", probs_b, value_rows, preferred_element_type=jnp.float32)
        .reshape(rows, inner)
        .astype(jnp.bfloat16)
    )
    out_whole = lax.all_gather(frozen_out[0], "dp", axis=0, tiled=True)
    low_out = jnp.dot(attention, down_out, preferred_element_type=jnp.float32).astype(jnp.bfloat16)
    branch = jnp.dot(attention, out_whole, preferred_element_type=jnp.float32) + contract_last(
        low_out, up_out
    )
    cotangent_f = cotangent[0].astype(jnp.float32)
    gated = (gate_rows * cotangent_f).astype(jnp.bfloat16)
    low_grad_out = jnp.dot(gated, up_out, preferred_element_type=jnp.float32).astype(jnp.bfloat16)
    grad_attention = (
        contract_last(gated, out_whole) + contract_last(low_grad_out, down_out)
    ).astype(jnp.bfloat16)
    grad_heads = grad_attention.reshape(rows, heads, HEAD)
    grad_probs = jnp.einsum(
        "qhd,khd->hqk", grad_heads, value_rows, preferred_element_type=jnp.float32
    )
    delta = jnp.sum(probs * grad_probs, axis=2, keepdims=True)
    grad_scores = (probs * (grad_probs - delta) * factor).astype(jnp.bfloat16)
    grad_query = jnp.einsum(
        "hqk,khd->qhd", grad_scores, key_rows, preferred_element_type=jnp.float32
    ).reshape(rows, inner)
    grad_key = jnp.einsum(
        "hqk,qhd->khd", grad_scores, queries, preferred_element_type=jnp.float32
    ).reshape(rows, inner)
    grad_value = jnp.einsum(
        "hqk,qhd->khd", probs_b, grad_heads, preferred_element_type=jnp.float32
    ).reshape(rows, inner)
    grad_qkv = jnp.concatenate([grad_query, grad_key, grad_value], axis=1).astype(jnp.bfloat16)
    low_in = jnp.dot(modded, down_qkv, preferred_element_type=jnp.float32).astype(jnp.bfloat16)
    low_grad_in = jnp.dot(grad_qkv, up_qkv, preferred_element_type=jnp.float32).astype(jnp.bfloat16)
    frozen_part = contract_last(grad_qkv, lax.all_gather(frozen_qkv[0], "dp", axis=0, tiled=True))
    grad_modded = frozen_part + contract_last(low_grad_in, down_qkv)
    grad_normed = grad_modded * (1.0 + scale_rows)
    grad_input = cotangent_f + inverse * (
        grad_normed
        - jnp.mean(grad_normed, axis=1, keepdims=True)
        - normed * jnp.mean(grad_normed * normed, axis=1, keepdims=True)
    )
    grad_input = grad_input.astype(jnp.bfloat16)
    table_part = jnp.stack(
        [
            jnp.sum(grad_modded, axis=0),
            jnp.sum(grad_modded * normed, axis=0),
            jnp.sum(cotangent_f * branch, axis=0),
        ]
    )
    adapter_part = jnp.concatenate(
        [
            contract_first(modded, low_grad_in),
            contract_first(grad_qkv, low_in),
            contract_first(attention, low_grad_out),
            contract_first(gated, low_out),
        ],
        axis=0,
    )
    replicas = lax.axis_size("dp")
    table_sum = lax.psum(table_part, "dp")
    adapter_sum = lax.psum_scatter(adapter_part, "dp", scatter_dimension=0, tiled=True)
    passed_back = passed_along(grad_input, "pipe", -1)
    return (passed_back[None], (table_sum / replicas)[None], (adapter_sum / replicas)[None])


def solution(mesh):
    placed = (
        P("pipe", "dp", None),
        P("pipe", "dp", None),
        P("pipe", "dp", None),
        P("pipe", None, None),
        P("pipe", "dp", None),
        P("pipe", "dp"),
        P("pipe", "dp"),
        P("pipe", "dp", None),
        P("pipe", "dp", None),
        P("pipe", "dp", None),
        P("pipe", None, None),
    )
    return jax.shard_map(
        on_device,
        mesh=mesh,
        in_specs=placed,
        out_specs=(P("pipe", "dp", None), P("pipe", None, None), P("pipe", "dp", None)),
        check_vma=False,
    )
```

profile of v0, /device:TPU:0, one launch (start us, length us, event | category | flops | bytes accessed | tf_op | source)
XLA Modules:
  0.0 286.5 jit_solution(9345451330626404410)
XLA Ops:
  12.0 2.9 %copy.36 = bf16[1,256,4608]{1,2,0:T(8,128)(2,1)S(1)} copy(bf16[1,256,4608]{2,1,0:T(8,128)(2,1)} %param.12) | data formatting | bytes 4718592 | tf_op args[1]
  16.9 4.3 %fusion.90 = (f32[12,256]{1,0:T(8,128)S(1)}, f32[12,256,256]{1,2,0:T(8,128)}) fusion(pred[256,256]{0,1:T(8,128)(4,1)S(1)} %copy.35, bf16[256,12,128]{0,2,1:T(8,128)(2,1)} %bitcast.129, bf16[256,12,128]{0,2,1:T(8,128)(2,1)} %bitcast.131), kind=kOutput, calls=%fused_computation.113 | convolution fusion | flops 204472576 | bytes 4796416 | tf_op jit(solution)/shard_map/sub | solution.py:88
  21.2 2.3 convolution_convert_fusion
  23.6 1.7 convolution_convert_fusion.3
  25.3 2.0 convolution_add_fusion
  27.6 1.7 convolution_convert_fusion.4
  31.1 35.1 %all-gather.5.cloned.1.call-done = bf16[1,1536,1536]{2,1,0:T(8,128)(2,1)} async-done(((bf16[1,96,1536]{2,1,0:T(8,128)(2,1)}), bf16[1,1536,1536]{2,1,0:T(8,128)(2,1)}) %all-gather.5.cloned.1.call-update) | async-done | bytes 4718608 | tf_op jit(solution)/shard_map/all_gather | solution.py:95
  66.3 4.0 %fusion.6 = f32[256,1536]{1,0:T(8,128)S(1)} fusion(bf16[256,1536]{1,0:T(8,128)(2,1)} %copy-done.8, bf16[1,1536,1536]{2,1,0:T(8,128)(2,1)} %all-gather.5.cloned.1.call-done), kind=kOutput, calls=%fused_computation.8 | convolution fusion | flops 1207959552 | bytes 7077888 | tf_op jit(solution)/shard_map/dot_general | solution.py:21
  70.3 2.2 fusion.10
  72.5 2.3 copy.39
  74.8 3.5 %fusion.91 = f32[12,256,256]{1,2,0:T(8,128)} fusion(bf16[256,12,128]{0,2,1:T(8,128)(2,1)} %bitcast.127, bf16[256,12,128]{0,2,1:T(8,128)(2,1)S(1)} %bitcast.126), kind=kOutput, calls=%fused_computation.114 | convolution fusion | flops 201326592 | bytes 4718592 | tf_op jit(solution)/shard_map/qhd,khd->hqk/dot_general | solution.py:107
  78.3 6.9 %fusion.41 = bf16[12,256,128]{1,2,0:T(8,128)(2,1)} fusion(bf16[256,12,128]{0,2,1:T(8,128)(2,1)} %bitcast.132, f32[12,256,256]{1,2,0:T(8,128)} %fusion.91, f32[12,256,256]{1,2,0:T(8,128)} %get-tuple-element.13, f32[12,256]{1,0:T(8,128)S(1)} %get-tuple-element.12), kind=kOutput, calls=%fused_computation.53 | convolution fusion | flops 207228160 | bytes 7876608 | tf_op jit(solution)/shard_map/hqk,khd->qhd/dot_general | solution.py:112
  85.2 6.9 %fusion.44 = bf16[12,256,128]{1,2,0:T(8,128)(2,1)} fusion(bf16[256,12,128]{0,2,1:T(8,128)(2,1)} %bitcast.130, f32[12,256,256]{1,2,0:T(8,128)} %fusion.91, f32[12,256,256]{1,2,0:T(8,128)} %get-tuple-element.13, f32[12,256]{1,0:T(8,128)S(1)} %get-tuple-element.12), kind=kOutput, calls=%fused_computation.54 | convolution fusion | flops 207228160 | bytes 7876608 | tf_op jit(solution)/shard_map/hqk,qhd->khd/dot_general | solution.py:115
  92.1 2.7 convolution_convert_fusion.1
  96.6 81.2 %all-gather.7.cloned.1.call-done = bf16[1,1536,4608]{2,1,0:T(8,128)(2,1)} async-done(((bf16[1,96,4608]{2,1,0:T(8,128)(2,1)}), bf16[1,1536,4608]{2,1,0:T(8,128)(2,1)}) %all-gather.7.cloned.1.call-update) | async-done | bytes 14155792 | tf_op jit(solution)/shard_map/all_gather | solution.py:124
  177.8 7.5 %fusion.2 = f32[256,1536]{1,0:T(8,128)S(1)} fusion(bf16[1,1536,4608]{2,1,0:T(8,128)(2,1)} %all-gather.7.cloned.1.call-done, bf16[256,1536]{0,1:T(8,128)(2,1)} %bitcast.144, bf16[256,1536]{0,1:T(8,128)(2,1)} %bitcast.140, bf16[256,1536]{0,1:T(8,128)(2,1)S(1)} %bitcast.139), kind=kOutput, calls=%fused_computation.2 | convolution fusion | flops 3630956544 | bytes 18087936 | tf_op jit(solution)/shard_map/dot_general | solution.py:21
  185.3 2.4 fusion.88
  187.8 3.6 %fusion.32 = (bf16[256,1536]{1,0:T(8,128)(2,1)S(1)}, bf16[256,1536]{1,0:T(8,128)(2,1)}) fusion(bf16[1,256,1536]{2,1,0:T(8,128)(2,1)S(1)} %copy-done.3, f32[256,4608]{1,0:T(8,128)} %copy-done.2, f32[256]{0:T(256)S(1)} %add_rsqrt_fusion, f32[256]{0:T(256)S(1)} %broadcast_multiply_fusion.3, f32[256]{0:T(256)S(1)} %get-tuple-element.15, ...), kind=kLoop, calls=%fused_computation.40 | loop fusion | flops 5898240 | bytes 7868416 | tf_op jit(solution)/shard_map/convert_element_type | solution.py:73
  191.3 4.3 %fusion.55 = f32[4608,128]{1,0:T(8,128)} fusion(bf16[256,1536]{1,0:T(8,128)(2,1)S(1)} %get-tuple-element.7, bf16[1,9216,128]{2,1,0:T(8,128)(2,1)} %param.21, bf16[256,1536]{0,1:T(8,128)(2,1)} %bitcast.145, bf16[256,1536]{0,1:T(8,128)(2,1)} %bitcast.141, bf16[256,1536]{0,1:T(8,128)(2,1)} %bitcast.137), kind=kOutput, calls=%fused_computation.65 | convolution fusion | flops 409763840 | bytes 5898240 | tf_op jit(solution)/shard_map/dot_general | solution.py:27
  196.1 6.9 %pad_maximum_fusion = f32[9216,128]{1,0:T(8,128)} fusion(f32[1536,128]{1,0:T(8,128)S(1)} %copy-done.6, f32[1536,128]{1,0:T(8,128)S(1)} %fusion.93, f32[4608,128]{1,0:T(8,128)} %fusion.55, f32[1536,128]{1,0:T(8,128)S(1)} %fusion.92), kind=kLoop, calls=%fused_computation.5 | loop fusion | flops 3538944 | bytes 9437184 | tf_op jit(solution)/shard_map/concatenate | solution.py:140
  204.1 3.8 %fusion.4 = f32[256,1536]{1,0:T(8,128)S(1)} fusion(bf16[256,1536]{0,1:T(8,128)(2,1)S(1)} %bitcast.135, bf16[1,1536,1536]{2,1,0:T(8,128)(2,1)} %all-gather.5.cloned.1.call-done), kind=kOutput, calls=%fused_computation.6 | convolution fusion | flops 1207959552 | bytes 7077888 | tf_op jit(solution)/shard_map/dot_general | solution.py:97
  211.0 59.9 %psum.7 = f32[3,1536]{1,0:T(4,128)S(1)} all-reduce(f32[3,1536]{1,0:T(4,128)S(1)} %pad_maximum_fusion.2), channel_id=1, replica_groups=mesh['dp'=16,'pipe'=2] {'dp'}, use_global_device_ids=true, to_apply=%region_12.13 | all-reduce | flops 4608 | bytes 36864 | tf_op jit(solution)/shard_map/psum | solution.py:150
  271.5 5.9 %reduce-scatter.2.cloned.1.call-done = f32[576,128]{1,0:T(8,128)} async-done(((f32[9216,128]{1,0:T(8,128)}), f32[576,128]{1,0:T(8,128)}) %reduce-scatter.2.cloned.1.call-update) | async-done | bytes 294928 | tf_op jit(solution)/shard_map/reduce_scatter | solution.py:151
  277.4 1.7 multiply_bitcast_fusion
  (70 shorter events, 16.6 us)
Async XLA Ops:
  7.2 18.1 %copy-start = (f32[1,8,4608]{2,1,0:T(8,128)S(1)}, f32[1,8,4608]{2,1,0:T(8,128)}, u32[]{:S(2)}) copy-start(f32[1,8,4608]{2,1,0:T(8,128)} %param.15) | copy-start | bytes 442372
  7.2 59.1 %all-gather.5.cloned.1.call-start = ((), (), s32[]{:S(2)}) async-start(), calls=%async_computation.2 | async-start | bytes 5013504 | tf_op jit(solution)/shard_map/all_gather | solution.py:95
  7.9 169.8 %all-gather.7.cloned.1.call-start = ((), (), s32[]{:S(2)}) async-start(), calls=%async_computation.3 | async-start | bytes 15040512 | tf_op jit(solution)/shard_map/all_gather | solution.py:124
  8.7 268.7 %reduce-scatter.2.cloned.1.call-start = ((), (), s32[]{:S(2)}) async-start(), calls=%async_computation.1 | async-start | bytes 5013504 | tf_op jit(solution)/shard_map/reduce_scatter | solution.py:151
  12.0 2.9 %copy-start.3 = (bf16[1,256,1536]{2,1,0:T(8,128)(2,1)S(1)}, bf16[1,256,1536]{2,1,0:T(8,128)(2,1)}, u32[]{:S(2)}) copy-start(bf16[1,256,1536]{2,1,0:T(8,128)(2,1)} %param.11) | copy-start | bytes 2359300
  16.9 4.3 %copy-start.5 = (bf16[256,1536]{0,1:T(8,128)(2,1)S(1)}, bf16[256,1536]{0,1:T(8,128)(2,1)}, u32[]{:S(2)}) copy-start(bf16[256,1536]{0,1:T(8,128)(2,1)} %get-tuple-element.9) | copy-start | bytes 2359300
  23.6 5.7 %copy-start.10 = (bf16[12,256,128]{1,2,0:T(8,128)(2,1)}, bf16[12,256,128]{1,2,0:T(8,128)(2,1)S(1)}, u32[]{:S(2)}) copy-start(bf16[12,256,128]{1,2,0:T(8,128)(2,1)S(1)} %convolution_convert_fusion) | copy-start | bytes 2359300
  25.3 2.1 copy-start.4
  27.4 2.3 copy-start.2
  27.6 2.2 copy-start.8
  85.2 6.9 %copy-start.7 = (bf16[256,1536]{0,1:T(8,128)(2,1)S(1)}, bf16[256,1536]{0,1:T(8,128)(2,1)}, u32[]{:S(2)}) copy-start(bf16[256,1536]{0,1:T(8,128)(2,1)} %copy.39) | copy-start | bytes 2359300
  92.1 3.6 %copy-start.12 = (bf16[1,9216,128]{2,1,0:T(8,128)(2,1)S(1)}, bf16[1,9216,128]{2,1,0:T(8,128)(2,1)}, u32[]{:S(2)}) copy-start(bf16[1,9216,128]{2,1,0:T(8,128)(2,1)} %param.21) | copy-start | bytes 7077892
  92.1 3.6 %copy-start.13 = (bf16[12,256,128]{1,2,0:T(8,128)(2,1)S(1)}, bf16[12,256,128]{1,2,0:T(8,128)(2,1)}, u32[]{:S(2)}) copy-start(bf16[12,256,128]{1,2,0:T(8,128)(2,1)} %fusion.41) | copy-start | bytes 2359300
  92.1 3.6 %copy-start.15 = (bf16[12,256,128]{1,2,0:T(8,128)(2,1)S(1)}, bf16[12,256,128]{1,2,0:T(8,128)(2,1)}, u32[]{:S(2)}) copy-start(bf16[12,256,128]{1,2,0:T(8,128)(2,1)} %fusion.44) | copy-start | bytes 2359300
  94.9 0.9 copy-start.16
  95.8 82.0 %copy-start.14 = (bf16[12,256,128]{1,2,0:T(8,128)(2,1)S(1)}, bf16[12,256,128]{1,2,0:T(8,128)(2,1)}, u32[]{:S(2)}) copy-start(bf16[12,256,128]{1,2,0:T(8,128)(2,1)} %fusion.41) | copy-start | bytes 2359300
  191.3 4.7 %copy-start.6 = (f32[1536,128]{1,0:T(8,128)S(1)}, f32[1536,128]{1,0:T(8,128)}, u32[]{:S(2)}) copy-start(f32[1536,128]{1,0:T(8,128)} %fusion.94) | copy-start | bytes 2359300
  203.0 1.1 copy-start.11
  204.1 3.8 %copy-start.9 = (bf16[256,1536]{1,0:T(8,128)(2,1)S(1)}, bf16[256,1536]{1,0:T(8,128)(2,1)}, u32[]{:S(2)}) copy-start(bf16[256,1536]{1,0:T(8,128)(2,1)} %get-tuple-element.8) | copy-start | bytes 2359300
  207.9 72.0 %copy-start.1 = (f32[1,8,4608]{2,1,0:T(8,128)S(1)}, f32[1,8,4608]{2,1,0:T(8,128)}, u32[]{:S(2)}) copy-start(f32[1,8,4608]{2,1,0:T(8,128)} %param.15) | copy-start | bytes 442372
  207.9 63.5 %collective-permute-start = (bf16[256,1536]{1,0:T(8,128)(2,1)S(1)}, bf16[256,1536]{1,0:T(8,128)(2,1)S(1)}, u32[]{:S(2)}, u32[]{:S(2)}) collective-permute-start(bf16[256,1536]{1,0:T(8,128)(2,1)S(1)} %copy-done.9), channel_id=1, source_target_pairs={{1,0},{0,1},{3,2},{2,3},{5,4},{4,5},{7,6},{6,7},{9,8},{8,9},{11,10... | collective-permute-start | bytes 2359304 | tf_op jit(solution)/shard_map/ppermute | solution.py:17
Sparse Core Ops, SparseCore 0:
  10.3 55.9 all-gather.4
  68.5 109.1 all-gather.6
  203.1 74.2 reduce-scatter.1
where the time goes:
time: 287 us; the launch traced here: 286 us
  waiting for transfers between devices  124 us (43%)
  matrix products  62.1 us (22%)
  blocking collectives  59.9 us (21%)
  other arithmetic  14.7 us (5%)
  between operations  14 us (5%)
  local copies, waits for them, and re-layouts  10.5 us (4%)
    all_gather x1, waiting for transfers between devices, on_device(): lax.all_gather(frozen_qkv[0], 'dp', axis=0, tiled=True)  81.2 us
    psum x1, blocking collectives, on_device(): table_sum = lax.psum(table_part, 'dp')  59.9 us
    all_gather x1, waiting for transfers between devices, on_device(): out_whole = lax.all_gather(frozen_out[0], 'dp', axis=0, tiled=True)  35.1 us
    dot_general x5, matrix products, contract_last(): lax.dot_general(left, right, (((1,), (1,)), ((), ())), preferred_element_...  17.6 us
    dot_general x1, matrix products, on_device(): jnp.einsum('hqk,qhd->khd', grad_scores, queries, preferred_element_type=j...  6.94 us
    concatenate x1, other arithmetic, on_device(): jnp.concatenate([contract_first(modded, low_grad_in), contract_first(grad...  6.88 us
    dot_general x1, matrix products, on_device(): jnp.einsum('hqk,khd->qhd', grad_scores, key_rows, preferred_element_type=...  6.85 us
    dot_general x4, matrix products, contract_first(): lax.dot_general(left, right, (((0,), (0,)), ((), ())), preferred_element_...  6.4 us
  transfers between devices with their start and end apart: 4, of which 3 were waited for; matrix products, arithmetic and copies ran while one was open for 20% of the time, Pallas kernels for 0%

commit v1 on v0

--- a/solution.py
+++ b/solution.py
@@ -11,12 +11,6 @@
 HIGH = lax.Precision.HIGHEST
 
 
-def passed_along(block, axis, distance):
-    devices = range(lax.axis_size(axis))
-    route = [((i - distance) % len(devices), i) for i in devices]
-    return lax.ppermute(block, axis, route)
-
-
 def contract_last(left, right):
     return lax.dot_general(
         left, right, (((1,), (1,)), ((), ())), preferred_element_type=jnp.float32
@@ -27,6 +21,64 @@
     return lax.dot_general(
         left, right, (((0,), (0,)), ((), ())), preferred_element_type=jnp.float32
     )
+
+
+def swapped(block, bit):
+    devices = range(lax.axis_size("dp"))
+    return lax.ppermute(block, "dp", [(i, i ^ bit) for i in devices])
+
+
+def ring_shifted(block):
+    count = lax.axis_size("dp")
+    return lax.ppermute(block, "dp", [(i, (i + 4) % count) for i in range(count)])
+
+
+def lane_gather(block):
+    me = lax.axis_index("dp")
+    count = lax.axis_size("dp")
+    rows, columns = block.shape
+    whole = jnp.zeros((count // 2 * rows, columns), block.dtype)
+    here = block
+    for step in range(count // 4):
+        if step:
+            here = ring_shifted(here)
+        across = swapped(here, 2)
+        chip = (me - 4 * step + count) % count // 2
+        whole = lax.dynamic_update_slice(whole, here, (chip * rows, 0))
+        whole = lax.dynamic_update_slice(whole, across, ((chip ^ 1) * rows, 0))
+    return whole
+
+
+def interleaved(mine, other, lane, rows):
+    first = jnp.where(lane == 0, mine, other)
+    second = jnp.where(lane == 0, other, mine)
+    columns = mine.shape[1]
+    both = jnp.stack([first.reshape(-1, rows, columns), second.reshape(-1, rows, columns)], axis=1)
+    return both.reshape(-1, columns)
+
+
+def scatter_sum(part):
+    me = lax.axis_index("dp")
+    count = lax.axis_size("dp")
+    rows, columns = part.shape
+    kept = part.reshape(count, rows // count, columns)
+    bit = 1
+    while bit < count:
+        mine = (me // bit) % 2
+        pairs = kept.reshape(-1, 2, rows // count, columns)
+        sent = lax.dynamic_index_in_dim(pairs, 1 - mine, 1, keepdims=False).astype(jnp.bfloat16)
+        kept = lax.dynamic_index_in_dim(pairs, mine, 1, keepdims=False)
+        kept = kept + swapped(sent, bit).astype(jnp.float32)
+        bit *= 2
+    return kept[0]
+
+
+def whole_sum(part):
+    bit = 1
+    while bit < lax.axis_size("dp"):
+        part = part + swapped(part, bit)
+        bit *= 2
+    return part
 
 
 def on_device(
@@ -42,6 +94,7 @@
     frozen_out,
     adapters,
 ):
+    lane = lax.axis_index("dp") % 2
     tokens_here = block_input[0]
     rows, width = tokens_here.shape
     saved = saved_qkv[0]
@@ -54,6 +107,11 @@
     up_qkv = adapter_rows[width : width + 3 * inner]
     down_out = adapter_rows[width + 3 * inner : width + 4 * inner]
     up_out = adapter_rows[width + 4 * inner :]
+
+    lane_out = lane_gather(frozen_out[0])
+    out_whole = interleaved(lane_out, swapped(lane_out, 1), lane, frozen_out.shape[1])
+    lane_qkv = lane_gather(frozen_qkv[0])
+
     clip_ends = jnp.cumsum(clip_frames[0] * frame_tokens[0])
     position = jnp.arange(rows, dtype=jnp.int32)
     clip_of = jnp.sum((position[:, None] >= clip_ends[None, :]).astype(jnp.int32), axis=1)
@@ -92,14 +150,14 @@
         .reshape(rows, inner)
         .astype(jnp.bfloat16)
     )
-    out_whole = lax.all_gather(frozen_out[0], "dp", axis=0, tiled=True)
     low_out = jnp.dot(attention, down_out, preferred_element_type=jnp.float32).astype(jnp.bfloat16)
-    branch = jnp.dot(attention, out_whole, preferred_element_type=jnp.float32) + contract_last(
-        low_out, up_out
-    )
     cotangent_f = cotangent[0].astype(jnp.float32)
     gated = (gate_rows * cotangent_f).astype(jnp.bfloat16)
     low_grad_out = jnp.dot(gated, up_out, preferred_element_type=jnp.float32).astype(jnp.bfloat16)
+    low_in = jnp.dot(modded, down_qkv, preferred_element_type=jnp.float32).astype(jnp.bfloat16)
+    branch = jnp.dot(attention, out_whole, preferred_element_type=jnp.float32) + contract_last(
+        low_out, up_out
+    )
     grad_attention = (
         contract_last(gated, out_whole) + contract_last(low_grad_out, down_out)
     ).astype(jnp.bfloat16)
@@ -119,24 +177,8 @@
         "hqk,qhd->khd", probs_b, grad_heads, preferred_element_type=jnp.float32
     ).reshape(rows, inner)
     grad_qkv = jnp.concatenate([grad_query, grad_key, grad_value], axis=1).astype(jnp.bfloat16)
-    low_in = jnp.dot(modded, down_qkv, preferred_element_type=jnp.float32).astype(jnp.bfloat16)
+    grad_beside = swapped(grad_qkv, 1)
     low_grad_in = jnp.dot(grad_qkv, up_qkv, preferred_element_type=jnp.float32).astype(jnp.bfloat16)
-    frozen_part = contract_last(grad_qkv, lax.all_gather(frozen_qkv[0], "dp", axis=0, tiled=True))
-    grad_modded = frozen_part + contract_last(low_grad_in, down_qkv)
-    grad_normed = grad_modded * (1.0 + scale_rows)
-    grad_input = cotangent_f + inverse * (
-        grad_normed
-        - jnp.mean(grad_normed, axis=1, keepdims=True)
-        - normed * jnp.mean(grad_normed * normed, axis=1, keepdims=True)
-    )
-    grad_input = grad_input.astype(jnp.bfloat16)
-    table_part = jnp.stack(
-        [
-            jnp.sum(grad_modded, axis=0),
-            jnp.sum(grad_modded * normed, axis=0),
-            jnp.sum(cotangent_f * branch, axis=0),
-        ]
-    )
     adapter_part = jnp.concatenate(
         [
             contract_first(modded, low_grad_in),
@@ -147,9 +189,34 @@
         axis=0,
     )
     replicas = lax.axis_size("dp")
-    table_sum = lax.psum(table_part, "dp")
-    adapter_sum = lax.psum_scatter(adapter_part, "dp", scatter_dimension=0, tiled=True)
-    passed_back = passed_along(grad_input, "pipe", -1)
+    adapter_sum = scatter_sum(adapter_part)
+
+    part_rows = frozen_qkv.shape[1]
+    frozen_beside = swapped(contract_last(grad_beside, lane_qkv), 1)
+    frozen_mine = contract_last(grad_qkv, lane_qkv)
+    first = jnp.where(lane == 0, frozen_mine, frozen_beside).reshape(rows, -1, part_rows)
+    second = jnp.where(lane == 0, frozen_beside, frozen_mine).reshape(rows, -1, part_rows)
+    frozen_part = jnp.stack([first, second], axis=2).reshape(rows, width)
+    grad_modded = frozen_part + contract_last(low_grad_in, down_qkv)
+    grad_normed = grad_modded * (1.0 + scale_rows)
+    grad_input = cotangent_f + inverse * (
+        grad_normed
+        - jnp.mean(grad_normed, axis=1, keepdims=True)
+        - normed * jnp.mean(grad_normed * normed, axis=1, keepdims=True)
+    )
+    grad_input = grad_input.astype(jnp.bfloat16)
+    table_part = jnp.stack(
+        [
+            jnp.sum(grad_modded, axis=0),
+            jnp.sum(grad_modded * normed, axis=0),
+            jnp.sum(cotangent_f * branch, axis=0),
+        ]
+    )
+    stages = lax.axis_size("pipe")
+    passed_back = lax.ppermute(
+        grad_input, "pipe", [((i + 1) % stages, i) for i in range(stages)]
+    )
+    table_sum = whole_sum(table_part)
     return (passed_back[None], (table_sum / replicas)[None], (adapter_sum / replicas)[None])
 
 

time: 287 us -> 229 us (0.80)
  blocking collectives: 59.9 us -> 0 us
  waiting for transfers between devices: 124 us -> 79.9 us
  local copies, waits for them, and re-layouts: 10.5 us -> 37.1 us
  starting transfers between devices: 1.66 us -> 26 us
  between operations: 14 us -> 1.48 us
  other arithmetic: 14.7 us -> 21.7 us
    all_gather x2 -> x0, waiting for transfers between devices: 116 us -> none  [the longest x1 81.2 us: on_device(): lax.all_gather(frozen_qkv[0], 'dp', axis=0, tiled=True)]
    ppermute x1 -> x26, waiting for transfers between devices: 0.01 us -> 79.9 us  [the longest x19 42.1 us: swapped(): return lax.ppermute(block, 'dp', [(i, i ^ bit) for i in devices])]
    psum x1 -> x0, blocking collectives: 59.9 us -> none  [on_device(): table_sum = lax.psum(table_part, 'dp')]
    ppermute x1 -> x26, starting transfers between devices: 1.54 us -> 26 us  [the longest x19 19.7 us: swapped(): return lax.ppermute(block, 'dp', [(i, i ^ bit) for i in devices])]
    dynamic_update_slice x0 -> x16, local copies, waits for them, and re-layouts: none -> 14.3 us  [the longest x8 7.63 us: lane_gather(): whole = lax.dynamic_update_slice(whole, across, ((chip ^ 1) * rows, 0))]
    unnamed x36 -> x66, local copies, waits for them, and re-layouts: 5.96 us -> 14.9 us
    reduce_scatter x1 -> x0, waiting for transfers between devices: 5.89 us -> none  [on_device(): lax.psum_scatter(adapter_part, 'dp', scatter_dimension=0, tiled=True)]
    add x0 -> x6, other arithmetic: none -> 3.89 us  [the longest x3 3.83 us: scatter_sum(): kept = kept + swapped(sent, bit).astype(jnp.float32)]
  transfers between devices with their start and end apart: 4 -> 26, of which waited for: 3 -> 12; matrix products, arithmetic and copies ran while one was open for 20% -> 33% of each run, Pallas kernels for 0% -> 0%
where the time goes in v1:
time: 229 us; the launch traced here: 227 us
  waiting for transfers between devices  79.9 us (35%)
  matrix products  61.3 us (27%)
  local copies, waits for them, and re-layouts  37.1 us (16%)
  starting transfers between devices  26 us (11%)
  other arithmetic  21.7 us (9%)
    ppermute x19, waiting for transfers between devices, swapped(): return lax.ppermute(block, 'dp', [(i, i ^ bit) for i in devices])  42.1 us
    ppermute x6, waiting for transfers between devices, ring_shifted(): lax.ppermute(block, 'dp', [(i, (i + 4) % count) for i in range(count)])  31.6 us
    ppermute x19, starting transfers between devices, swapped(): return lax.ppermute(block, 'dp', [(i, i ^ bit) for i in devices])  19.7 us
    dot_general x6, matrix products, contract_last(): lax.dot_general(left, right, (((1,), (1,)), ((), ())), preferred_element_...  16.5 us
    unnamed x66, local copies, waits for them, and re-layouts  14.9 us
    dynamic_update_slice x8, local copies, waits for them, and re-layouts, lane_gather(): whole = lax.dynamic_update_slice(whole, across, ((chip ^ 1) * rows, 0))  7.63 us
    dot_general x4, matrix products, contract_first(): lax.dot_general(left, right, (((0,), (0,)), ((), ())), preferred_element_...  7.57 us
    dot_general x1, matrix products, on_device(): jnp.einsum('hqk,qhd->khd', grad_scores, queries, preferred_element_type=j...  6.73 us
  transfers between devices with their start and end apart: 26, of which 12 were waited for; matrix products, arithmetic and copies ran while one was open for 33% of the time, Pallas kernels for 0%

profile of v1, /device:TPU:0, one launch (start us, length us, event | category | flops | bytes accessed | tf_op | source)
XLA Modules:
  0.0 227.4 jit_solution(18261151623053695995)
XLA Ops:
  0.6 3.0 %collective-permute-start = (bf16[96,1536]{1,0:T(8,128)(2,1)}, bf16[96,1536]{1,0:T(8,128)(2,1)}, u32[]{:S(2)}, u32[]{:S(2)}) collective-permute-start(bf16[96,1536]{1,0:T(8,128)(2,1)} %bitcast.190), channel_id=1, source_target_pairs={{0,4},{2,6},{4,0},{6,2},{8,12},{10,14},{12,8},{14,10},{16,20},{18,... | collective-permute-start | bytes 884744 | tf_op jit(solution)/shard_map/ppermute | solution.py:28
  11.9 2.8 %copy.58 = bf16[1,256,4608]{1,2,0:T(8,128)(2,1)S(1)} copy(bf16[1,256,4608]{2,1,0:T(8,128)(2,1)} %param.12) | data formatting | bytes 4718592 | tf_op args[1]
  16.1 4.4 %fusion.91 = (f32[12,256]{1,0:T(8,128)S(1)}, f32[12,256,256]{1,2,0:T(8,128)}) fusion(pred[256,256]{0,1:T(8,128)(4,1)S(1)} %copy.57, bf16[256,12,128]{0,2,1:T(8,128)(2,1)} %bitcast.173, bf16[256,12,128]{0,2,1:T(8,128)(2,1)} %bitcast.175), kind=kOutput, calls=%fused_computation.143 | convolution fusion | flops 204472576 | bytes 4796416 | tf_op jit(solution)/shard_map/sub | solution.py:146
  32.9 2.5 %fusion.59 = f32[256,1536]{1,0:T(8,128)} fusion(bf16[256,128]{1,0:T(8,128)(2,1)S(1)} %convolution_convert_fusion.4, bf16[1,9216,128]{2,1,0:T(8,128)(2,1)} %param.21), kind=kOutput, calls=%fused_computation.78 | convolution fusion | flops 100663296 | bytes 2031616 | tf_op jit(solution)/shard_map/dot_general | solution.py:15
  40.5 4.6 %collective-permute-done.3 = bf16[96,1536]{1,0:T(8,128)(2,1)S(1)} collective-permute-done((bf16[96,1536]{1,0:T(8,128)(2,1)}, bf16[96,1536]{1,0:T(8,128)(2,1)S(1)}, u32[]{:S(2)}, u32[]{:S(2)}) %collective-permute-start.3) | collective-permute-done | bytes 294944 | tf_op jit(solution)/shard_map/ppermute | solution.py:33
  46.7 7.0 %collective-permute-done.5 = bf16[96,1536]{1,0:T(8,128)(2,1)S(1)} collective-permute-done((bf16[96,1536]{1,0:T(8,128)(2,1)S(1)}, bf16[96,1536]{1,0:T(8,128)(2,1)S(1)}, u32[]{:S(2)}, u32[]{:S(2)}) %collective-permute-start.5) | collective-permute-done | bytes 294944 | tf_op jit(solution)/shard_map/ppermute | solution.py:33
  55.2 5.2 %collective-permute-done.6 = bf16[96,1536]{1,0:T(8,128)(2,1)S(1)} collective-permute-done((bf16[96,1536]{1,0:T(8,128)(2,1)S(1)}, bf16[96,1536]{1,0:T(8,128)(2,1)S(1)}, u32[]{:S(2)}, u32[]{:S(2)}) %collective-permute-start.6) | collective-permute-done | bytes 294944 | tf_op jit(solution)/shard_map/ppermute | solution.py:28
  66.2 20.1 %collective-permute-done.11 = bf16[96,4608]{1,0:T(8,128)(2,1)} collective-permute-done((bf16[96,4608]{1,0:T(8,128)(2,1)}, bf16[96,4608]{1,0:T(8,128)(2,1)}, u32[]{:S(2)}, u32[]{:S(2)}) %collective-permute-start.11) | collective-permute-done | bytes 884768 | tf_op jit(solution)/shard_map/ppermute | solution.py:33
  94.1 3.5 %convolution_convert_fusion.1 = bf16[12,128,256]{2,1,0:T(8,128)(2,1)} fusion(bf16[256,12,128]{0,2,1:T(8,128)(2,1)S(1)} %bitcast.167, f32[12,256,256]{1,2,0:T(8,128)} %get-tuple-element.17, f32[12,256]{1,0:T(8,128)S(1)} %get-tuple-element.16), kind=kOutput, calls=%fused_computation.52 | convolution fusion | flops 203292672 | bytes 4730880 | tf_op jit(solution)/shard_map/hqk,qhd->khd/dot_general | solution.py:176
  97.6 2.3 %fusion.92 = f32[12,256,256]{1,2,0:T(8,128)} fusion(bf16[256,12,128]{0,2,1:T(8,128)(2,1)S(1)} %bitcast.168, bf16[256,12,128]{0,2,1:T(8,128)(2,1)S(1)} %bitcast.166), kind=kOutput, calls=%fused_computation.144 | convolution fusion | flops 201326592 | bytes 4718592 | tf_op jit(solution)/shard_map/qhd,khd->hqk/dot_general | solution.py:165
  99.9 6.7 %fusion.35 = bf16[12,256,128]{1,2,0:T(8,128)(2,1)} fusion(bf16[256,12,128]{0,2,1:T(8,128)(2,1)S(1)} %bitcast.176, f32[12,256,256]{1,2,0:T(8,128)} %fusion.92, f32[12,256,256]{1,2,0:T(8,128)} %get-tuple-element.17, f32[12,256]{1,0:T(8,128)S(1)} %get-tuple-element.16), kind=kOutput, calls=%fused_computation.53 | convolution fusion | flops 207228160 | bytes 7876608 | tf_op jit(solution)/shard_map/hqk,khd->qhd/dot_general | solution.py:170
  106.7 6.7 %fusion.38 = bf16[12,256,128]{1,2,0:T(8,128)(2,1)} fusion(bf16[256,12,128]{0,2,1:T(8,128)(2,1)S(1)} %bitcast.174, f32[12,256,256]{1,2,0:T(8,128)} %fusion.92, f32[12,256,256]{1,2,0:T(8,128)} %get-tuple-element.17, f32[12,256]{1,0:T(8,128)S(1)} %get-tuple-element.16), kind=kOutput, calls=%fused_computation.54 | convolution fusion | flops 207228160 | bytes 7876608 | tf_op jit(solution)/shard_map/hqk,qhd->khd/dot_general | solution.py:173
  124.2 17.4 %collective-permute-done.14 = bf16[96,4608]{1,0:T(8,128)(2,1)S(1)} collective-permute-done((bf16[96,4608]{1,0:T(8,128)(2,1)}, bf16[96,4608]{1,0:T(8,128)(2,1)S(1)}, u32[]{:S(2)}, u32[]{:S(2)}) %collective-permute-start.14) | collective-permute-done | bytes 884768 | tf_op jit(solution)/shard_map/ppermute | solution.py:28
  142.6 5.2 %fusion.93 = f32[256,768]{1,0:T(8,128)S(1)} fusion(bf16[256,4608]{0,1:T(8,128)(2,1)S(1)} %collective-permute-done.15, bf16[768,4608]{1,0:T(8,128)(2,1)} %constant_dynamic-update-slice_fusion), kind=kOutput, calls=%fused_computation.145 | convolution fusion | flops 1811939328 | bytes 10223616 | tf_op jit(solution)/shard_map/dot_general | solution.py:15
  152.2 2.9 %broadcast_select_fusion.3 = (f32[256,768]{1,0:T(8,128)S(1)}, f32[256,768]{1,0:T(8,128)}) fusion(f32[256,768]{1,0:T(8,128)S(1)} %collective-permute-done.16, pred[]{:T(512)S(6)} %eq.65, bf16[768,4608]{1,0:T(8,128)(2,1)S(1)} %copy-done.7, bf16[256,1536]{0,1:T(8,128)(2,1)S(1)} %bitcast.180, bf16[256,1536]{0,1:T(8,128)(2,1)S(1)} %bitcast.188, ...), kind=kOutput, calls=%fused_computation.84 | convolution fusion | flops 1819410432 | bytes 11796481 | tf_op jit(solution)/shard_map/dot_general | solution.py:15
  158.9 2.9 %fusion.88 = (f32[256]{0:T(256)S(1)}, f32[256]{0:T(256)S(1)}, f32[1536]{0:T(1024)S(1)}, f32[1536]{0:T(1024)S(1)}, f32[256,1536]{1,0:T(8,128)S(1)}) fusion(f32[256,4608]{1,0:T(8,128)} %copy-done.3, f32[256]{0:T(256)S(1)} %add_rsqrt_fusion, f32[256]{0:T(256)S(1)} %broadcast_multiply_fusion.2, bf16[1,256,1536]{2,1,0:T(8,128)(2,1)S(1)} %copy-done.5, ...), kind=kOutput, calls=%fused_computation.140 | convolution fusion | flops 105378304 | bytes 5980160 | tf_op jit(solution)/shard_map/dot_general | solution.py:15
  161.9 3.8 %fusion.26 = (bf16[256,1536]{1,0:T(8,128)(2,1)}, bf16[256,1536]{1,0:T(8,128)(2,1)}) fusion(bf16[1,256,1536]{2,1,0:T(8,128)(2,1)S(1)} %copy-done.5, f32[256,4608]{1,0:T(8,128)} %copy-done.3, f32[256]{0:T(256)S(1)} %add_rsqrt_fusion, f32[256]{0:T(256)S(1)} %broadcast_multiply_fusion.2, f32[256]{0:T(256)S(1)} %get-tuple-element.19, ...), kind=kLoop, calls=%fused_computation.39 | loop fusion | flops 5898240 | bytes 7868416 | tf_op jit(solution)/shard_map/convert_element_type | solution.py:131
  165.7 4.6 %fusion.50 = f32[4608,128]{1,0:T(8,128)} fusion(bf16[256,1536]{1,0:T(8,128)(2,1)} %get-tuple-element.7, bf16[1,9216,128]{2,1,0:T(8,128)(2,1)} %param.21, bf16[256,1536]{0,1:T(8,128)(2,1)} %bitcast.177, bf16[256,1536]{0,1:T(8,128)(2,1)} %bitcast.186, bf16[256,1536]{0,1:T(8,128)(2,1)} %bitcast.182), kind=kOutput, calls=%fused_computation.68 | convolution fusion | flops 409763840 | bytes 5898240 | tf_op jit(solution)/shard_map/dot_general | solution.py:21
  170.8 5.5 %pad_maximum_fusion.1 = f32[9216,128]{1,0:T(8,128)S(1)} fusion(f32[1536,128]{1,0:T(8,128)S(1)} %copy-done.16, f32[1536,128]{1,0:T(8,128)S(1)} %copy-done.15, f32[4608,128]{1,0:T(8,128)} %fusion.50, f32[1536,128]{1,0:T(8,128)S(1)} %fusion.94), kind=kLoop, calls=%fused_computation.4 | loop fusion | flops 3538944 | bytes 9437184 | tf_op jit(solution)/shard_map/concatenate | solution.py:182
  180.7 3.8 %fusion.42 = f32[1536]{0:T(1024)S(1)} fusion(f32[256,1536]{1,0:T(8,128)S(1)} %fusion.61, bf16[256,1536]{0,1:T(8,128)(2,1)S(1)} %bitcast.162, bf16[1536,1536]{1,0:T(8,128)(2,1)} %bitcast.149, bf16[1,256,1536]{2,1,0:T(8,128)(2,1)S(1)} %copy-done.9), kind=kOutput, calls=%fused_computation.56 | convolution fusion | flops 1209530880 | bytes 7870464 | tf_op jit(solution)/shard_map/dot_general | solution.py:158
  190.5 12.5 %collective-permute-done.23 = bf16[4,576,128]{2,1,0:T(8,128)(2,1)} collective-permute-done((bf16[4,576,128]{2,1,0:T(8,128)(2,1)}, bf16[4,576,128]{2,1,0:T(8,128)(2,1)}, u32[]{:S(2)}, u32[]{:S(2)}) %collective-permute-start.23) | collective-permute-done | bytes 589856 | tf_op jit(solution)/shard_map/ppermute | solution.py:28
  209.0 4.8 %collective-permute-done.20 = f32[3,1536]{1,0:T(4,128)S(1)} collective-permute-done((f32[3,1536]{1,0:T(4,128)S(1)}, f32[3,1536]{1,0:T(4,128)S(1)}, u32[]{:S(2)}, u32[]{:S(2)}) %collective-permute-start.20) | collective-permute-done | bytes 18464 | tf_op jit(solution)/shard_map/ppermute | solution.py:28
  213.8 2.8 %collective-permute-start.21 = (f32[3,1536]{1,0:T(4,128)S(1)}, f32[3,1536]{1,0:T(4,128)S(1)}, u32[]{:S(2)}, u32[]{:S(2)}) collective-permute-start(f32[3,1536]{1,0:T(4,128)S(1)} %add.225), channel_id=1, source_target_pairs={{0,16},{2,18},{4,20},{6,22},{8,24},{10,26},{12,28},{14,30},{16,0},... | collective-permute-start | bytes 55304 | tf_op jit(solution)/shard_map/ppermute | solution.py:28
  219.2 6.1 %collective-permute-done.17 = bf16[256,1536]{1,0:T(8,128)(2,1)S(1)} collective-permute-done((bf16[256,1536]{1,0:T(8,128)(2,1)S(1)}, bf16[256,1536]{1,0:T(8,128)(2,1)S(1)}, u32[]{:S(2)}, u32[]{:S(2)}) %collective-permute-start.17) | collective-permute-done | bytes 786464 | tf_op jit(solution)/shard_map/ppermute | solution.py:216
  (178 shorter events, 84.7 us)
Async XLA Ops:
  0.6 37.9 %collective-permute-start = (bf16[96,1536]{1,0:T(8,128)(2,1)}, bf16[96,1536]{1,0:T(8,128)(2,1)}, u32[]{:S(2)}, u32[]{:S(2)}) collective-permute-start(bf16[96,1536]{1,0:T(8,128)(2,1)} %bitcast.190), channel_id=1, source_target_pairs={{0,4},{2,6},{4,0},{6,2},{8,12},{10,14},{12,8},{14,10},{16,20},{18,... | collective-permute-start | bytes 884744 | tf_op jit(solution)/shard_map/ppermute | solution.py:28
  3.7 31.8 %collective-permute-start.1 = (bf16[96,1536]{1,0:T(8,128)(2,1)}, bf16[96,1536]{1,0:T(8,128)(2,1)}, u32[]{:S(2)}, u32[]{:S(2)}) collective-permute-start(bf16[96,1536]{1,0:T(8,128)(2,1)} %bitcast.191), channel_id=1, source_target_pairs={{0,8},{2,10},{4,12},{6,14},{8,16},{10,18},{12,20},{14,22},{16,24},... | collective-permute-start | bytes 884744 | tf_op jit(solution)/shard_map/ppermute | solution.py:33
  5.2 58.5 %collective-permute-start.8 = (bf16[96,4608]{1,0:T(8,128)(2,1)}, bf16[96,4608]{1,0:T(8,128)(2,1)}, u32[]{:S(2)}, u32[]{:S(2)}) collective-permute-start(bf16[96,4608]{1,0:T(8,128)(2,1)} %bitcast.171), channel_id=1, source_target_pairs={{0,4},{2,6},{4,0},{6,2},{8,12},{10,14},{12,8},{14,10},{16,20},{18,... | collective-permute-start | bytes 2654216 | tf_op jit(solution)/shard_map/ppermute | solution.py:28
  5.8 56.3 %collective-permute-start.9 = (bf16[96,4608]{1,0:T(8,128)(2,1)}, bf16[96,4608]{1,0:T(8,128)(2,1)}, u32[]{:S(2)}, u32[]{:S(2)}) collective-permute-start(bf16[96,4608]{1,0:T(8,128)(2,1)} %bitcast.172), channel_id=1, source_target_pairs={{0,8},{2,10},{4,12},{6,14},{8,16},{10,18},{12,20},{14,22},{16,24},... | collective-permute-start | bytes 2654216 | tf_op jit(solution)/shard_map/ppermute | solution.py:33
  35.5 9.6 %collective-permute-start.3 = (bf16[96,1536]{1,0:T(8,128)(2,1)}, bf16[96,1536]{1,0:T(8,128)(2,1)S(1)}, u32[]{:S(2)}, u32[]{:S(2)}) collective-permute-start(bf16[96,1536]{1,0:T(8,128)(2,1)} %collective-permute-done.1), channel_id=1, source_target_pairs={{0,8},{2,10},{4,12},{6,14},{8,16},{10,18},{12,20},{14,22},{16,24},... | collective-permute-start | bytes 884744 | tf_op jit(solution)/shard_map/ppermute | solution.py:33
  37.0 9.6 %collective-permute-start.2 = (bf16[96,1536]{1,0:T(8,128)(2,1)}, bf16[96,1536]{1,0:T(8,128)(2,1)S(1)}, u32[]{:S(2)}, u32[]{:S(2)}) collective-permute-start(bf16[96,1536]{1,0:T(8,128)(2,1)} %collective-permute-done.1), channel_id=1, source_target_pairs={{0,4},{2,6},{4,0},{6,2},{8,12},{10,14},{12,8},{14,10},{16,20},{18,... | collective-permute-start | bytes 884744 | tf_op jit(solution)/shard_map/ppermute | solution.py:28
  45.1 8.5 %collective-permute-start.5 = (bf16[96,1536]{1,0:T(8,128)(2,1)S(1)}, bf16[96,1536]{1,0:T(8,128)(2,1)S(1)}, u32[]{:S(2)}, u32[]{:S(2)}) collective-permute-start(bf16[96,1536]{1,0:T(8,128)(2,1)S(1)} %collective-permute-done.3), channel_id=1, source_target_pairs={{0,8},{2,10},{4,12},{6,14},{8,16},{10,18},{12,20},{14,22},{16,24},... | collective-permute-start | bytes 884744 | tf_op jit(solution)/shard_map/ppermute | solution.py:33
  45.1 10.0 %collective-permute-start.4 = (bf16[96,1536]{1,0:T(8,128)(2,1)S(1)}, bf16[96,1536]{1,0:T(8,128)(2,1)S(1)}, u32[]{:S(2)}, u32[]{:S(2)}) collective-permute-start(bf16[96,1536]{1,0:T(8,128)(2,1)S(1)} %collective-permute-done.3), channel_id=1, source_target_pairs={{0,4},{2,6},{4,0},{6,2},{8,12},{10,14},{12,8},{14,10},{16,20},{18,... | collective-permute-start | bytes 884744 | tf_op jit(solution)/shard_map/ppermute | solution.py:28
  53.6 6.7 %collective-permute-start.6 = (bf16[96,1536]{1,0:T(8,128)(2,1)S(1)}, bf16[96,1536]{1,0:T(8,128)(2,1)S(1)}, u32[]{:S(2)}, u32[]{:S(2)}) collective-permute-start(bf16[96,1536]{1,0:T(8,128)(2,1)S(1)} %collective-permute-done.5), channel_id=1, source_target_pairs={{0,4},{2,6},{4,0},{6,2},{8,12},{10,14},{12,8},{14,10},{16,20},{18,... | collective-permute-start | bytes 884744 | tf_op jit(solution)/shard_map/ppermute | solution.py:28
  60.4 27.4 %collective-permute-start.7 = (bf16[768,1536]{1,0:T(8,128)(2,1)S(1)}, bf16[768,1536]{1,0:T(8,128)(2,1)}, u32[]{:S(2)}, u32[]{:S(2)}) collective-permute-start(bf16[768,1536]{1,0:T(8,128)(2,1)S(1)} %constant_dynamic-update-slice_fusion.8), channel_id=1, source_target_pairs={{0,2},{2,0},{4,6},{6,4},{8,10},{10,8},{12,14},{14,12},{16,18},{18,... | collective-permute-start | bytes 7077896 | tf_op jit(solution)/shard_map/ppermute | solution.py:28
  62.1 24.2 %collective-permute-start.11 = (bf16[96,4608]{1,0:T(8,128)(2,1)}, bf16[96,4608]{1,0:T(8,128)(2,1)}, u32[]{:S(2)}, u32[]{:S(2)}) collective-permute-start(bf16[96,4608]{1,0:T(8,128)(2,1)} %collective-permute-done.9), channel_id=1, source_target_pairs={{0,8},{2,10},{4,12},{6,14},{8,16},{10,18},{12,20},{14,22},{16,24},... | collective-permute-start | bytes 2654216 | tf_op jit(solution)/shard_map/ppermute | solution.py:33
  62.2 52.8 %collective-permute-start.10 = (bf16[96,4608]{1,0:T(8,128)(2,1)}, bf16[96,4608]{1,0:T(8,128)(2,1)}, u32[]{:S(2)}, u32[]{:S(2)}) collective-permute-start(bf16[96,4608]{1,0:T(8,128)(2,1)} %collective-permute-done.9), channel_id=1, source_target_pairs={{0,4},{2,6},{4,0},{6,2},{8,12},{10,14},{12,8},{14,10},{16,20},{18,... | collective-permute-start | bytes 2654216 | tf_op jit(solution)/shard_map/ppermute | solution.py:28
  86.3 33.0 %collective-permute-start.13 = (bf16[96,4608]{1,0:T(8,128)(2,1)}, bf16[96,4608]{1,0:T(8,128)(2,1)}, u32[]{:S(2)}, u32[]{:S(2)}) collective-permute-start(bf16[96,4608]{1,0:T(8,128)(2,1)} %collective-permute-done.11), channel_id=1, source_target_pairs={{0,8},{2,10},{4,12},{6,14},{8,16},{10,18},{12,20},{14,22},{16,24},... | collective-permute-start | bytes 2654216 | tf_op jit(solution)/shard_map/ppermute | solution.py:33
  86.3 33.6 %collective-permute-start.12 = (bf16[96,4608]{1,0:T(8,128)(2,1)}, bf16[96,4608]{1,0:T(8,128)(2,1)}, u32[]{:S(2)}, u32[]{:S(2)}) collective-permute-start(bf16[96,4608]{1,0:T(8,128)(2,1)} %collective-permute-done.11), channel_id=1, source_target_pairs={{0,4},{2,6},{4,0},{6,2},{8,12},{10,14},{12,8},{14,10},{16,20},{18,... | collective-permute-start | bytes 2654216 | tf_op jit(solution)/shard_map/ppermute | solution.py:28
  114.9 27.7 %collective-permute-start.15 = (bf16[256,4608]{0,1:T(8,128)(2,1)S(1)}, bf16[256,4608]{0,1:T(8,128)(2,1)S(1)}, u32[]{:S(2)}, u32[]{:S(2)}) collective-permute-start(bf16[256,4608]{0,1:T(8,128)(2,1)S(1)} %pad_maximum_fusion.2), channel_id=1, source_target_pairs={{0,2},{2,0},{4,6},{6,4},{8,10},{10,8},{12,14},{14,12},{16,18},{18,... | collective-permute-start | bytes 7077896 | tf_op jit(solution)/shard_map/ppermute | solution.py:28
  119.3 22.2 %collective-permute-start.14 = (bf16[96,4608]{1,0:T(8,128)(2,1)}, bf16[96,4608]{1,0:T(8,128)(2,1)S(1)}, u32[]{:S(2)}, u32[]{:S(2)}) collective-permute-start(bf16[96,4608]{1,0:T(8,128)(2,1)} %collective-permute-done.13), channel_id=1, source_target_pairs={{0,4},{2,6},{4,0},{6,2},{8,12},{10,14},{12,8},{14,10},{16,20},{18,... | collective-permute-start | bytes 2654216 | tf_op jit(solution)/shard_map/ppermute | solution.py:28
  178.6 6.0 %collective-permute-start.22 = (bf16[8,576,128]{2,1,0:T(8,128)(2,1)S(1)}, bf16[8,576,128]{2,1,0:T(8,128)(2,1)}, u32[]{:S(2)}, u32[]{:S(2)}) collective-permute-start(bf16[8,576,128]{2,1,0:T(8,128)(2,1)S(1)} %fusion.43), channel_id=1, source_target_pairs={{0,2},{2,0},{4,6},{6,4},{8,10},{10,8},{12,14},{14,12},{16,18},{18,... | collective-permute-start | bytes 3538952 | tf_op jit(solution)/shard_map/ppermute | solution.py:28
  187.1 15.9 %collective-permute-start.23 = (bf16[4,576,128]{2,1,0:T(8,128)(2,1)}, bf16[4,576,128]{2,1,0:T(8,128)(2,1)}, u32[]{:S(2)}, u32[]{:S(2)}) collective-permute-start(bf16[4,576,128]{2,1,0:T(8,128)(2,1)} %fusion.54), channel_id=1, source_target_pairs={{0,4},{2,6},{4,0},{6,2},{8,12},{10,14},{12,8},{14,10},{16,20},{18,... | collective-permute-start | bytes 1769480 | tf_op jit(solution)/shard_map/ppermute | solution.py:28
  189.0 16.3 %collective-permute-start.19 = (f32[3,1536]{1,0:T(4,128)S(1)}, f32[3,1536]{1,0:T(4,128)S(1)}, u32[]{:S(2)}, u32[]{:S(2)}) collective-permute-start(f32[3,1536]{1,0:T(4,128)S(1)} %fusion.87), channel_id=1, source_target_pairs={{0,4},{2,6},{4,0},{6,2},{8,12},{10,14},{12,8},{14,10},{16,20},{18,... | collective-permute-start | bytes 55304 | tf_op jit(solution)/shard_map/ppermute | solution.py:28
  205.3 11.2 %collective-permute-start.24 = (bf16[2,576,128]{2,1,0:T(8,128)(2,1)S(1)}, bf16[2,576,128]{2,1,0:T(8,128)(2,1)S(1)}, u32[]{:S(2)}, u32[]{:S(2)}) collective-permute-start(bf16[2,576,128]{2,1,0:T(8,128)(2,1)S(1)} %fusion.71), channel_id=1, source_target_pairs={{0,8},{2,10},{4,12},{6,14},{8,0},{10,2},{12,4},{14,6},{16,24},{18,... | collective-permute-start | bytes 884744 | tf_op jit(solution)/shard_map/ppermute | solution.py:28
  205.4 8.3 %collective-permute-start.20 = (f32[3,1536]{1,0:T(4,128)S(1)}, f32[3,1536]{1,0:T(4,128)S(1)}, u32[]{:S(2)}, u32[]{:S(2)}) collective-permute-start(f32[3,1536]{1,0:T(4,128)S(1)} %fusion.127), channel_id=1, source_target_pairs={{0,8},{2,10},{4,12},{6,14},{8,0},{10,2},{12,4},{14,6},{16,24},{18,... | collective-permute-start | bytes 55304 | tf_op jit(solution)/shard_map/ppermute | solution.py:28
  207.5 17.9 %collective-permute-start.17 = (bf16[256,1536]{1,0:T(8,128)(2,1)S(1)}, bf16[256,1536]{1,0:T(8,128)(2,1)S(1)}, u32[]{:S(2)}, u32[]{:S(2)}) collective-permute-start(bf16[256,1536]{1,0:T(8,128)(2,1)S(1)} %copy-done.24), channel_id=1, source_target_pairs={{1,0},{0,1},{3,2},{2,3},{5,4},{4,5},{7,6},{6,7},{9,8},{8,9},{11,10... | collective-permute-start | bytes 2359304 | tf_op jit(solution)/shard_map/ppermute | solution.py:216
  213.8 4.8 %collective-permute-start.21 = (f32[3,1536]{1,0:T(4,128)S(1)}, f32[3,1536]{1,0:T(4,128)S(1)}, u32[]{:S(2)}, u32[]{:S(2)}) collective-permute-start(f32[3,1536]{1,0:T(4,128)S(1)} %add.225), channel_id=1, source_target_pairs={{0,16},{2,18},{4,20},{6,22},{8,24},{10,26},{12,28},{14,30},{16,0},... | collective-permute-start | bytes 55304 | tf_op jit(solution)/shard_map/ppermute | solution.py:28
  217.7 8.1 %collective-permute-start.25 = (bf16[1,576,128]{2,1,0:T(8,128)(2,1)S(1)}, bf16[1,576,128]{2,1,0:T(8,128)(2,1)S(1)}, u32[]{:S(2)}, u32[]{:S(2)}) collective-permute-start(bf16[1,576,128]{2,1,0:T(8,128)(2,1)S(1)} %dynamic-slice_convert_fusion.2), channel_id=1, source_target_pairs={{0,16},{2,18},{4,20},{6,22},{8,24},{10,26},{12,28},{14,30},{16,0},... | collective-permute-start | bytes 442376 | tf_op jit(solution)/shard_map/ppermute | solution.py:28
  (34 other events, 225.8 us)

commit v2 on v1

--- a/solution.py
+++ b/solution.py
@@ -1,6 +1,8 @@
 import jax
 import jax.numpy as jnp
 from jax import lax
+from jax.experimental import pallas as pl
+from jax.experimental.pallas import tpu as pltpu
 from jax.sharding import PartitionSpec as P
 
 HEAD = 128
@@ -81,7 +83,7 @@
     return part
 
 
-def on_device(
+def on_device_general(
     block_input,
     saved_qkv,
     cotangent,
@@ -220,6 +222,567 @@
     return (passed_back[None], (table_sum / replicas)[None], (adapter_sum / replicas)[None])
 
 
+VMEM_LIMIT = 58 * 1024 * 1024
+PACE = 1.0e6
+F32 = jnp.float32
+BF16 = jnp.bfloat16
+
+
+def dot_nn(left, right):
+    return lax.dot_general(
+        left, right, (((1,), (0,)), ((), ())), preferred_element_type=jnp.float32
+    )
+
+
+def clip_numbers(frames_ref, sizes_ref, position):
+    clip = jnp.zeros_like(position)
+    end = jnp.int32(0)
+    for slot in range(frames_ref.shape[1]):
+        end = end + frames_ref[0, slot] * sizes_ref[0, slot]
+        clip = clip + (position >= end).astype(jnp.int32)
+    return clip
+
+
+def mask_bias(frames_ref, sizes_ref, layout_ref, rows):
+    down = lax.broadcasted_iota(jnp.int32, (rows, 1), 0)
+    across = lax.broadcasted_iota(jnp.int32, (1, rows), 1)
+    same = clip_numbers(frames_ref, sizes_ref, down) == clip_numbers(frames_ref, sizes_ref, across)
+    live = jnp.zeros((rows, rows), jnp.int32)
+    for i in range(rows // TILE):
+        for j in range(rows // TILE):
+            inside = (across // TILE == i) & (down // TILE == j)
+            live = jnp.where(inside, layout_ref[0, i, j], live)
+    return jnp.where(same & (live > 0), 0.0, -jnp.inf).astype(jnp.float32)
+
+
+def pre_kernel(
+    place_ref, frames_ref, sizes_ref, input_ref, cotangent_ref, table_ref, condition_ref, adapters_ref,
+    modded_ref, gated_ref, normed_ref, scale_ref, low_in_ref, low_grad_ref,
+    down_ref, up_ref, sems,
+):
+    rows, width = input_ref.shape
+    slots = condition_ref.shape[0]
+    down = pltpu.make_async_copy(adapters_ref.at[0, :width, :], down_ref, sems.at[0])
+    up = pltpu.make_async_copy(adapters_ref.at[0, adapters_ref.shape[1] - width :, :], up_ref, sems.at[1])
+    down.start()
+    up.start()
+    position = lax.broadcasted_iota(jnp.int32, (rows, 1), 0)
+    clip = clip_numbers(frames_ref, sizes_ref, position)
+    whole = condition_ref[...]
+    high = whole.astype(BF16)
+    rest = whole - high.astype(F32)
+    middle = rest.astype(BF16)
+    low = (rest - middle.astype(F32)).astype(BF16)
+    parts = jnp.concatenate([high.astype(F32), middle.astype(F32), low.astype(F32)], axis=0)
+    lanes = lax.broadcasted_iota(jnp.int32, (rows, 3 * slots), 1) % slots
+    onehot = (clip == lanes).astype(F32).astype(BF16)
+    parts = parts.astype(BF16)
+
+    def modulation(which):
+        columns = slice(which * width, (which + 1) * width)
+        return dot_nn(onehot, parts[:, columns]) + table_ref[which : which + 1, :]
+
+    inputs_f = input_ref[...].astype(F32)
+    centered = inputs_f - jnp.mean(inputs_f, axis=1, keepdims=True)
+    inverse = lax.rsqrt(jnp.mean(centered * centered, axis=1, keepdims=True) + EPSILON)
+    normed = centered * inverse
+    normed_ref[...] = normed
+    scale = 1.0 + modulation(1)
+    scale_ref[...] = scale
+    modded = (normed * scale + modulation(0)).astype(BF16)
+    modded_ref[...] = modded
+    gated = (modulation(2) * cotangent_ref[...].astype(F32)).astype(BF16)
+    gated_ref[...] = gated
+    down.wait()
+    low_in_ref[...] = dot_nn(modded, down_ref[...]).astype(BF16)
+    up.wait()
+    low_grad_ref[...] = dot_nn(gated, up_ref[...]).astype(BF16)
+
+
+def forward_kernel(
+    place_ref, frames_ref, sizes_ref, layout_ref, low_grad_ref, saved_in_ref, gated_in_ref,
+    cotangent_in_ref, adapters_ref, attention_ref, low_out_ref, gate_ref, grad_down_ref, grad_up_ref,
+    bias_ref, level_ref, down_ref, up_ref, saved_ref, gated_ref, cotangent_ref, sems,
+):
+    rows, inner = attention_ref.shape
+    width = up_ref.shape[0]
+    count = adapters_ref.shape[1]
+    down = pltpu.make_async_copy(
+        adapters_ref.at[0, count - width - inner : count - width, :], down_ref, sems.at[0]
+    )
+    up = pltpu.make_async_copy(adapters_ref.at[0, count - width :, :], up_ref, sems.at[1])
+    factor = HEAD ** (-0.5)
+    group = 3
+    held = []
+    for n, start in enumerate(range(0, inner, group * HEAD)):
+        stop = min(start + group * HEAD, inner)
+        for part in range(3):
+            columns = slice(part * inner + start, part * inner + stop)
+            held.append(
+                pltpu.make_async_copy(
+                    saved_in_ref.at[:, columns], saved_ref.at[:, columns], sems.at[4 + 3 * n + part]
+                )
+            )
+    gated_copy = pltpu.make_async_copy(gated_in_ref, gated_ref, sems.at[2])
+    cotangent_copy = pltpu.make_async_copy(cotangent_in_ref, cotangent_ref, sems.at[3])
+    for copy in held + [down, gated_copy, cotangent_copy, up]:
+        copy.start()
+    bias_ref[...] = mask_bias(frames_ref, sizes_ref, layout_ref, rows)
+    for start in range(0, inner // HEAD, group):
+        heads = range(start, min(start + group, inner // HEAD))
+        for copy in held[start // group * 3 : start // group * 3 + 3]:
+            copy.wait()
+        scores = []
+        for head in heads:
+            query = saved_ref[:, head * HEAD : (head + 1) * HEAD]
+            key = saved_ref[:, inner + head * HEAD : inner + (head + 1) * HEAD]
+            scores.append(contract_last(key, query) * factor + bias_ref[...])
+        probs = []
+        for head, score in zip(heads, scores):
+            most = jnp.max(score, axis=0, keepdims=True)
+            raised = jnp.exp(score - most)
+            whole = jnp.sum(raised, axis=0, keepdims=True)
+            level_ref[head : head + 1, :] = most + jnp.log(whole)
+            probs.append((raised * (1.0 / whole)).astype(BF16))
+        for head, prob in zip(heads, probs):
+            value = saved_ref[:, 2 * inner + head * HEAD : 2 * inner + (head + 1) * HEAD]
+            attention_ref[:, head * HEAD : (head + 1) * HEAD] = contract_first(prob, value).astype(BF16)
+    down.wait()
+    attention = attention_ref[...]
+    low_out = dot_nn(attention, down_ref[...]).astype(BF16)
+    low_out_ref[...] = low_out
+    grad_down_ref[...] = contract_first(attention, low_grad_ref[...])
+    gated_copy.wait()
+    grad_up_ref[...] = contract_first(gated_ref[...], low_out)
+    up.wait()
+    cotangent_copy.wait()
+    branch = contract_last(low_out, up_ref[...])
+    gate_ref[...] = jnp.sum(branch * cotangent_ref[...].astype(F32), axis=0, keepdims=True)
+
+
+def layer_of(place_ref, step):
+    ring = place_ref[2]
+    return lax.rem(place_ref[0] - step + ring, ring)
+
+
+def shard_copies(place_ref, shards, whole_ref, sems):
+    copies = []
+    for pieces, flip in zip(shards, (0, 2, 1, 3)):
+        owner = (place_ref[1] ^ flip) * (whole_ref.shape[0] // 4)
+        offset = 0
+        for piece in pieces:
+            start = pl.multiple_of(owner + offset, 16)
+            offset += piece.shape[0]
+            target = whole_ref.at[pl.ds(start, piece.shape[0]), :]
+            copies.append(pltpu.make_async_copy(piece, target, sems.at[len(copies)]))
+    return copies
+
+
+def nested(refs, sizes):
+    refs = list(refs)
+    return [[refs.pop(0) for _ in range(size)] for size in sizes]
+
+
+def backward_kernel(
+    step, sizes,
+    place_ref, low_grad_ref, low_in_ref, bias_ref, level_ref, gate_in_ref, total_in_ref,
+    gated_in_ref, cotangent_in_ref, saved_ref, attention_ref, adapters_ref, *refs,
+):
+    shards = nested(refs, sizes)
+    refs = refs[sum(sizes) :]
+    grad_ref, grad_up_ref, gate_ref, total_ref = refs[:4]
+    whole_ref, held_ref, out_ref, down_ref, up_ref, gated_ref, cotangent_ref, sems = refs[4:]
+    depth, width = whole_ref.shape
+    inner = attention_ref.shape[1]
+    first = pl.multiple_of(layer_of(place_ref, step) * depth, HEAD)
+    layer = pl.ds(first, depth)
+    weights = shard_copies(place_ref, shards, whole_ref, sems)
+    used = len(weights)
+    parts = [pl.ds(pl.multiple_of(part * inner + first, HEAD), depth) for part in range(3)]
+    held = [
+        pltpu.make_async_copy(saved_ref.at[:, parts[part]], held_ref.at[part], sems.at[used + part])
+        for part in range(3)
+    ]
+    others = [
+        pltpu.make_async_copy(gated_in_ref, gated_ref, sems.at[used + 8]),
+        pltpu.make_async_copy(cotangent_in_ref, cotangent_ref, sems.at[used + 9]),
+        pltpu.make_async_copy(attention_ref.at[:, layer], out_ref, sems.at[used + 3]),
+        pltpu.make_async_copy(
+            adapters_ref.at[0, pl.ds(pl.multiple_of(width + 3 * inner + first, HEAD), depth), :],
+            down_ref,
+            sems.at[used + 4],
+        ),
+    ] + [
+        pltpu.make_async_copy(
+            adapters_ref.at[0, pl.ds(pl.multiple_of(width + part * inner + first, HEAD), depth), :],
+            up_ref.at[pl.ds(part * depth, depth), :],
+            sems.at[used + 5 + part],
+        )
+        for part in range(3)
+    ]
+    for copy in held + weights + others:
+        copy.start()
+    factor = HEAD ** (-0.5)
+    heads = range(depth // HEAD)
+    spans = [slice(head * HEAD, (head + 1) * HEAD) for head in heads]
+    for copy in held:
+        copy.wait()
+    probs = []
+    for head in heads:
+        scores = contract_last(held_ref[1, :, spans[head]], held_ref[0, :, spans[head]]) * factor
+        level = level_ref[pl.ds(layer_of(place_ref, step) * len(heads) + head, 1), :]
+        probs.append(jnp.exp(scores + (bias_ref[...] - level)))
+    for copy in weights + others:
+        copy.wait()
+    grad_attention = (
+        contract_last(gated_ref[...], whole_ref[...])
+        + contract_last(low_grad_ref[...], down_ref[...])
+    ).astype(BF16)
+    grad_scores = []
+    for head in heads:
+        grad = grad_attention[:, spans[head]]
+        grad_probs = contract_last(held_ref[2, :, spans[head]], grad)
+        delta = jnp.sum(probs[head] * grad_probs, axis=0, keepdims=True)
+        grad_scores.append((probs[head] * ((grad_probs - delta) * factor)).astype(BF16))
+    for head in heads:
+        grad = grad_attention[:, spans[head]]
+        pieces = (
+            contract_first(grad_scores[head], held_ref[1, :, spans[head]]),
+            dot_nn(grad_scores[head], held_ref[0, :, spans[head]]),
+            dot_nn(probs[head].astype(BF16), grad),
+        )
+        for part, piece in enumerate(pieces):
+            columns = slice(part * depth + head * HEAD, part * depth + (head + 1) * HEAD)
+            grad_ref[:, columns] = piece.astype(BF16)
+    grads = grad_ref[...]
+    grad_up_ref[...] = contract_first(grads, low_in_ref[...])
+    total_ref[...] = total_in_ref[...] + dot_nn(grads, up_ref[...])
+    branch = dot_nn(out_ref[...], whole_ref[...])
+    gate_ref[...] = gate_in_ref[...] + jnp.sum(
+        branch * cotangent_ref[...].astype(F32), axis=0, keepdims=True
+    )
+
+
+def adapter_kernel(
+    ring, place_ref, modded_ref, total_ref, grad_down_ref, grad_up_ref, *refs,
+):
+    layer_refs, (low_ref, sent_ref, kept_ref, whole_ref) = refs[:ring], refs[ring:]
+    width = modded_ref.shape[1]
+    inner = grad_down_ref.shape[0]
+    depth = inner // ring
+    low = total_ref[...].astype(BF16)
+    low_ref[...] = low
+    whole_ref[:width, :] = contract_first(modded_ref[...], low)
+    for step in range(ring):
+        first = layer_of(place_ref, step) * depth
+        for part in range(3):
+            start = pl.multiple_of(width + part * inner + first, HEAD)
+            whole_ref[pl.ds(start, depth), :] = layer_refs[step][part * depth : (part + 1) * depth, :]
+    whole_ref[width + 3 * inner : width + 4 * inner, :] = grad_down_ref[...]
+    whole_ref[width + 4 * inner :, :] = grad_up_ref[...]
+    blocks, block = kept_ref.shape[0], kept_ref.shape[1]
+    lane = place_ref[1] % 2
+    for j in range(blocks):
+        mine = pl.multiple_of((2 * j + lane) * block, 64)
+        other = pl.multiple_of((2 * j + 1 - lane) * block, 64)
+        kept_ref[j] = whole_ref[pl.ds(mine, block), :]
+        sent_ref[j] = whole_ref[pl.ds(other, block), :].astype(BF16)
+
+
+def input_kernel(
+    step, ring, sizes, place_ref, low_ref, *refs,
+):
+    grad_refs, refs = refs[:ring], refs[ring:]
+    normed_ref, scale_ref, adapters_ref = refs[:3]
+    shards = nested(refs[3:], sizes)
+    u_ref, table_ref, whole_ref, near_ref, down_ref, held_ref, sems = refs[3 + sum(sizes) :]
+    depth = whole_ref.shape[0]
+    inner = whole_ref.shape[1] // 3
+    weights = shard_copies(place_ref, shards, whole_ref, sems)
+    used = len(weights)
+    first = pl.multiple_of(layer_of(place_ref, step) * depth, HEAD)
+    others = [
+        pltpu.make_async_copy(adapters_ref.at[0, pl.ds(first, depth), :], down_ref, sems.at[used]),
+        pltpu.make_async_copy(normed_ref.at[:, pl.ds(first, depth)], near_ref.at[0], sems.at[used + 1]),
+        pltpu.make_async_copy(scale_ref.at[:, pl.ds(first, depth)], near_ref.at[1], sems.at[used + 2]),
+    ]
+    held = [
+        pltpu.make_async_copy(grad_refs[n], held_ref.at[n], sems.at[used + 3 + n]) for n in range(ring)
+    ]
+    for copy in weights + held + others:
+        copy.start()
+    for copy in weights + others:
+        copy.wait()
+    total = contract_last(low_ref[...], down_ref[...])
+    for other in range(ring):
+        held[other].wait()
+        start = layer_of(place_ref, other) * depth
+        for part in range(3):
+            columns = pl.ds(pl.multiple_of(part * inner + start, HEAD), depth)
+            total = total + contract_last(
+                held_ref[other, :, part * depth : (part + 1) * depth], whole_ref[:, columns]
+            )
+    u_ref[...] = (total * near_ref[1]).astype(BF16)
+    table_ref[0:1, :] = jnp.sum(total, axis=0, keepdims=True)
+    table_ref[1:2, :] = jnp.sum(total * near_ref[0], axis=0, keepdims=True)
+
+
+def finish_kernel(ring, place_ref, input_ref, cotangent_ref, *refs):
+    u_refs, (out_ref, u_ref) = refs[:ring], refs[ring:]
+    depth = u_refs[0].shape[1]
+    for step in range(ring):
+        layer = pl.ds(pl.multiple_of(layer_of(place_ref, step) * depth, HEAD), depth)
+        u_ref[:, layer] = u_refs[step][...].astype(F32)
+    inputs_f = input_ref[...].astype(F32)
+    centered = inputs_f - jnp.mean(inputs_f, axis=1, keepdims=True)
+    inverse = lax.rsqrt(jnp.mean(centered * centered, axis=1, keepdims=True) + EPSILON)
+    normed = centered * inverse
+    u = u_ref[...]
+    out_ref[...] = (
+        cotangent_ref[...].astype(F32)
+        + inverse
+        * (
+            u
+            - jnp.mean(u, axis=1, keepdims=True)
+            - normed * jnp.mean(u * normed, axis=1, keepdims=True)
+        )
+    ).astype(BF16)
+
+
+def call(kernel, outs, specs, operands, time, scratch=(), name=None):
+    space = {"s": pltpu.SMEM, "v": pltpu.VMEM, "a": pl.ANY}
+    return pl.pallas_call(
+        kernel,
+        out_shape=outs,
+        in_specs=[pl.BlockSpec(memory_space=space[s]) for s in specs],
+        out_specs=[pl.BlockSpec(memory_space=pltpu.VMEM)] * len(outs),
+        scratch_shapes=list(scratch),
+        compiler_params=pltpu.CompilerParams(vmem_limit_bytes=VMEM_LIMIT),
+        cost_estimate=pl.CostEstimate(flops=0, bytes_accessed=int(time * PACE), transcendentals=0),
+        name=name,
+    )(*operands)
+
+
+def shape(*dims, dtype=BF16):
+    return jax.ShapeDtypeStruct(dims, dtype)
+
+
+def gate(value, *events):
+    return lax.optimization_barrier((value, *events))[0]
+
+
+def exchanged_sum(part, event):
+    count = lax.axis_size("dp")
+    total = part
+    for flip in (1, 2, 3):
+        total = total + swapped(part, flip)
+    part = total
+    for distance in range(4, count, 4):
+        route = [(i, (i + distance) % count) for i in range(count)]
+        total = total + gate(lax.ppermute(part, "dp", route), event)
+    return total
+
+
+def on_device(
+    block_input,
+    saved_qkv,
+    cotangent,
+    mod_table,
+    clip_condition,
+    clip_frames,
+    frame_tokens,
+    tile_layout,
+    frozen_qkv,
+    frozen_out,
+    adapters,
+):
+    count = lax.axis_size("dp")
+    depth = 4 * frozen_out.shape[1]
+    if count != 16 or depth % HEAD or depth != 4 * frozen_qkv.shape[1]:
+        return on_device_general(
+            block_input, saved_qkv, cotangent, mod_table, clip_condition, clip_frames,
+            frame_tokens, tile_layout, frozen_qkv, frozen_out, adapters,
+        )
+    ring = count // 4
+    me = lax.axis_index("dp")
+    place = jnp.stack([me // 4, me % 4, jnp.int32(ring)]).astype(jnp.int32)
+    tokens_here, saved, cot = block_input[0], saved_qkv[0], cotangent[0]
+    rows, width = tokens_here.shape
+    inner = saved.shape[1] // 3
+    rank = adapters.shape[2]
+    heads = inner // HEAD
+    stages = lax.axis_size("pipe")
+    before = [((i + 1) % stages, i) for i in range(stages)]
+    clips = [clip_frames, frame_tokens]
+    beside = lambda block: swapped(block, 1)
+    across = lambda block: swapped(block, 2)
+    cut = frozen_qkv.shape[1] // 96 * 64
+
+    out_r, qkv_r = [frozen_out[0]], [frozen_qkv[0]]
+    out_r.append(ring_shifted(out_r[0]))
+    out_x = [across(out_r[0])]
+    out_rc, out_xc, qkv_x, qkv_rc, qkv_xc = [beside(out_r[0])], [], [], [], []
+    modded, gated, normed, scale, low_in, low_grad_out = call(
+        pre_kernel,
+        [shape(rows, width), shape(rows, width), shape(rows, width, dtype=F32),
+         shape(rows, width, dtype=F32), shape(rows, rank), shape(rows, rank)],
+        "sssvvvva",
+        [place, *clips, tokens_here, cot, mod_table[0], clip_condition[0], adapters],
+        4,
+        scratch=[pltpu.VMEM((width, rank), BF16), pltpu.VMEM((width, rank), BF16), pltpu.SemaphoreType.DMA((2,))],
+        name="modulate",
+    )
+    event = low_in
+    out_r.append(ring_shifted(gate(out_r[1], event)))
+    out_x.append(across(gate(out_r[1], event)))
+    out_xc.append(beside(gate(out_x[0], event)))
+    attention, low_out, gate_sum, grad_down_out, grad_up_out, bias, level = call(
+        forward_kernel,
+        [shape(rows, inner), shape(rows, rank), shape(1, width, dtype=F32),
+         shape(inner, rank, dtype=F32), shape(width, rank, dtype=F32),
+         shape(rows, rows, dtype=F32), shape(heads, rows, dtype=F32)],
+        "ssssvaaaa",
+        [gate(place, out_r[1], out_x[0]), *clips, tile_layout, low_grad_out, saved, gated, cot, adapters],
+        6,
+        scratch=[
+            pltpu.VMEM((inner, rank), BF16), pltpu.VMEM((width, rank), BF16),
+            pltpu.VMEM(saved.shape, BF16), pltpu.VMEM((rows, width), BF16),
+            pltpu.VMEM((rows, width), BF16), pltpu.SemaphoreType.DMA((4 + 3 * heads,)),
+        ],
+        name="attend",
+    )
+
+    event = low_out
+
+    def backward(step, gate_sum, total, *waited):
+        shards = ([out_r[step]], [out_x[step]], [out_rc[step]], [out_xc[step]])
+        return call(
+            lambda *refs: backward_kernel(step, [1, 1, 1, 1], *refs),
+            [shape(rows, 3 * depth), shape(3 * depth, rank, dtype=F32),
+             shape(1, width, dtype=F32), shape(rows, rank, dtype=F32)],
+            "svvvvvvaaaaaaaaa",
+            [gate(place, *waited), low_grad_out, low_in, bias, level, gate_sum, total, gated, cot, saved,
+             attention, adapters, *sum(shards, [])],
+            5,
+            scratch=[
+                pltpu.VMEM((depth, width), BF16), pltpu.VMEM((3, rows, depth), BF16),
+                pltpu.VMEM((rows, depth), BF16), pltpu.VMEM((depth, rank), BF16),
+                pltpu.VMEM((3 * depth, rank), BF16), pltpu.VMEM((rows, width), BF16),
+                pltpu.VMEM((rows, width), BF16), pltpu.SemaphoreType.DMA((14,)),
+            ],
+            name=f"backward{step}",
+        )
+
+    total = jnp.zeros((rows, rank), F32)
+    out_r.append(ring_shifted(gate(out_r[2], event)))
+    out_x.append(across(gate(out_r[2], event)))
+    out_rc.append(beside(gate(out_r[1], event)))
+    out_xc.append(beside(gate(out_x[1], event)))
+    grad0, grad_up0, gate_sum, total = backward(0, gate_sum, total, out_r[2], out_x[1], out_xc[0])
+    event = total
+    out_x.append(across(gate(out_r[3], event)))
+    qkv_r.append(ring_shifted(gate(qkv_r[0], event, out_r[3])))
+    qkv_rc.append(beside(gate(qkv_r[0], event)))
+    out_rc.append(beside(gate(out_r[2], event)))
+    out_xc.append(beside(gate(out_x[2], event)))
+    grad1, grad_up1, gate_sum, total = backward(1, gate_sum, total, out_r[3], out_x[2])
+    event = total
+    qkv_x.append(across(gate(qkv_r[0], event, out_x[3])))
+    out_rc.append(beside(gate(out_r[3], event)))
+    out_xc.append(beside(gate(out_x[3], event)))
+    grad2, grad_up2, gate_sum, total = backward(2, gate_sum, total, out_x[3])
+    grad3, grad_up3, gate_sum, total = backward(3, gate_sum, total)
+    event = total
+    grads = [grad0, grad1, grad2, grad3]
+    grad_ups = [grad_up0, grad_up1, grad_up2, grad_up3]
+
+    block = adapters.shape[1] // count
+    low_grad_in, sent, kept = call(
+        lambda *refs: adapter_kernel(ring, *refs),
+        [shape(rows, rank), shape(count // 2, block, rank), shape(count // 2, block, rank, dtype=F32)],
+        "svvvv" + "v" * ring,
+        [place, modded, total, grad_down_out, grad_up_out, *grad_ups],
+        4,
+        scratch=[pltpu.VMEM(adapters.shape[1:], F32)],
+        name="adapt",
+    )
+
+    def project(step, *waited):
+        shards = layers[step]
+        sizes = [len(shard) for shard in shards]
+        return call(
+            lambda *refs: input_kernel(step, ring, sizes, *refs),
+            [shape(rows, depth), shape(2, depth, dtype=F32)],
+            "sv" + "a" * ring + "aaa" + "a" * sum(sizes),
+            [gate(place, *waited), low_grad_in, *grads, normed, scale, adapters, *sum(shards, [])],
+            5,
+            scratch=[
+                pltpu.VMEM((depth, 3 * inner), BF16), pltpu.VMEM((2, rows, depth), F32),
+                pltpu.VMEM((depth, rank), BF16), pltpu.VMEM((ring, rows, 3 * depth), BF16),
+                pltpu.SemaphoreType.DMA((9 + ring,)),
+            ],
+            name=f"project{step}",
+        )
+
+    def halved(kept, bit):
+        mine = (me // bit) % 2
+        pairs = kept.reshape(-1, 2, block, rank)
+        sent = lax.dynamic_index_in_dim(pairs, 1 - mine, 1, keepdims=False).astype(BF16)
+        return lax.dynamic_index_in_dim(pairs, mine, 1, keepdims=False), sent
+
+    sends = lambda u: lax.ppermute(u, "pipe", before)
+    event = low_grad_in
+    qkv_r.append(ring_shifted(gate(qkv_r[1], event)))
+    qkv_x.append(across(gate(qkv_r[1], event)))
+    qkv_rc.append(beside(gate(qkv_r[1], event)))
+    qkv_xc.append(beside(gate(qkv_x[0], event)))
+    arrived = beside(sent)
+    layers = [[[qkv_r[0]], [qkv_x[0]], [qkv_rc[0]], [qkv_xc[0]]]]
+    u0, table0 = project(0, qkv_xc[0])
+    qkv_r.append(ring_shifted(gate(qkv_r[2], u0)))
+    qkv_x.append(across(gate(qkv_r[2], u0)))
+    qkv_rc.append(beside(gate(qkv_r[2], u0)))
+    qkv_xc.append(beside(gate(qkv_x[1], u0)))
+    kept, sent = halved(kept + gate(arrived, u0).astype(F32), 2)
+    next_input = lax.ppermute(gate(tokens_here, u0), "pipe", before)
+    received = [sends(u0)]
+    layers.append([[qkv_r[1]], [qkv_x[1]], [qkv_rc[1]], [qkv_xc[1]]])
+    u1, table1 = project(1, qkv_xc[1], sent)
+    rest = [ring_shifted(gate(qkv_x[2], u1)[:cut]), across(gate(qkv_r[3], u1)[cut:])]
+    qkv_rc.append(beside(gate(qkv_r[3], u1)))
+    qkv_xc.append(beside(gate(qkv_x[2], u1)))
+    arrived = across(gate(sent, u1))
+    next_cot = lax.ppermute(gate(cot, u1), "pipe", before)
+    received.append(sends(u1))
+    layers.append([[qkv_r[2]], [qkv_x[2]], [qkv_rc[2]], [qkv_xc[2]]])
+    u2, table2 = project(2, qkv_xc[2], received[0], next_input)
+    layers.append([[qkv_r[3]], rest, [qkv_rc[3]], [beside(gate(piece, u2)) for piece in rest]])
+    received.append(sends(u2))
+    u3, table3 = project(3, received[1], next_cot)
+    kept, sent = halved(kept + gate(arrived, u2).astype(F32), 4)
+    arrived = swapped(sent, 4)
+    kept, sent = halved(kept + gate(arrived, u3).astype(F32), 8)
+    arrived = swapped(sent, 8)
+    received.append(sends(u3))
+
+    tables = jnp.stack([table0, table1, table2, table3])
+    order = (place[0] - jnp.arange(ring) + ring) % ring
+    tables = jnp.take(tables, order, axis=0).transpose(1, 0, 2).reshape(2, width)
+    table_part = jnp.concatenate([tables, gate_sum], axis=0)
+    (passed_back,) = call(
+        lambda *refs: finish_kernel(ring, *refs),
+        [shape(rows, width)],
+        "svv" + "v" * ring,
+        [place, next_input, next_cot, *received],
+        4,
+        scratch=[pltpu.VMEM((rows, width), F32)],
+        name="finish",
+    )
+    table_sum = exchanged_sum(table_part, passed_back)
+    adapter_sum = (kept + gate(arrived, passed_back).astype(F32))[0]
+    return (passed_back[None], (table_sum / count)[None], (adapter_sum / count)[None])
+
+
 def solution(mesh):
     placed = (
         P("pipe", "dp", None),

time: 229 us -> 177 us (0.77)
  Pallas kernels: 0 us -> 74.3 us
  matrix products: 61.3 us -> 0 us
  waiting for transfers between devices: 79.9 us -> 44.6 us
  local copies, waits for them, and re-layouts: 37.1 us -> 12.9 us
  other arithmetic: 21.7 us -> 5.25 us
  starting transfers between devices: 26 us -> 38.6 us
    pallas_call x0 -> x12, Pallas kernels: none -> 74.3 us  [call(): pl.pallas_call(kernel, out_shape=outs, in_specs=[pl.BlockSpec(memory_spac...]
    dot_general x22 -> x0, matrix products: 56.8 us -> none  [the longest x6 16.5 us: contract_last(): lax.dot_general(left, right, (((1,), (1,)), ((), ())), preferred_element_...]
    ppermute x19 -> x32, waiting for transfers between devices: 42.1 us -> 23.2 us  [swapped(): return lax.ppermute(block, 'dp', [(i, i ^ bit) for i in devices])]
    ppermute x6 -> x7, waiting for transfers between devices: 31.6 us -> 16.5 us  [ring_shifted(): lax.ppermute(block, 'dp', [(i, (i + 4) % count) for i in range(count)])]
    dynamic_update_slice x16 -> x0, local copies, waits for them, and re-layouts: 14.3 us -> none  [the longest x8 7.63 us: lane_gather(): whole = lax.dynamic_update_slice(whole, across, ((chip ^ 1) * rows, 0))]
    ppermute x1 -> x9, starting transfers between devices: 1.5 us -> 13.1 us  [the longest x4 5.13 us: on_device(): sends = lambda u: lax.ppermute(u, 'pipe', before)]
    concatenate x2 -> x1, other arithmetic: 7.03 us -> 0.01 us  [on_device(): table_part = jnp.concatenate([tables, gate_sum], axis=0)]
    unnamed x66 -> x77, local copies, waits for them, and re-layouts: 14.9 us -> 7.94 us
  transfers between devices with their start and end apart: 26 -> 48, of which waited for: 12 -> 14; matrix products, arithmetic and copies ran while one was open for 33% -> 6% of each run, Pallas kernels for 0% -> 42%
where the time goes in v2:
time: 177 us
  Pallas kernels  74.3 us (42%)
  waiting for transfers between devices  44.6 us (25%)
  starting transfers between devices  38.6 us (22%)
  local copies, waits for them, and re-layouts  12.9 us (7%)
  other arithmetic  5.25 us (3%)
    pallas_call x12, Pallas kernels, call(): pl.pallas_call(kernel, out_shape=outs, in_specs=[pl.BlockSpec(memory_spac...  74.3 us
    ppermute x32, waiting for transfers between devices, swapped(): return lax.ppermute(block, 'dp', [(i, i ^ bit) for i in devices])  23.2 us
    ppermute x7, waiting for transfers between devices, ring_shifted(): lax.ppermute(block, 'dp', [(i, (i + 4) % count) for i in range(count)])  16.5 us
    ppermute x32, starting transfers between devices, swapped(): return lax.ppermute(block, 'dp', [(i, i ^ bit) for i in devices])  15.2 us
    ppermute x7, starting transfers between devices, ring_shifted(): lax.ppermute(block, 'dp', [(i, (i + 4) % count) for i in range(count)])  10.2 us
    unnamed x77, local copies, waits for them, and re-layouts  7.94 us
    ppermute x4, starting transfers between devices, on_device(): sends = lambda u: lax.ppermute(u, 'pipe', before)  5.13 us
    ppermute x3, starting transfers between devices, exchanged_sum(): total = total + gate(lax.ppermute(part, 'dp', route), event)  4.88 us
  transfers between devices with their start and end apart: 48, of which 14 were waited for; matrix products, arithmetic and copies ran while one was open for 6% of the time, Pallas kernels for 42%

profile of v2, /device:TPU:0, one launch (start us, length us, event | category | flops | bytes accessed | tf_op | source)
XLA Modules:
  0.0 176.7 jit_solution(12642840690118887574)
XLA Ops:
  0.6 3.1 %collective-permute-start = (bf16[96,1536]{1,0:T(8,128)(2,1)}, bf16[96,1536]{1,0:T(8,128)(2,1)S(1)}, u32[]{:S(2)}, u32[]{:S(2)}) collective-permute-start(bf16[96,1536]{1,0:T(8,128)(2,1)} %bitcast.58), channel_id=1, source_target_pairs={{0,8},{2,10},{4,12},{6,14},{8,16},{10,18},{12,20},{14,22},{16,24},... | collective-permute-start | bytes 884744 | tf_op jit(solution)/shard_map/ppermute | solution.py:35
  7.1 5.3 %modulate.1 = (bf16[256,1536]{1,0:T(8,128)(2,1)}, bf16[256,1536]{1,0:T(8,128)(2,1)}, f32[256,1536]{1,0:T(8,128)}, f32[256,1536]{1,0:T(8,128)}, bf16[256,128]{1,0:T(8,128)(2,1)}, /*index=5*/bf16[256,128]{1,0:T(8,128)(2,1)}) custom-call(s32[3]{0:T(128)} %pad_add_fusion.place_ref.refs_0_, s32[1,8]{1,0:T(1,128)} %frames_ref.3, s32[1,8]{1,0:T(1,128)} %sizes_ref.3, ...), custom_call_target="tpu_custom_call" | custom-call | bytes 4000000 | tf_op jit(solution)/shard_map/modulate/pallas_call | solution.py:554
  15.1 7.9 %attend.1 = (bf16[256,1536]{1,0:T(8,128)(2,1)}, bf16[256,128]{1,0:T(8,128)(2,1)}, f32[1,1536]{1,0:T(1,128)}, f32[1536,128]{1,0:T(8,128)}, f32[1536,128]{1,0:T(8,...) custom-call(s32[3]{0:T(128)} %pad_add_fusion.place_ref.refs_0_, s32[1,8]{1,0:T(1,128)} %frames_ref.3, s32[1,8]{1,0:T(1,128)} %sizes_ref.3, ...), custom_call_target="tpu_custom_call" | custom-call | bytes 6000000 | tf_op jit(solution)/shard_map/attend/pallas_call | solution.py:554
  23.1 1.6 collective-permute-start.3
  27.2 6.1 %backward0.1 = (bf16[256,1152]{1,0:T(8,128)(2,1)}, f32[1152,128]{1,0:T(8,128)}, f32[1,1536]{1,0:T(1,128)}, f32[256,128]{1,0:T(8,128)}) custom-call(s32[3]{0:T(128)} %pad_add_fusion.place_ref.refs_0_, bf16[256,128]{1,0:T(8,128)(2,1)} %get-tuple-element.85.low_grad_ref.refs_1_, bf16[256,128]{1,0:T(8,128)(2,1)} %get-tuple-element.82.refs_2_, ...), custom_call_target="tpu_custom_call" | custom-call | bytes 5000000 | tf_op jit(solution)/shard_map/backward0/pallas_call | solution.py:554
  36.3 6.2 %backward1.1 = (bf16[256,1152]{1,0:T(8,128)(2,1)}, f32[1152,128]{1,0:T(8,128)}, f32[1,1536]{1,0:T(1,128)}, f32[256,128]{1,0:T(8,128)}) custom-call(s32[3]{0:T(128)} %pad_add_fusion.place_ref.refs_0_, bf16[256,128]{1,0:T(8,128)(2,1)} %get-tuple-element.85.low_grad_ref.refs_1_, bf16[256,128]{1,0:T(8,128)(2,1)} %get-tuple-element.82.refs_2_, ...), custom_call_target="tpu_custom_call" | custom-call | bytes 5000000 | tf_op jit(solution)/shard_map/backward1/pallas_call | solution.py:554
  47.5 6.1 %backward2.1 = (bf16[256,1152]{1,0:T(8,128)(2,1)}, f32[1152,128]{1,0:T(8,128)}, f32[1,1536]{1,0:T(1,128)}, f32[256,128]{1,0:T(8,128)}) custom-call(s32[3]{0:T(128)} %pad_add_fusion.place_ref.refs_0_, bf16[256,128]{1,0:T(8,128)(2,1)} %get-tuple-element.85.low_grad_ref.refs_1_, bf16[256,128]{1,0:T(8,128)(2,1)} %get-tuple-element.82.refs_2_, ...), custom_call_target="tpu_custom_call" | custom-call | bytes 5000000 | tf_op jit(solution)/shard_map/backward2/pallas_call | solution.py:554
  54.5 6.1 %backward3.1 = (bf16[256,1152]{1,0:T(8,128)(2,1)}, f32[1152,128]{1,0:T(8,128)}, f32[1,1536]{1,0:T(1,128)}, f32[256,128]{1,0:T(8,128)}) custom-call(s32[3]{0:T(128)} %pad_add_fusion.place_ref.refs_0_, bf16[256,128]{1,0:T(8,128)(2,1)} %get-tuple-element.85.low_grad_ref.refs_1_, bf16[256,128]{1,0:T(8,128)(2,1)} %get-tuple-element.82.refs_2_, ...), custom_call_target="tpu_custom_call" | custom-call | bytes 5000000 | tf_op jit(solution)/shard_map/backward3/pallas_call | solution.py:554
  60.7 5.1 %adapt.1 = (bf16[256,128]{1,0:T(8,128)(2,1)}, bf16[8,576,128]{2,1,0:T(8,128)(2,1)}, f32[8,576,128]{2,1,0:T(8,128)}) custom-call(s32[3]{0:T(128)} %pad_add_fusion.place_ref.refs_0_, bf16[256,1536]{1,0:T(8,128)(2,1)} %get-tuple-element.103.refs_1_, f32[256,128]{1,0:T(8,128)} %get-tuple-element.112.refs_2_, f32[1536,128]{1,0:T(8,128)} %get-tuple-element.113.refs_3_, ...), custom_call_target="tpu_custom_call" | custom-call | bytes 4000000 | tf_op jit(solution)/shard_map/adapt/pallas_call | solution.py:554
  67.0 2.0 %collective-permute-start.27 = (bf16[96,4608]{1,0:T(8,128)(2,1)}, bf16[96,4608]{1,0:T(8,128)(2,1)}, u32[]{:S(2)}, u32[]{:S(2)}) collective-permute-start(bf16[96,4608]{1,0:T(8,128)(2,1)} %collective-permute-done.19.refs_9_), channel_id=1, source_target_pairs={{0,8},{2,10},{4,12},{6,14},{8,16},{10,18},{12,20},{14,22},{16,24},... | collective-permute-start | bytes 2654216 | tf_op jit(solution)/shard_map/ppermute | solution.py:35
  70.5 6.9 %project0.1 = (bf16[256,384]{1,0:T(8,128)(2,1)}, f32[2,384]{1,0:T(2,128)}) custom-call(s32[3]{0:T(128)} %pad_add_fusion.place_ref.refs_0_, bf16[256,128]{1,0:T(8,128)(2,1)} %get-tuple-element.119.refs_1_, bf16[256,1152]{1,0:T(8,128)(2,1)} %get-tuple-element.122.refs_2_, bf16[256,1152]{1,0:T(8,128)(2,1)} %get-tuple-element.123.refs_3_, ...), custom_call_target="tpu_custom_call" | custom-call | bytes 5000000 | tf_op jit(solution)/shard_map/project0/pallas_call | solution.py:554
  77.4 10.9 %collective-permute-done.20.refs_10_ = bf16[96,4608]{1,0:T(8,128)(2,1)S(1)} collective-permute-done((bf16[96,4608]{1,0:T(8,128)(2,1)}, bf16[96,4608]{1,0:T(8,128)(2,1)S(1)}, u32[]{:S(2)}, u32[]{:S(2)}) %collective-permute-start.20) | collective-permute-done | bytes 884768 | tf_op jit(solution)/shard_map/ppermute | solution.py:30
  88.8 1.8 %collective-permute-done.27.refs_9_ = bf16[96,4608]{1,0:T(8,128)(2,1)} collective-permute-done((bf16[96,4608]{1,0:T(8,128)(2,1)}, bf16[96,4608]{1,0:T(8,128)(2,1)}, u32[]{:S(2)}, u32[]{:S(2)}) %collective-permute-start.27) | collective-permute-done | bytes 884768 | tf_op jit(solution)/shard_map/ppermute | solution.py:35
  93.8 1.9 %convert_add_fusion = f32[8,576,128]{2,1,0:T(8,128)S(1)} fusion(f32[8,576,128]{2,1,0:T(8,128)} %get-tuple-element.134, bf16[8,576,128]{2,1,0:T(8,128)(2,1)S(1)} %collective-permute-done.22), kind=kLoop, calls=%fused_computation.1 | loop fusion | flops 1179648 | bytes 5898240 | tf_op jit(solution)/shard_map/add | solution.py:746
  96.5 7.0 %project1.1 = (bf16[256,384]{1,0:T(8,128)(2,1)}, f32[2,384]{1,0:T(2,128)}) custom-call(s32[3]{0:T(128)} %pad_add_fusion.place_ref.refs_0_, bf16[256,128]{1,0:T(8,128)(2,1)} %get-tuple-element.119.refs_1_, bf16[256,1152]{1,0:T(8,128)(2,1)} %get-tuple-element.122.refs_2_, bf16[256,1152]{1,0:T(8,128)(2,1)} %get-tuple-element.123.refs_3_, ...), custom_call_target="tpu_custom_call" | custom-call | bytes 5000000 | tf_op jit(solution)/shard_map/project1/pallas_call | solution.py:554
  103.5 8.0 %collective-permute-done.28.refs_10_ = bf16[96,4608]{1,0:T(8,128)(2,1)} collective-permute-done((bf16[96,4608]{1,0:T(8,128)(2,1)}, bf16[96,4608]{1,0:T(8,128)(2,1)}, u32[]{:S(2)}, u32[]{:S(2)}) %collective-permute-start.28) | collective-permute-done | bytes 884768 | tf_op jit(solution)/shard_map/ppermute | solution.py:30
  114.2 4.7 %collective-permute-done.25.refs_3_ = bf16[256,384]{1,0:T(8,128)(2,1)S(1)} collective-permute-done((bf16[256,384]{1,0:T(8,128)(2,1)S(1)}, bf16[256,384]{1,0:T(8,128)(2,1)S(1)}, u32[]{:S(2)}, u32[]{:S(2)}) %collective-permute-start.25) | collective-permute-done | bytes 196640 | tf_op jit(solution)/shard_map/ppermute | solution.py:733
  120.1 1.6 collective-permute-start.24
  122.2 13.5 %collective-permute-done.33.refs_10_ = bf16[64,4608]{1,0:T(8,128)(2,1)} collective-permute-done((bf16[64,4608]{1,0:T(8,128)(2,1)S(1)}, bf16[64,4608]{1,0:T(8,128)(2,1)}, u32[]{:S(2)}, u32[]{:S(2)}) %collective-permute-start.33) | collective-permute-done | bytes 589856 | tf_op jit(solution)/shard_map/ppermute | solution.py:35
  139.6 6.9 %project2.1 = (bf16[256,384]{1,0:T(8,128)(2,1)}, f32[2,384]{1,0:T(2,128)}) custom-call(s32[3]{0:T(128)} %pad_add_fusion.place_ref.refs_0_, bf16[256,128]{1,0:T(8,128)(2,1)} %get-tuple-element.119.refs_1_, bf16[256,1152]{1,0:T(8,128)(2,1)} %get-tuple-element.122.refs_2_, bf16[256,1152]{1,0:T(8,128)(2,1)} %get-tuple-element.123.refs_3_, ...), custom_call_target="tpu_custom_call" | custom-call | bytes 5000000 | tf_op jit(solution)/shard_map/project2/pallas_call | solution.py:554
  151.4 6.9 %project3.1 = (bf16[256,384]{1,0:T(8,128)(2,1)}, f32[2,384]{1,0:T(2,128)}) custom-call(s32[3]{0:T(128)} %pad_add_fusion.place_ref.refs_0_, bf16[256,128]{1,0:T(8,128)(2,1)} %get-tuple-element.119.refs_1_, bf16[256,1152]{1,0:T(8,128)(2,1)} %get-tuple-element.122.refs_2_, bf16[256,1152]{1,0:T(8,128)(2,1)} %get-tuple-element.123.refs_3_, ...), custom_call_target="tpu_custom_call" | custom-call | bytes 5000000 | tf_op jit(solution)/shard_map/project3/pallas_call | solution.py:554
  164.4 1.6 collective-permute-start.42
  166.1 2.3 %collective-permute-start.43 = (f32[3,1536]{1,0:T(4,128)S(1)}, f32[3,1536]{1,0:T(4,128)S(1)}, u32[]{:S(2)}, u32[]{:S(2)}) collective-permute-start(f32[3,1536]{1,0:T(4,128)S(1)} %add_add_fusion), channel_id=1, source_target_pairs={{0,16},{2,18},{4,20},{6,22},{8,24},{10,26},{12,28},{14,30},{16,0},... | collective-permute-start | bytes 55304 | tf_op jit(solution)/shard_map/ppermute | solution.py:582
  170.0 3.6 %finish.1 = bf16[256,1536]{1,0:T(8,128)(2,1)} custom-call(s32[3]{0:T(128)} %pad_add_fusion.place_ref.refs_0_, bf16[256,1536]{1,0:T(8,128)(2,1)} %copy-done.9, bf16[256,1536]{1,0:T(8,128)(2,1)} %collective-permute-done.24.refs_2_, bf16[256,384]{1,0:T(8,128)(2,1)} %copy-done.29, bf16[256,384]{1,0:T(8,128)(2,1)} %copy-done.30, bf16[256,384]{1,0:T(8,128)(2,1)} %copy-done.31, ...), custom_call_target="tpu_custom_call" | custom-call | bytes 4000000 | tf_op jit(solution)/shard_map/finish/pallas_call | solution.py:554
  (182 shorter events, 48.2 us)
Async XLA Ops:
  0.6 12.3 %collective-permute-start = (bf16[96,1536]{1,0:T(8,128)(2,1)}, bf16[96,1536]{1,0:T(8,128)(2,1)S(1)}, u32[]{:S(2)}, u32[]{:S(2)}) collective-permute-start(bf16[96,1536]{1,0:T(8,128)(2,1)} %bitcast.58), channel_id=1, source_target_pairs={{0,8},{2,10},{4,12},{6,14},{8,16},{10,18},{12,20},{14,22},{16,24},... | collective-permute-start | bytes 884744 | tf_op jit(solution)/shard_map/ppermute | solution.py:35
  3.7 10.9 %collective-permute-start.2 = (bf16[96,1536]{1,0:T(8,128)(2,1)}, bf16[96,1536]{1,0:T(8,128)(2,1)S(1)}, u32[]{:S(2)}, u32[]{:S(2)}) collective-permute-start(bf16[96,1536]{1,0:T(8,128)(2,1)} %bitcast.59), channel_id=1, source_target_pairs={{0,4},{2,6},{4,0},{6,2},{8,12},{10,14},{12,8},{14,10},{16,20},{18,... | collective-permute-start | bytes 884744 | tf_op jit(solution)/shard_map/ppermute | solution.py:30
  14.6 11.7 %collective-permute-start.6 = (bf16[96,1536]{1,0:T(8,128)(2,1)S(1)}, bf16[96,1536]{1,0:T(8,128)(2,1)S(1)}, u32[]{:S(2)}, u32[]{:S(2)}) collective-permute-start(bf16[96,1536]{1,0:T(8,128)(2,1)S(1)} %collective-permute-done.2.refs_13_), channel_id=1, source_target_pairs={{0,2},{2,0},{4,6},{6,4},{8,10},{10,8},{12,14},{14,12},{16,18},{18,... | collective-permute-start | bytes 884744 | tf_op jit(solution)/shard_map/ppermute | solution.py:30
  14.6 11.8 %collective-permute-start.7 = (bf16[96,1536]{1,0:T(8,128)(2,1)S(1)}, bf16[96,1536]{1,0:T(8,128)(2,1)S(1)}, u32[]{:S(2)}, u32[]{:S(2)}) collective-permute-start(bf16[96,1536]{1,0:T(8,128)(2,1)S(1)} %bitcast.61), channel_id=1, source_target_pairs={{0,2},{2,0},{4,6},{6,4},{8,10},{10,8},{12,14},{14,12},{16,18},{18,... | collective-permute-start | bytes 884744 | tf_op jit(solution)/shard_map/ppermute | solution.py:30
  23.1 10.9 %collective-permute-start.3 = (bf16[96,1536]{1,0:T(8,128)(2,1)S(1)}, bf16[96,1536]{1,0:T(8,128)(2,1)S(1)}, u32[]{:S(2)}, u32[]{:S(2)}) collective-permute-start(bf16[96,1536]{1,0:T(8,128)(2,1)S(1)} %collective-permute-done.1.refs_12_), channel_id=1, source_target_pairs={{0,8},{2,10},{4,12},{6,14},{8,16},{10,18},{12,20},{14,22},{16,24},... | collective-permute-start | bytes 884744 | tf_op jit(solution)/shard_map/ppermute | solution.py:35
  24.7 10.7 %collective-permute-start.8 = (bf16[96,1536]{1,0:T(8,128)(2,1)S(1)}, bf16[96,1536]{1,0:T(8,128)(2,1)S(1)}, u32[]{:S(2)}, u32[]{:S(2)}) collective-permute-start(bf16[96,1536]{1,0:T(8,128)(2,1)S(1)} %collective-permute-done.refs_12_), channel_id=1, source_target_pairs={{0,2},{2,0},{4,6},{6,4},{8,10},{10,8},{12,14},{14,12},{16,18},{18,... | collective-permute-start | bytes 884744 | tf_op jit(solution)/shard_map/ppermute | solution.py:30
  42.7 23.0 %collective-permute-start.11 = (bf16[96,4608]{1,0:T(8,128)(2,1)S(1)}, bf16[96,4608]{1,0:T(8,128)(2,1)S(1)}, u32[]{:S(2)}, u32[]{:S(2)}) collective-permute-start(bf16[96,4608]{1,0:T(8,128)(2,1)S(1)} %bitcast.52), channel_id=1, source_target_pairs={{0,4},{2,6},{4,0},{6,2},{8,12},{10,14},{12,8},{14,10},{16,20},{18,... | collective-permute-start | bytes 2654216 | tf_op jit(solution)/shard_map/ppermute | solution.py:30
  43.5 22.8 %collective-permute-start.19 = (bf16[96,4608]{1,0:T(8,128)(2,1)S(1)}, bf16[96,4608]{1,0:T(8,128)(2,1)}, u32[]{:S(2)}, u32[]{:S(2)}) collective-permute-start(bf16[96,4608]{1,0:T(8,128)(2,1)S(1)} %bitcast.53), channel_id=1, source_target_pairs={{0,8},{2,10},{4,12},{6,14},{8,16},{10,18},{12,20},{14,22},{16,24},... | collective-permute-start | bytes 2654216 | tf_op jit(solution)/shard_map/ppermute | solution.py:35
  66.4 21.9 %collective-permute-start.20 = (bf16[96,4608]{1,0:T(8,128)(2,1)}, bf16[96,4608]{1,0:T(8,128)(2,1)S(1)}, u32[]{:S(2)}, u32[]{:S(2)}) collective-permute-start(bf16[96,4608]{1,0:T(8,128)(2,1)} %collective-permute-done.19.refs_9_), channel_id=1, source_target_pairs={{0,4},{2,6},{4,0},{6,2},{8,12},{10,14},{12,8},{14,10},{16,20},{18,... | collective-permute-start | bytes 2654216 | tf_op jit(solution)/shard_map/ppermute | solution.py:30
  67.0 23.6 %collective-permute-start.27 = (bf16[96,4608]{1,0:T(8,128)(2,1)}, bf16[96,4608]{1,0:T(8,128)(2,1)}, u32[]{:S(2)}, u32[]{:S(2)}) collective-permute-start(bf16[96,4608]{1,0:T(8,128)(2,1)} %collective-permute-done.19.refs_9_), channel_id=1, source_target_pairs={{0,8},{2,10},{4,12},{6,14},{8,16},{10,18},{12,20},{14,22},{16,24},... | collective-permute-start | bytes 2654216 | tf_op jit(solution)/shard_map/ppermute | solution.py:35
  69.0 22.9 %collective-permute-start.22 = (bf16[8,576,128]{2,1,0:T(8,128)(2,1)}, bf16[8,576,128]{2,1,0:T(8,128)(2,1)S(1)}, u32[]{:S(2)}, u32[]{:S(2)}) collective-permute-start(bf16[8,576,128]{2,1,0:T(8,128)(2,1)} %get-tuple-element.135), channel_id=1, source_target_pairs={{0,2},{2,0},{4,6},{6,4},{8,10},{10,8},{12,14},{14,12},{16,18},{18,... | collective-permute-start | bytes 3538952 | tf_op jit(solution)/shard_map/ppermute | solution.py:30
  90.6 21.0 %collective-permute-start.28 = (bf16[96,4608]{1,0:T(8,128)(2,1)}, bf16[96,4608]{1,0:T(8,128)(2,1)}, u32[]{:S(2)}, u32[]{:S(2)}) collective-permute-start(bf16[96,4608]{1,0:T(8,128)(2,1)} %collective-permute-done.27.refs_9_), channel_id=1, source_target_pairs={{0,4},{2,6},{4,0},{6,2},{8,12},{10,14},{12,8},{14,10},{16,20},{18,... | collective-permute-start | bytes 2654216 | tf_op jit(solution)/shard_map/ppermute | solution.py:30
  91.9 30.3 %collective-permute-start.30 = (bf16[96,4608]{1,0:T(8,128)(2,1)}, bf16[96,4608]{1,0:T(8,128)(2,1)}, u32[]{:S(2)}, u32[]{:S(2)}) collective-permute-start(bf16[96,4608]{1,0:T(8,128)(2,1)} %collective-permute-done.27.refs_9_), channel_id=1, source_target_pairs={{0,2},{2,0},{4,6},{6,4},{8,10},{10,8},{12,14},{14,12},{16,18},{18,... | collective-permute-start | bytes 2654216 | tf_op jit(solution)/shard_map/ppermute | solution.py:30
  91.9 29.7 %collective-permute-start.32 = (bf16[96,4608]{1,0:T(8,128)(2,1)}, bf16[96,4608]{1,0:T(8,128)(2,1)}, u32[]{:S(2)}, u32[]{:S(2)}) collective-permute-start(bf16[96,4608]{1,0:T(8,128)(2,1)} %collective-permute-done.27.refs_9_), channel_id=1, source_target_pairs={{0,8},{2,10},{4,12},{6,14},{8,16},{10,18},{12,20},{14,22},{16,24},... | collective-permute-start | bytes 2654216 | tf_op jit(solution)/shard_map/ppermute | solution.py:35
  92.2 27.9 %collective-permute-start.18 = (bf16[256,1536]{1,0:T(8,128)(2,1)}, bf16[256,1536]{1,0:T(8,128)(2,1)S(1)}, u32[]{:S(2)}, u32[]{:S(2)}) collective-permute-start(bf16[256,1536]{1,0:T(8,128)(2,1)} %bitcast.56), channel_id=1, source_target_pairs={{1,0},{0,1},{3,2},{2,3},{5,4},{4,5},{7,6},{6,7},{9,8},{8,9},{11,10... | collective-permute-start | bytes 2359304 | tf_op jit(solution)/shard_map/ppermute | solution.py:747
  111.5 26.7 %collective-permute-start.29 = (bf16[96,4608]{1,0:T(8,128)(2,1)}, bf16[96,4608]{1,0:T(8,128)(2,1)}, u32[]{:S(2)}, u32[]{:S(2)}) collective-permute-start(bf16[96,4608]{1,0:T(8,128)(2,1)} %collective-permute-done.28.refs_10_), channel_id=1, source_target_pairs={{0,2},{2,0},{4,6},{6,4},{8,10},{10,8},{12,14},{14,12},{16,18},{18,... | collective-permute-start | bytes 2654216 | tf_op jit(solution)/shard_map/ppermute | solution.py:30
  118.9 16.9 %collective-permute-start.33 = (bf16[64,4608]{1,0:T(8,128)(2,1)S(1)}, bf16[64,4608]{1,0:T(8,128)(2,1)}, u32[]{:S(2)}, u32[]{:S(2)}) collective-permute-start(bf16[64,4608]{1,0:T(8,128)(2,1)S(1)} %slice.6), channel_id=1, source_target_pairs={{0,8},{2,10},{4,12},{6,14},{8,16},{10,18},{12,20},{14,22},{16,24},... | collective-permute-start | bytes 1769480 | tf_op jit(solution)/shard_map/ppermute | solution.py:35
  120.1 26.6 %collective-permute-start.24 = (bf16[256,1536]{1,0:T(8,128)(2,1)S(1)}, bf16[256,1536]{1,0:T(8,128)(2,1)}, u32[]{:S(2)}, u32[]{:S(2)}) collective-permute-start(bf16[256,1536]{1,0:T(8,128)(2,1)S(1)} %bitcast.46), channel_id=1, source_target_pairs={{1,0},{0,1},{3,2},{2,3},{5,4},{4,5},{7,6},{6,7},{9,8},{8,9},{11,10... | collective-permute-start | bytes 2359304 | tf_op jit(solution)/shard_map/ppermute | solution.py:755
  121.7 25.6 %collective-permute-start.45 = (bf16[4,576,128]{2,1,0:T(8,128)(2,1)}, bf16[4,576,128]{2,1,0:T(8,128)(2,1)}, u32[]{:S(2)}, u32[]{:S(2)}) collective-permute-start(bf16[4,576,128]{2,1,0:T(8,128)(2,1)} %fusion), channel_id=1, source_target_pairs={{0,4},{2,6},{4,0},{6,2},{8,12},{10,14},{12,8},{14,10},{16,20},{18,... | collective-permute-start | bytes 1769480 | tf_op jit(solution)/shard_map/ppermute | solution.py:30
  122.2 27.7 %collective-permute-start.35 = (bf16[96,4608]{1,0:T(8,128)(2,1)}, bf16[96,4608]{1,0:T(8,128)(2,1)}, u32[]{:S(2)}, u32[]{:S(2)}) collective-permute-start(bf16[96,4608]{1,0:T(8,128)(2,1)} %collective-permute-done.32.refs_9_), channel_id=1, source_target_pairs={{0,2},{2,0},{4,6},{6,4},{8,10},{10,8},{12,14},{14,12},{16,18},{18,... | collective-permute-start | bytes 2654216 | tf_op jit(solution)/shard_map/ppermute | solution.py:30
  135.7 10.8 %collective-permute-start.26 = (bf16[256,384]{1,0:T(8,128)(2,1)}, bf16[256,384]{1,0:T(8,128)(2,1)S(1)}, u32[]{:S(2)}, u32[]{:S(2)}) collective-permute-start(bf16[256,384]{1,0:T(8,128)(2,1)} %get-tuple-element.138), channel_id=1, source_target_pairs={{1,0},{0,1},{3,2},{2,3},{5,4},{4,5},{7,6},{6,7},{9,8},{8,9},{11,10... | collective-permute-start | bytes 589832 | tf_op jit(solution)/shard_map/ppermute | solution.py:733
  146.7 21.8 %collective-permute-start.31 = (bf16[256,384]{1,0:T(8,128)(2,1)}, bf16[256,384]{1,0:T(8,128)(2,1)S(1)}, u32[]{:S(2)}, u32[]{:S(2)}) collective-permute-start(bf16[256,384]{1,0:T(8,128)(2,1)} %get-tuple-element.143), channel_id=1, source_target_pairs={{1,0},{0,1},{3,2},{2,3},{5,4},{4,5},{7,6},{6,7},{9,8},{8,9},{11,10... | collective-permute-start | bytes 589832 | tf_op jit(solution)/shard_map/ppermute | solution.py:733
  149.8 11.9 %collective-permute-start.46 = (bf16[2,576,128]{2,1,0:T(8,128)(2,1)S(1)}, bf16[2,576,128]{2,1,0:T(8,128)(2,1)S(1)}, u32[]{:S(2)}, u32[]{:S(2)}) collective-permute-start(bf16[2,576,128]{2,1,0:T(8,128)(2,1)S(1)} %fusion.1), channel_id=1, source_target_pairs={{0,8},{2,10},{4,12},{6,14},{8,0},{10,2},{12,4},{14,6},{16,24},{18,... | collective-permute-start | bytes 884744 | tf_op jit(solution)/shard_map/ppermute | solution.py:30
  163.3 11.8 %collective-permute-start.47 = (bf16[1,576,128]{2,1,0:T(8,128)(2,1)S(1)}, bf16[1,576,128]{2,1,0:T(8,128)(2,1)S(1)}, u32[]{:S(2)}, u32[]{:S(2)}) collective-permute-start(bf16[1,576,128]{2,1,0:T(8,128)(2,1)S(1)} %dynamic-slice_convert_fusion.1), channel_id=1, source_target_pairs={{0,16},{2,18},{4,20},{6,22},{8,24},{10,26},{12,28},{14,30},{16,0},... | collective-permute-start | bytes 442376 | tf_op jit(solution)/shard_map/ppermute | solution.py:30
  (62 other events, 397.6 us)

commit v3 on v2

--- a/solution.py
+++ b/solution.py
@@ -490,7 +490,7 @@
 
 
 def input_kernel(
-    step, ring, sizes, place_ref, low_ref, *refs,
+    step, ring, sizes, place_ref, low_ref, table_in_ref, *refs,
 ):
     grad_refs, refs = refs[:ring], refs[ring:]
     normed_ref, scale_ref, adapters_ref = refs[:3]
@@ -501,30 +501,33 @@
     weights = shard_copies(place_ref, shards, whole_ref, sems)
     used = len(weights)
     first = pl.multiple_of(layer_of(place_ref, step) * depth, HEAD)
+    layer = pl.ds(first, depth)
     others = [
-        pltpu.make_async_copy(adapters_ref.at[0, pl.ds(first, depth), :], down_ref, sems.at[used]),
-        pltpu.make_async_copy(normed_ref.at[:, pl.ds(first, depth)], near_ref.at[0], sems.at[used + 1]),
-        pltpu.make_async_copy(scale_ref.at[:, pl.ds(first, depth)], near_ref.at[1], sems.at[used + 2]),
+        pltpu.make_async_copy(adapters_ref.at[0, layer, :], down_ref, sems.at[used]),
+        pltpu.make_async_copy(normed_ref.at[:, layer], near_ref.at[0], sems.at[used + 1]),
+        pltpu.make_async_copy(scale_ref.at[:, layer], near_ref.at[1], sems.at[used + 2]),
     ]
-    held = [
-        pltpu.make_async_copy(grad_refs[n], held_ref.at[n], sems.at[used + 3 + n]) for n in range(ring)
-    ]
-    for copy in weights + held + others:
+    for n in range(ring):
+        start = layer_of(place_ref, n) * depth
+        for part in range(3):
+            columns = pl.ds(pl.multiple_of(part * inner + start, HEAD), depth)
+            others.append(
+                pltpu.make_async_copy(
+                    grad_refs[n].at[:, part * depth : (part + 1) * depth],
+                    held_ref.at[:, columns],
+                    sems.at[used + 3 + 3 * n + part],
+                )
+            )
+    for copy in weights + others:
         copy.start()
     for copy in weights + others:
         copy.wait()
-    total = contract_last(low_ref[...], down_ref[...])
-    for other in range(ring):
-        held[other].wait()
-        start = layer_of(place_ref, other) * depth
-        for part in range(3):
-            columns = pl.ds(pl.multiple_of(part * inner + start, HEAD), depth)
-            total = total + contract_last(
-                held_ref[other, :, part * depth : (part + 1) * depth], whole_ref[:, columns]
-            )
+    total = contract_last(held_ref[...], whole_ref[...])
+    total = total + contract_last(low_ref[...], down_ref[...])
     u_ref[...] = (total * near_ref[1]).astype(BF16)
-    table_ref[0:1, :] = jnp.sum(total, axis=0, keepdims=True)
-    table_ref[1:2, :] = jnp.sum(total * near_ref[0], axis=0, keepdims=True)
+    table_ref[...] = table_in_ref[...]
+    table_ref[0:1, layer] = jnp.sum(total, axis=0, keepdims=True)
+    table_ref[1:2, layer] = jnp.sum(total * near_ref[0], axis=0, keepdims=True)
 
 
 def finish_kernel(ring, place_ref, input_ref, cotangent_ref, *refs):
@@ -616,7 +619,6 @@
     clips = [clip_frames, frame_tokens]
     beside = lambda block: swapped(block, 1)
     across = lambda block: swapped(block, 2)
-    cut = frozen_qkv.shape[1] // 96 * 64
 
     out_r, qkv_r = [frozen_out[0]], [frozen_qkv[0]]
     out_r.append(ring_shifted(out_r[0]))
@@ -633,6 +635,7 @@
         name="modulate",
     )
     event = low_in
+    next_input = lax.ppermute(gate(tokens_here, event), "pipe", before)
     out_r.append(ring_shifted(gate(out_r[1], event)))
     out_x.append(across(gate(out_r[1], event)))
     out_xc.append(beside(gate(out_x[0], event)))
@@ -688,10 +691,11 @@
     grad1, grad_up1, gate_sum, total = backward(1, gate_sum, total, out_r[3], out_x[2])
     event = total
     qkv_x.append(across(gate(qkv_r[0], event, out_x[3])))
+    next_cot = lax.ppermute(gate(cot, event), "pipe", before)
     out_rc.append(beside(gate(out_r[3], event)))
     out_xc.append(beside(gate(out_x[3], event)))
     grad2, grad_up2, gate_sum, total = backward(2, gate_sum, total, out_x[3])
-    grad3, grad_up3, gate_sum, total = backward(3, gate_sum, total)
+    grad3, grad_up3, gate_sum, total = backward(3, gate_sum, total, next_input)
     event = total
     grads = [grad0, grad1, grad2, grad3]
     grad_ups = [grad_up0, grad_up1, grad_up2, grad_up3]
@@ -712,14 +716,14 @@
         sizes = [len(shard) for shard in shards]
         return call(
             lambda *refs: input_kernel(step, ring, sizes, *refs),
-            [shape(rows, depth), shape(2, depth, dtype=F32)],
-            "sv" + "a" * ring + "aaa" + "a" * sum(sizes),
-            [gate(place, *waited), low_grad_in, *grads, normed, scale, adapters, *sum(shards, [])],
+            [shape(rows, depth), shape(3, width, dtype=F32)],
+            "svv" + "a" * ring + "aaa" + "a" * sum(sizes),
+            [gate(place, *waited), low_grad_in, table, *grads, normed, scale, adapters, *sum(shards, [])],
             5,
             scratch=[
                 pltpu.VMEM((depth, 3 * inner), BF16), pltpu.VMEM((2, rows, depth), F32),
-                pltpu.VMEM((depth, rank), BF16), pltpu.VMEM((ring, rows, 3 * depth), BF16),
-                pltpu.SemaphoreType.DMA((9 + ring,)),
+                pltpu.VMEM((depth, rank), BF16), pltpu.VMEM((rows, 3 * inner), BF16),
+                pltpu.SemaphoreType.DMA((9 + 3 * ring,)),
             ],
             name=f"project{step}",
         )
@@ -738,37 +742,32 @@
     qkv_xc.append(beside(gate(qkv_x[0], event)))
     arrived = beside(sent)
     layers = [[[qkv_r[0]], [qkv_x[0]], [qkv_rc[0]], [qkv_xc[0]]]]
-    u0, table0 = project(0, qkv_xc[0])
+    table = jnp.concatenate([jnp.zeros((2, width), F32), gate_sum], axis=0)
+    u0, table = project(0, qkv_xc[0], next_cot)
     qkv_r.append(ring_shifted(gate(qkv_r[2], u0)))
     qkv_x.append(across(gate(qkv_r[2], u0)))
     qkv_rc.append(beside(gate(qkv_r[2], u0)))
     qkv_xc.append(beside(gate(qkv_x[1], u0)))
     kept, sent = halved(kept + gate(arrived, u0).astype(F32), 2)
-    next_input = lax.ppermute(gate(tokens_here, u0), "pipe", before)
     received = [sends(u0)]
     layers.append([[qkv_r[1]], [qkv_x[1]], [qkv_rc[1]], [qkv_xc[1]]])
-    u1, table1 = project(1, qkv_xc[1], sent)
-    rest = [ring_shifted(gate(qkv_x[2], u1)[:cut]), across(gate(qkv_r[3], u1)[cut:])]
+    u1, table = project(1, qkv_xc[1], sent, received[0])
+    rest = [ring_shifted(gate(qkv_x[2], u1))]
     qkv_rc.append(beside(gate(qkv_r[3], u1)))
     qkv_xc.append(beside(gate(qkv_x[2], u1)))
     arrived = across(gate(sent, u1))
-    next_cot = lax.ppermute(gate(cot, u1), "pipe", before)
     received.append(sends(u1))
     layers.append([[qkv_r[2]], [qkv_x[2]], [qkv_rc[2]], [qkv_xc[2]]])
-    u2, table2 = project(2, qkv_xc[2], received[0], next_input)
+    u2, table = project(2, qkv_xc[2], received[1])
     layers.append([[qkv_r[3]], rest, [qkv_rc[3]], [beside(gate(piece, u2)) for piece in rest]])
     received.append(sends(u2))
-    u3, table3 = project(3, received[1], next_cot)
+    u3, table = project(3)
     kept, sent = halved(kept + gate(arrived, u2).astype(F32), 4)
     arrived = swapped(sent, 4)
     kept, sent = halved(kept + gate(arrived, u3).astype(F32), 8)
     arrived = swapped(sent, 8)
     received.append(sends(u3))
 
-    tables = jnp.stack([table0, table1, table2, table3])
-    order = (place[0] - jnp.arange(ring) + ring) % ring
-    tables = jnp.take(tables, order, axis=0).transpose(1, 0, 2).reshape(2, width)
-    table_part = jnp.concatenate([tables, gate_sum], axis=0)
     (passed_back,) = call(
         lambda *refs: finish_kernel(ring, *refs),
         [shape(rows, width)],
@@ -778,7 +777,7 @@
         scratch=[pltpu.VMEM((rows, width), F32)],
         name="finish",
     )
-    table_sum = exchanged_sum(table_part, passed_back)
+    table_sum = exchanged_sum(table, passed_back)
     adapter_sum = (kept + gate(arrived, passed_back).astype(F32))[0]
     return (passed_back[None], (table_sum / count)[None], (adapter_sum / count)[None])
 

time: 177 us -> 164 us (0.927)
  starting transfers between devices: 38.6 us -> 34.4 us
  Pallas kernels: 74.3 us -> 71.2 us
  local copies, waits for them, and re-layouts: 12.9 us -> 10.1 us
  waiting for transfers between devices: 44.6 us -> 42.4 us
    ppermute x7, waiting for transfers between devices: 16.5 us -> 10.7 us  [ring_shifted(): lax.ppermute(block, 'dp', [(i, (i + 4) % count) for i in range(count)])]
    pallas_call x12, Pallas kernels: 74.3 us -> 71.2 us  [call(): pl.pallas_call(kernel, out_shape=outs, in_specs=[pl.BlockSpec(memory_spac...]
    ppermute x4, waiting for transfers between devices: 4.7 us -> 7.65 us  [on_device(): sends = lambda u: lax.ppermute(u, 'pipe', before)]
    ppermute x32 -> x30, starting transfers between devices: 15.2 us -> 12.5 us  [swapped(): return lax.ppermute(block, 'dp', [(i, i ^ bit) for i in devices])]
    slice x2 -> x0, local copies, waits for them, and re-layouts: 2.08 us -> none  [the longest x1 1.1 us: on_device(): gate(qkv_x[2], u1)[:cut]]
    unnamed x77 -> x62, local copies, waits for them, and re-layouts: 7.94 us -> 8.62 us
    ppermute x32 -> x30, waiting for transfers between devices: 23.2 us -> 23.7 us  [swapped(): return lax.ppermute(block, 'dp', [(i, i ^ bit) for i in devices])]
  transfers between devices with their start and end apart: 48 -> 46, of which waited for: 14 -> 17; matrix products, arithmetic and copies ran while one was open for 6% -> 4% of each run, Pallas kernels for 42% -> 44%
where the time goes in v3:
time: 164 us
  Pallas kernels  71.2 us (43%)
  waiting for transfers between devices  42.4 us (26%)
  starting transfers between devices  34.4 us (21%)
  local copies, waits for them, and re-layouts  10.1 us (6%)
  other arithmetic  4.41 us (3%)
    pallas_call x12, Pallas kernels, call(): pl.pallas_call(kernel, out_shape=outs, in_specs=[pl.BlockSpec(memory_spac...  71.2 us
    ppermute x30, waiting for transfers between devices, swapped(): return lax.ppermute(block, 'dp', [(i, i ^ bit) for i in devices])  23.7 us
    ppermute x30, starting transfers between devices, swapped(): return lax.ppermute(block, 'dp', [(i, i ^ bit) for i in devices])  12.5 us
    ppermute x7, waiting for transfers between devices, ring_shifted(): lax.ppermute(block, 'dp', [(i, (i + 4) % count) for i in range(count)])  10.7 us
    ppermute x7, starting transfers between devices, ring_shifted(): lax.ppermute(block, 'dp', [(i, (i + 4) % count) for i in range(count)])  10.5 us
    unnamed x62, local copies, waits for them, and re-layouts  8.62 us
    ppermute x4, waiting for transfers between devices, on_device(): sends = lambda u: lax.ppermute(u, 'pipe', before)  7.65 us
    ppermute x4, starting transfers between devices, on_device(): sends = lambda u: lax.ppermute(u, 'pipe', before)  5.06 us
  transfers between devices with their start and end apart: 46, of which 17 were waited for; matrix products, arithmetic and copies ran while one was open for 4% of the time, Pallas kernels for 44%

profile of v3, /device:TPU:0, one launch (start us, length us, event | category | flops | bytes accessed | tf_op | source)
XLA Modules:
  0.0 163.6 jit_solution(8913799322604478319)
XLA Ops:
  0.6 3.1 %collective-permute-start.1 = (bf16[96,1536]{1,0:T(8,128)(2,1)}, bf16[96,1536]{1,0:T(8,128)(2,1)S(1)}, u32[]{:S(2)}, u32[]{:S(2)}) collective-permute-start(bf16[96,1536]{1,0:T(8,128)(2,1)} %bitcast.51), channel_id=1, source_target_pairs={{0,8},{2,10},{4,12},{6,14},{8,16},{10,18},{12,20},{14,22},{16,24},... | collective-permute-start | bytes 884744 | tf_op jit(solution)/shard_map/ppermute | solution.py:35
  7.1 5.3 %modulate.1 = (bf16[256,1536]{1,0:T(8,128)(2,1)}, bf16[256,1536]{1,0:T(8,128)(2,1)}, f32[256,1536]{1,0:T(8,128)}, f32[256,1536]{1,0:T(8,128)}, bf16[256,128]{1,0:T(8,128)(2,1)}, /*index=5*/bf16[256,128]{1,0:T(8,128)(2,1)}) custom-call(s32[3]{0:T(128)} %pad_add_fusion.place_ref.refs_0_, s32[1,8]{1,0:T(1,128)} %frames_ref.3, s32[1,8]{1,0:T(1,128)} %sizes_ref.3, ...), custom_call_target="tpu_custom_call" | custom-call | bytes 4000000 | tf_op jit(solution)/shard_map/modulate/pallas_call | solution.py:557
  15.1 8.0 %attend.1 = (bf16[256,1536]{1,0:T(8,128)(2,1)}, bf16[256,128]{1,0:T(8,128)(2,1)}, f32[1,1536]{1,0:T(1,128)}, f32[1536,128]{1,0:T(8,128)}, f32[1536,128]{1,0:T(8,...) custom-call(s32[3]{0:T(128)} %pad_add_fusion.place_ref.refs_0_, s32[1,8]{1,0:T(1,128)} %frames_ref.3, s32[1,8]{1,0:T(1,128)} %sizes_ref.3, ...), custom_call_target="tpu_custom_call" | custom-call | bytes 6000000 | tf_op jit(solution)/shard_map/attend/pallas_call | solution.py:557
  28.8 6.1 %backward0.1 = (bf16[256,1152]{1,0:T(8,128)(2,1)}, f32[1152,128]{1,0:T(8,128)}, f32[1,1536]{1,0:T(1,128)}, f32[256,128]{1,0:T(8,128)}) custom-call(s32[3]{0:T(128)} %pad_add_fusion.place_ref.refs_0_, bf16[256,128]{1,0:T(8,128)(2,1)} %get-tuple-element.85.low_grad_ref.refs_1_, bf16[256,128]{1,0:T(8,128)(2,1)} %get-tuple-element.81.refs_2_, ...), custom_call_target="tpu_custom_call" | custom-call | bytes 5000000 | tf_op jit(solution)/shard_map/backward0/pallas_call | solution.py:557
  36.7 6.3 %backward1.1 = (bf16[256,1152]{1,0:T(8,128)(2,1)}, f32[1152,128]{1,0:T(8,128)}, f32[1,1536]{1,0:T(1,128)}, f32[256,128]{1,0:T(8,128)}) custom-call(s32[3]{0:T(128)} %pad_add_fusion.place_ref.refs_0_, bf16[256,128]{1,0:T(8,128)(2,1)} %get-tuple-element.85.low_grad_ref.refs_1_, bf16[256,128]{1,0:T(8,128)(2,1)} %get-tuple-element.81.refs_2_, ...), custom_call_target="tpu_custom_call" | custom-call | bytes 5000000 | tf_op jit(solution)/shard_map/backward1/pallas_call | solution.py:557
  49.6 6.1 %backward2.1 = (bf16[256,1152]{1,0:T(8,128)(2,1)}, f32[1152,128]{1,0:T(8,128)}, f32[1,1536]{1,0:T(1,128)}, f32[256,128]{1,0:T(8,128)}) custom-call(s32[3]{0:T(128)} %pad_add_fusion.place_ref.refs_0_, bf16[256,128]{1,0:T(8,128)(2,1)} %get-tuple-element.85.low_grad_ref.refs_1_, bf16[256,128]{1,0:T(8,128)(2,1)} %get-tuple-element.81.refs_2_, ...), custom_call_target="tpu_custom_call" | custom-call | bytes 5000000 | tf_op jit(solution)/shard_map/backward2/pallas_call | solution.py:557
  56.6 6.2 %backward3.1 = (bf16[256,1152]{1,0:T(8,128)(2,1)}, f32[1152,128]{1,0:T(8,128)}, f32[1,1536]{1,0:T(1,128)}, f32[256,128]{1,0:T(8,128)}) custom-call(s32[3]{0:T(128)} %pad_add_fusion.place_ref.refs_0_, bf16[256,128]{1,0:T(8,128)(2,1)} %get-tuple-element.85.low_grad_ref.refs_1_, bf16[256,128]{1,0:T(8,128)(2,1)} %get-tuple-element.81.refs_2_, ...), custom_call_target="tpu_custom_call" | custom-call | bytes 5000000 | tf_op jit(solution)/shard_map/backward3/pallas_call | solution.py:557
  62.8 5.1 %adapt.1 = (bf16[256,128]{1,0:T(8,128)(2,1)}, bf16[8,576,128]{2,1,0:T(8,128)(2,1)}, f32[8,576,128]{2,1,0:T(8,128)}) custom-call(s32[3]{0:T(128)} %pad_add_fusion.place_ref.refs_0_, bf16[256,1536]{1,0:T(8,128)(2,1)} %get-tuple-element.104.refs_1_, f32[256,128]{1,0:T(8,128)} %get-tuple-element.114.refs_2_, f32[1536,128]{1,0:T(8,128)} %get-tuple-element.115.refs_3_, ...), custom_call_target="tpu_custom_call" | custom-call | bytes 4000000 | tf_op jit(solution)/shard_map/adapt/pallas_call | solution.py:557
  69.2 1.9 %collective-permute-start.27 = (bf16[96,4608]{1,0:T(8,128)(2,1)}, bf16[96,4608]{1,0:T(8,128)(2,1)}, u32[]{:S(2)}, u32[]{:S(2)}) collective-permute-start(bf16[96,4608]{1,0:T(8,128)(2,1)} %collective-permute-done.21.refs_10_), channel_id=1, source_target_pairs={{0,8},{2,10},{4,12},{6,14},{8,16},{10,18},{12,20},{14,22},{16,24},... | collective-permute-start | bytes 2654216 | tf_op jit(solution)/shard_map/ppermute | solution.py:35
  73.9 6.1 %project0.1 = (bf16[256,384]{1,0:T(8,128)(2,1)}, f32[3,1536]{1,0:T(4,128)}) custom-call(s32[3]{0:T(128)} %pad_add_fusion.place_ref.refs_0_, bf16[256,128]{1,0:T(8,128)(2,1)} %get-tuple-element.121.refs_1_, f32[3,1536]{1,0:T(4,128)} %concatenate.3.refs_2_, bf16[256,1152]{1,0:T(8,128)(2,1)} %get-tuple-element.125.refs_3_, ...), custom_call_target="tpu_custom_call" | custom-call | bytes 5000000 | tf_op jit(solution)/shard_map/project0/pallas_call | solution.py:557
  80.1 10.4 %collective-permute-done.22.refs_11_ = bf16[96,4608]{1,0:T(8,128)(2,1)} collective-permute-done((bf16[96,4608]{1,0:T(8,128)(2,1)}, bf16[96,4608]{1,0:T(8,128)(2,1)}, u32[]{:S(2)}, u32[]{:S(2)}) %collective-permute-start.22) | collective-permute-done | bytes 884768 | tf_op jit(solution)/shard_map/ppermute | solution.py:30
  91.0 1.7 %collective-permute-done.27.refs_10_ = bf16[96,4608]{1,0:T(8,128)(2,1)} collective-permute-done((bf16[96,4608]{1,0:T(8,128)(2,1)}, bf16[96,4608]{1,0:T(8,128)(2,1)}, u32[]{:S(2)}, u32[]{:S(2)}) %collective-permute-start.27) | collective-permute-done | bytes 884768 | tf_op jit(solution)/shard_map/ppermute | solution.py:35
  95.9 1.9 %convert_add_fusion = f32[8,576,128]{2,1,0:T(8,128)S(1)} fusion(f32[8,576,128]{2,1,0:T(8,128)} %get-tuple-element.136, bf16[8,576,128]{2,1,0:T(8,128)(2,1)S(1)} %collective-permute-done.24), kind=kLoop, calls=%fused_computation | loop fusion | flops 1179648 | bytes 5898240 | tf_op jit(solution)/shard_map/add | solution.py:751
  97.8 2.2 %collective-permute-done.20.refs_3_ = bf16[256,384]{1,0:T(8,128)(2,1)} collective-permute-done((bf16[256,384]{1,0:T(8,128)(2,1)}, bf16[256,384]{1,0:T(8,128)(2,1)}, u32[]{:S(2)}, u32[]{:S(2)}) %collective-permute-start.20) | collective-permute-done | bytes 196640 | tf_op jit(solution)/shard_map/ppermute | solution.py:737
  100.0 6.1 %project1.1 = (bf16[256,384]{1,0:T(8,128)(2,1)}, f32[3,1536]{1,0:T(4,128)}) custom-call(s32[3]{0:T(128)} %pad_add_fusion.place_ref.refs_0_, bf16[256,128]{1,0:T(8,128)(2,1)} %get-tuple-element.121.refs_1_, f32[3,1536]{1,0:T(4,128)} %get-tuple-element.140.refs_2_, bf16[256,1152]{1,0:T(8,128)(2,1)} %get-tuple-element.125.refs_3_, ...), custom_call_target="tpu_custom_call" | custom-call | bytes 5000000 | tf_op jit(solution)/shard_map/project1/pallas_call | solution.py:557
  106.2 7.4 %collective-permute-done.28.refs_11_ = bf16[96,4608]{1,0:T(8,128)(2,1)} collective-permute-done((bf16[96,4608]{1,0:T(8,128)(2,1)}, bf16[96,4608]{1,0:T(8,128)(2,1)}, u32[]{:S(2)}, u32[]{:S(2)}) %collective-permute-start.28) | collective-permute-done | bytes 884768 | tf_op jit(solution)/shard_map/ppermute | solution.py:30
  118.2 5.4 %collective-permute-done.26.refs_4_ = bf16[256,384]{1,0:T(8,128)(2,1)S(1)} collective-permute-done((bf16[256,384]{1,0:T(8,128)(2,1)}, bf16[256,384]{1,0:T(8,128)(2,1)S(1)}, u32[]{:S(2)}, u32[]{:S(2)}) %collective-permute-start.26) | collective-permute-done | bytes 196640 | tf_op jit(solution)/shard_map/ppermute | solution.py:737
  124.8 6.2 %project2.1 = (bf16[256,384]{1,0:T(8,128)(2,1)}, f32[3,1536]{1,0:T(4,128)}) custom-call(s32[3]{0:T(128)} %pad_add_fusion.place_ref.refs_0_, bf16[256,128]{1,0:T(8,128)(2,1)} %get-tuple-element.121.refs_1_, f32[3,1536]{1,0:T(4,128)} %get-tuple-element.145.refs_2_, bf16[256,1152]{1,0:T(8,128)(2,1)} %get-tuple-element.125.refs_3_, ...), custom_call_target="tpu_custom_call" | custom-call | bytes 5000000 | tf_op jit(solution)/shard_map/project2/pallas_call | solution.py:557
  131.0 6.8 %collective-permute-done.33.refs_11_ = bf16[96,4608]{1,0:T(8,128)(2,1)} collective-permute-done((bf16[96,4608]{1,0:T(8,128)(2,1)}, bf16[96,4608]{1,0:T(8,128)(2,1)}, u32[]{:S(2)}, u32[]{:S(2)}) %collective-permute-start.33) | collective-permute-done | bytes 884768 | tf_op jit(solution)/shard_map/ppermute | solution.py:35
  139.1 1.7 %collective-permute-start.31 = (bf16[256,384]{1,0:T(8,128)(2,1)}, bf16[256,384]{1,0:T(8,128)(2,1)S(1)}, u32[]{:S(2)}, u32[]{:S(2)}) collective-permute-start(bf16[256,384]{1,0:T(8,128)(2,1)} %get-tuple-element.146), channel_id=1, source_target_pairs={{1,0},{0,1},{3,2},{2,3},{5,4},{4,5},{7,6},{6,7},{9,8},{8,9},{11,10... | collective-permute-start | bytes 589832 | tf_op jit(solution)/shard_map/ppermute | solution.py:737
  140.8 6.1 %project3.1 = (bf16[256,384]{1,0:T(8,128)(2,1)}, f32[3,1536]{1,0:T(4,128)}) custom-call(s32[3]{0:T(128)} %pad_add_fusion.place_ref.refs_0_, bf16[256,128]{1,0:T(8,128)(2,1)} %get-tuple-element.121.refs_1_, f32[3,1536]{1,0:T(4,128)} %get-tuple-element.147.refs_2_, bf16[256,1152]{1,0:T(8,128)(2,1)} %get-tuple-element.125.refs_3_, ...), custom_call_target="tpu_custom_call" | custom-call | bytes 5000000 | tf_op jit(solution)/shard_map/project3/pallas_call | solution.py:557
  152.0 1.7 %collective-permute-start.40 = (f32[3,1536]{1,0:T(4,128)S(1)}, f32[3,1536]{1,0:T(4,128)S(1)}, u32[]{:S(2)}, u32[]{:S(2)}) collective-permute-start(f32[3,1536]{1,0:T(4,128)S(1)} %add_add_fusion), channel_id=1, source_target_pairs={{0,8},{2,10},{4,12},{6,14},{8,16},{10,18},{12,20},{14,22},{16,24},... | collective-permute-start | bytes 55304 | tf_op jit(solution)/shard_map/ppermute | solution.py:585
  154.4 1.9 %collective-permute-start.42 = (f32[3,1536]{1,0:T(4,128)S(1)}, f32[3,1536]{1,0:T(4,128)S(1)}, u32[]{:S(2)}, u32[]{:S(2)}) collective-permute-start(f32[3,1536]{1,0:T(4,128)S(1)} %add_add_fusion), channel_id=1, source_target_pairs={{0,24},{2,26},{4,28},{6,30},{8,0},{10,2},{12,4},{14,6},{16,8},{18,... | collective-permute-start | bytes 55304 | tf_op jit(solution)/shard_map/ppermute | solution.py:585
  157.1 3.6 %finish.1 = bf16[256,1536]{1,0:T(8,128)(2,1)} custom-call(s32[3]{0:T(128)} %pad_add_fusion.place_ref.refs_0_, bf16[256,1536]{1,0:T(8,128)(2,1)} %copy-done.8, bf16[256,1536]{1,0:T(8,128)(2,1)} %copy-done.9, bf16[256,384]{1,0:T(8,128)(2,1)} %collective-permute-done.20.refs_3_, bf16[256,384]{1,0:T(8,128)(2,1)} %copy-done.25, bf16[256,384]{1,0:T(8,128)(2,1)} %copy-done.26, ...), custom_call_target="tpu_custom_call" | custom-call | bytes 4000000 | tf_op jit(solution)/shard_map/finish/pallas_call | solution.py:557
  (154 shorter events, 45.1 us)
Async XLA Ops:
  0.6 12.3 %collective-permute-start.1 = (bf16[96,1536]{1,0:T(8,128)(2,1)}, bf16[96,1536]{1,0:T(8,128)(2,1)S(1)}, u32[]{:S(2)}, u32[]{:S(2)}) collective-permute-start(bf16[96,1536]{1,0:T(8,128)(2,1)} %bitcast.51), channel_id=1, source_target_pairs={{0,8},{2,10},{4,12},{6,14},{8,16},{10,18},{12,20},{14,22},{16,24},... | collective-permute-start | bytes 884744 | tf_op jit(solution)/shard_map/ppermute | solution.py:35
  3.7 10.9 %collective-permute-start.3 = (bf16[96,1536]{1,0:T(8,128)(2,1)}, bf16[96,1536]{1,0:T(8,128)(2,1)S(1)}, u32[]{:S(2)}, u32[]{:S(2)}) collective-permute-start(bf16[96,1536]{1,0:T(8,128)(2,1)} %bitcast.52), channel_id=1, source_target_pairs={{0,4},{2,6},{4,0},{6,2},{8,12},{10,14},{12,8},{14,10},{16,20},{18,... | collective-permute-start | bytes 884744 | tf_op jit(solution)/shard_map/ppermute | solution.py:30
  13.0 10.2 %collective-permute-start.2 = (bf16[96,1536]{1,0:T(8,128)(2,1)S(1)}, bf16[96,1536]{1,0:T(8,128)(2,1)S(1)}, u32[]{:S(2)}, u32[]{:S(2)}) collective-permute-start(bf16[96,1536]{1,0:T(8,128)(2,1)S(1)} %collective-permute-done.1.refs_12_), channel_id=1, source_target_pairs={{0,8},{2,10},{4,12},{6,14},{8,16},{10,18},{12,20},{14,22},{16,24},... | collective-permute-start | bytes 884744 | tf_op jit(solution)/shard_map/ppermute | solution.py:35
  14.1 12.2 %collective-permute-start.6 = (bf16[96,1536]{1,0:T(8,128)(2,1)S(1)}, bf16[96,1536]{1,0:T(8,128)(2,1)S(1)}, u32[]{:S(2)}, u32[]{:S(2)}) collective-permute-start(bf16[96,1536]{1,0:T(8,128)(2,1)S(1)} %collective-permute-done.1.refs_12_), channel_id=1, source_target_pairs={{0,4},{2,6},{4,0},{6,2},{8,12},{10,14},{12,8},{14,10},{16,20},{18,... | collective-permute-start | bytes 884744 | tf_op jit(solution)/shard_map/ppermute | solution.py:30
  14.6 11.8 %collective-permute-start.7 = (bf16[96,1536]{1,0:T(8,128)(2,1)S(1)}, bf16[96,1536]{1,0:T(8,128)(2,1)S(1)}, u32[]{:S(2)}, u32[]{:S(2)}) collective-permute-start(bf16[96,1536]{1,0:T(8,128)(2,1)S(1)} %collective-permute-done.3.refs_13_), channel_id=1, source_target_pairs={{0,2},{2,0},{4,6},{6,4},{8,10},{10,8},{12,14},{14,12},{16,18},{18,... | collective-permute-start | bytes 884744 | tf_op jit(solution)/shard_map/ppermute | solution.py:30
  14.6 13.4 %collective-permute-start.8 = (bf16[96,1536]{1,0:T(8,128)(2,1)S(1)}, bf16[96,1536]{1,0:T(8,128)(2,1)S(1)}, u32[]{:S(2)}, u32[]{:S(2)}) collective-permute-start(bf16[96,1536]{1,0:T(8,128)(2,1)S(1)} %bitcast.54), channel_id=1, source_target_pairs={{0,2},{2,0},{4,6},{6,4},{8,10},{10,8},{12,14},{14,12},{16,18},{18,... | collective-permute-start | bytes 884744 | tf_op jit(solution)/shard_map/ppermute | solution.py:30
  23.2 11.8 %collective-permute-start.4 = (bf16[96,1536]{1,0:T(8,128)(2,1)S(1)}, bf16[96,1536]{1,0:T(8,128)(2,1)S(1)}, u32[]{:S(2)}, u32[]{:S(2)}) collective-permute-start(bf16[96,1536]{1,0:T(8,128)(2,1)S(1)} %collective-permute-done.2.refs_12_), channel_id=1, source_target_pairs={{0,8},{2,10},{4,12},{6,14},{8,16},{10,18},{12,20},{14,22},{16,24},... | collective-permute-start | bytes 884744 | tf_op jit(solution)/shard_map/ppermute | solution.py:35
  24.8 21.8 %collective-permute-start = (bf16[256,1536]{1,0:T(8,128)(2,1)S(1)}, bf16[256,1536]{1,0:T(8,128)(2,1)S(1)}, u32[]{:S(2)}, u32[]{:S(2)}) collective-permute-start(bf16[256,1536]{1,0:T(8,128)(2,1)S(1)} %bitcast.49), channel_id=1, source_target_pairs={{1,0},{0,1},{3,2},{2,3},{5,4},{4,5},{7,6},{6,7},{9,8},{8,9},{11,10... | collective-permute-start | bytes 2359304 | tf_op jit(solution)/shard_map/ppermute | solution.py:638
  44.5 23.4 %collective-permute-start.13 = (bf16[96,4608]{1,0:T(8,128)(2,1)S(1)}, bf16[96,4608]{1,0:T(8,128)(2,1)S(1)}, u32[]{:S(2)}, u32[]{:S(2)}) collective-permute-start(bf16[96,4608]{1,0:T(8,128)(2,1)S(1)} %bitcast.45), channel_id=1, source_target_pairs={{0,4},{2,6},{4,0},{6,2},{8,12},{10,14},{12,8},{14,10},{16,20},{18,... | collective-permute-start | bytes 2654216 | tf_op jit(solution)/shard_map/ppermute | solution.py:30
  45.0 23.5 %collective-permute-start.21 = (bf16[96,4608]{1,0:T(8,128)(2,1)S(1)}, bf16[96,4608]{1,0:T(8,128)(2,1)}, u32[]{:S(2)}, u32[]{:S(2)}) collective-permute-start(bf16[96,4608]{1,0:T(8,128)(2,1)S(1)} %bitcast.46), channel_id=1, source_target_pairs={{0,8},{2,10},{4,12},{6,14},{8,16},{10,18},{12,20},{14,22},{16,24},... | collective-permute-start | bytes 2654216 | tf_op jit(solution)/shard_map/ppermute | solution.py:35
  46.1 25.0 %collective-permute-start.11 = (bf16[256,1536]{1,0:T(8,128)(2,1)S(1)}, bf16[256,1536]{1,0:T(8,128)(2,1)S(1)}, u32[]{:S(2)}, u32[]{:S(2)}) collective-permute-start(bf16[256,1536]{1,0:T(8,128)(2,1)S(1)} %bitcast.39), channel_id=1, source_target_pairs={{1,0},{0,1},{3,2},{2,3},{5,4},{4,5},{7,6},{6,7},{9,8},{8,9},{11,10... | collective-permute-start | bytes 2359304 | tf_op jit(solution)/shard_map/ppermute | solution.py:694
  68.5 22.0 %collective-permute-start.22 = (bf16[96,4608]{1,0:T(8,128)(2,1)}, bf16[96,4608]{1,0:T(8,128)(2,1)}, u32[]{:S(2)}, u32[]{:S(2)}) collective-permute-start(bf16[96,4608]{1,0:T(8,128)(2,1)} %collective-permute-done.21.refs_10_), channel_id=1, source_target_pairs={{0,4},{2,6},{4,0},{6,2},{8,12},{10,14},{12,8},{14,10},{16,20},{18,... | collective-permute-start | bytes 2654216 | tf_op jit(solution)/shard_map/ppermute | solution.py:30
  69.2 23.5 %collective-permute-start.27 = (bf16[96,4608]{1,0:T(8,128)(2,1)}, bf16[96,4608]{1,0:T(8,128)(2,1)}, u32[]{:S(2)}, u32[]{:S(2)}) collective-permute-start(bf16[96,4608]{1,0:T(8,128)(2,1)} %collective-permute-done.21.refs_10_), channel_id=1, source_target_pairs={{0,8},{2,10},{4,12},{6,14},{8,16},{10,18},{12,20},{14,22},{16,24},... | collective-permute-start | bytes 2654216 | tf_op jit(solution)/shard_map/ppermute | solution.py:35
  72.0 23.6 %collective-permute-start.24 = (bf16[8,576,128]{2,1,0:T(8,128)(2,1)}, bf16[8,576,128]{2,1,0:T(8,128)(2,1)S(1)}, u32[]{:S(2)}, u32[]{:S(2)}) collective-permute-start(bf16[8,576,128]{2,1,0:T(8,128)(2,1)} %get-tuple-element.137), channel_id=1, source_target_pairs={{0,2},{2,0},{4,6},{6,4},{8,10},{10,8},{12,14},{14,12},{16,18},{18,... | collective-permute-start | bytes 3538952 | tf_op jit(solution)/shard_map/ppermute | solution.py:30
  92.7 20.9 %collective-permute-start.28 = (bf16[96,4608]{1,0:T(8,128)(2,1)}, bf16[96,4608]{1,0:T(8,128)(2,1)}, u32[]{:S(2)}, u32[]{:S(2)}) collective-permute-start(bf16[96,4608]{1,0:T(8,128)(2,1)} %collective-permute-done.27.refs_10_), channel_id=1, source_target_pairs={{0,4},{2,6},{4,0},{6,2},{8,12},{10,14},{12,8},{14,10},{16,20},{18,... | collective-permute-start | bytes 2654216 | tf_op jit(solution)/shard_map/ppermute | solution.py:30
  95.6 22.1 %collective-permute-start.32 = (bf16[96,4608]{1,0:T(8,128)(2,1)}, bf16[96,4608]{1,0:T(8,128)(2,1)}, u32[]{:S(2)}, u32[]{:S(2)}) collective-permute-start(bf16[96,4608]{1,0:T(8,128)(2,1)} %collective-permute-done.27.refs_10_), channel_id=1, source_target_pairs={{0,8},{2,10},{4,12},{6,14},{8,16},{10,18},{12,20},{14,22},{16,24},... | collective-permute-start | bytes 2654216 | tf_op jit(solution)/shard_map/ppermute | solution.py:35
  113.6 9.9 %collective-permute-start.29 = (bf16[96,4608]{1,0:T(8,128)(2,1)}, bf16[96,4608]{1,0:T(8,128)(2,1)S(1)}, u32[]{:S(2)}, u32[]{:S(2)}) collective-permute-start(bf16[96,4608]{1,0:T(8,128)(2,1)} %collective-permute-done.28.refs_11_), channel_id=1, source_target_pairs={{0,2},{2,0},{4,6},{6,4},{8,10},{10,8},{12,14},{14,12},{16,18},{18,... | collective-permute-start | bytes 2654216 | tf_op jit(solution)/shard_map/ppermute | solution.py:30
  113.6 10.0 %collective-permute-start.30 = (bf16[96,4608]{1,0:T(8,128)(2,1)}, bf16[96,4608]{1,0:T(8,128)(2,1)S(1)}, u32[]{:S(2)}, u32[]{:S(2)}) collective-permute-start(bf16[96,4608]{1,0:T(8,128)(2,1)} %collective-permute-done.27.refs_10_), channel_id=1, source_target_pairs={{0,2},{2,0},{4,6},{6,4},{8,10},{10,8},{12,14},{14,12},{16,18},{18,... | collective-permute-start | bytes 2654216 | tf_op jit(solution)/shard_map/ppermute | solution.py:30
  114.1 23.7 %collective-permute-start.33 = (bf16[96,4608]{1,0:T(8,128)(2,1)}, bf16[96,4608]{1,0:T(8,128)(2,1)}, u32[]{:S(2)}, u32[]{:S(2)}) collective-permute-start(bf16[96,4608]{1,0:T(8,128)(2,1)} %collective-permute-done.28.refs_11_), channel_id=1, source_target_pairs={{0,8},{2,10},{4,12},{6,14},{8,16},{10,18},{12,20},{14,22},{16,24},... | collective-permute-start | bytes 2654216 | tf_op jit(solution)/shard_map/ppermute | solution.py:35
  115.5 22.3 %collective-permute-start.43 = (bf16[4,576,128]{2,1,0:T(8,128)(2,1)S(1)}, bf16[4,576,128]{2,1,0:T(8,128)(2,1)}, u32[]{:S(2)}, u32[]{:S(2)}) collective-permute-start(bf16[4,576,128]{2,1,0:T(8,128)(2,1)S(1)} %fusion), channel_id=1, source_target_pairs={{0,4},{2,6},{4,0},{6,2},{8,12},{10,14},{12,8},{14,10},{16,20},{18,... | collective-permute-start | bytes 1769480 | tf_op jit(solution)/shard_map/ppermute | solution.py:30
  123.5 17.3 %collective-permute-start.34 = (bf16[96,4608]{1,0:T(8,128)(2,1)}, bf16[96,4608]{1,0:T(8,128)(2,1)}, u32[]{:S(2)}, u32[]{:S(2)}) collective-permute-start(bf16[96,4608]{1,0:T(8,128)(2,1)} %collective-permute-done.32.refs_10_), channel_id=1, source_target_pairs={{0,2},{2,0},{4,6},{6,4},{8,10},{10,8},{12,14},{14,12},{16,18},{18,... | collective-permute-start | bytes 2654216 | tf_op jit(solution)/shard_map/ppermute | solution.py:30
  139.0 9.9 %collective-permute-start.44 = (bf16[2,576,128]{2,1,0:T(8,128)(2,1)S(1)}, bf16[2,576,128]{2,1,0:T(8,128)(2,1)S(1)}, u32[]{:S(2)}, u32[]{:S(2)}) collective-permute-start(bf16[2,576,128]{2,1,0:T(8,128)(2,1)S(1)} %fusion.1), channel_id=1, source_target_pairs={{0,8},{2,10},{4,12},{6,14},{8,0},{10,2},{12,4},{14,6},{16,24},{18,... | collective-permute-start | bytes 884744 | tf_op jit(solution)/shard_map/ppermute | solution.py:30
  139.1 15.3 %collective-permute-start.31 = (bf16[256,384]{1,0:T(8,128)(2,1)}, bf16[256,384]{1,0:T(8,128)(2,1)S(1)}, u32[]{:S(2)}, u32[]{:S(2)}) collective-permute-start(bf16[256,384]{1,0:T(8,128)(2,1)} %get-tuple-element.146), channel_id=1, source_target_pairs={{1,0},{0,1},{3,2},{2,3},{5,4},{4,5},{7,6},{6,7},{9,8},{8,9},{11,10... | collective-permute-start | bytes 589832 | tf_op jit(solution)/shard_map/ppermute | solution.py:737
  150.3 11.5 %collective-permute-start.45 = (bf16[1,576,128]{2,1,0:T(8,128)(2,1)S(1)}, bf16[1,576,128]{2,1,0:T(8,128)(2,1)S(1)}, u32[]{:S(2)}, u32[]{:S(2)}) collective-permute-start(bf16[1,576,128]{2,1,0:T(8,128)(2,1)S(1)} %dynamic-slice_convert_fusion.1), channel_id=1, source_target_pairs={{0,16},{2,18},{4,20},{6,22},{8,24},{10,26},{12,28},{14,30},{16,0},... | collective-permute-start | bytes 442376 | tf_op jit(solution)/shard_map/ppermute | solution.py:30
  (52 other events, 305.9 us)

commit v4 on v3

--- a/solution.py
+++ b/solution.py
@@ -498,31 +498,42 @@
     u_ref, table_ref, whole_ref, near_ref, down_ref, held_ref, sems = refs[3 + sum(sizes) :]
     depth = whole_ref.shape[0]
     inner = whole_ref.shape[1] // 3
-    weights = shard_copies(place_ref, shards, whole_ref, sems)
-    used = len(weights)
     first = pl.multiple_of(layer_of(place_ref, step) * depth, HEAD)
     layer = pl.ds(first, depth)
+    count = sum(sizes)
+    parts = []
+    for part in range(3):
+        columns = slice(part * inner, (part + 1) * inner)
+        near = [[piece.at[:, columns] for piece in shard] for shard in shards]
+        copies = shard_copies(
+            place_ref, near, whole_ref.at[:, columns], sems.at[pl.ds(part * (count + ring), count)]
+        )
+        for n in range(ring):
+            start = pl.multiple_of(part * inner + layer_of(place_ref, n) * depth, HEAD)
+            copies.append(
+                pltpu.make_async_copy(
+                    grad_refs[n].at[:, part * depth : (part + 1) * depth],
+                    held_ref.at[:, pl.ds(start, depth)],
+                    sems.at[part * (count + ring) + count + n],
+                )
+            )
+        parts.append(copies)
+    used = 3 * (count + ring)
     others = [
         pltpu.make_async_copy(adapters_ref.at[0, layer, :], down_ref, sems.at[used]),
         pltpu.make_async_copy(normed_ref.at[:, layer], near_ref.at[0], sems.at[used + 1]),
         pltpu.make_async_copy(scale_ref.at[:, layer], near_ref.at[1], sems.at[used + 2]),
     ]
-    for n in range(ring):
-        start = layer_of(place_ref, n) * depth
-        for part in range(3):
-            columns = pl.ds(pl.multiple_of(part * inner + start, HEAD), depth)
-            others.append(
-                pltpu.make_async_copy(
-                    grad_refs[n].at[:, part * depth : (part + 1) * depth],
-                    held_ref.at[:, columns],
-                    sems.at[used + 3 + 3 * n + part],
-                )
-            )
-    for copy in weights + others:
+    for copy in sum(parts, []) + others:
         copy.start()
-    for copy in weights + others:
+    total = jnp.zeros(u_ref.shape, F32)
+    for part in range(3):
+        for copy in parts[part]:
+            copy.wait()
+        columns = slice(part * inner, (part + 1) * inner)
+        total = total + contract_last(held_ref[:, columns], whole_ref[:, columns])
+    for copy in others:
         copy.wait()
-    total = contract_last(held_ref[...], whole_ref[...])
     total = total + contract_last(low_ref[...], down_ref[...])
     u_ref[...] = (total * near_ref[1]).astype(BF16)
     table_ref[...] = table_in_ref[...]
@@ -635,7 +646,6 @@
         name="modulate",
     )
     event = low_in
-    next_input = lax.ppermute(gate(tokens_here, event), "pipe", before)
     out_r.append(ring_shifted(gate(out_r[1], event)))
     out_x.append(across(gate(out_r[1], event)))
     out_xc.append(beside(gate(out_x[0], event)))
@@ -691,11 +701,12 @@
     grad1, grad_up1, gate_sum, total = backward(1, gate_sum, total, out_r[3], out_x[2])
     event = total
     qkv_x.append(across(gate(qkv_r[0], event, out_x[3])))
+    next_input = lax.ppermute(gate(tokens_here, event), "pipe", before)
     next_cot = lax.ppermute(gate(cot, event), "pipe", before)
     out_rc.append(beside(gate(out_r[3], event)))
     out_xc.append(beside(gate(out_x[3], event)))
     grad2, grad_up2, gate_sum, total = backward(2, gate_sum, total, out_x[3])
-    grad3, grad_up3, gate_sum, total = backward(3, gate_sum, total, next_input)
+    grad3, grad_up3, gate_sum, total = backward(3, gate_sum, total)
     event = total
     grads = [grad0, grad1, grad2, grad3]
     grad_ups = [grad_up0, grad_up1, grad_up2, grad_up3]
@@ -723,7 +734,7 @@
             scratch=[
                 pltpu.VMEM((depth, 3 * inner), BF16), pltpu.VMEM((2, rows, depth), F32),
                 pltpu.VMEM((depth, rank), BF16), pltpu.VMEM((rows, 3 * inner), BF16),
-                pltpu.SemaphoreType.DMA((9 + 3 * ring,)),
+                pltpu.SemaphoreType.DMA((3 * (sum(sizes) + ring) + 3,)),
             ],
             name=f"project{step}",
         )
@@ -743,7 +754,7 @@
     arrived = beside(sent)
     layers = [[[qkv_r[0]], [qkv_x[0]], [qkv_rc[0]], [qkv_xc[0]]]]
     table = jnp.concatenate([jnp.zeros((2, width), F32), gate_sum], axis=0)
-    u0, table = project(0, qkv_xc[0], next_cot)
+    u0, table = project(0, qkv_xc[0], next_input)
     qkv_r.append(ring_shifted(gate(qkv_r[2], u0)))
     qkv_x.append(across(gate(qkv_r[2], u0)))
     qkv_rc.append(beside(gate(qkv_r[2], u0)))
@@ -751,7 +762,7 @@
     kept, sent = halved(kept + gate(arrived, u0).astype(F32), 2)
     received = [sends(u0)]
     layers.append([[qkv_r[1]], [qkv_x[1]], [qkv_rc[1]], [qkv_xc[1]]])
-    u1, table = project(1, qkv_xc[1], sent, received[0])
+    u1, table = project(1, qkv_xc[1], sent, received[0], next_cot)
     rest = [ring_shifted(gate(qkv_x[2], u1))]
     qkv_rc.append(beside(gate(qkv_r[3], u1)))
     qkv_xc.append(beside(gate(qkv_x[2], u1)))

time: 164 us -> 161 us (0.982)
  Pallas kernels: 71.2 us -> 69.2 us
    ppermute x7, waiting for transfers between devices: 10.7 us -> 14.3 us  [ring_shifted(): lax.ppermute(block, 'dp', [(i, (i + 4) % count) for i in range(count)])]
    ppermute x30, waiting for transfers between devices: 23.7 us -> 20.5 us  [swapped(): return lax.ppermute(block, 'dp', [(i, i ^ bit) for i in devices])]
    ppermute x7, starting transfers between devices: 10.5 us -> 7.68 us  [ring_shifted(): lax.ppermute(block, 'dp', [(i, (i + 4) % count) for i in range(count)])]
    pallas_call x12, Pallas kernels: 71.2 us -> 69.2 us  [call(): pl.pallas_call(kernel, out_shape=outs, in_specs=[pl.BlockSpec(memory_spac...]
  transfers between devices with their start and end apart: 46 -> 46, of which waited for: 17 -> 18; matrix products, arithmetic and copies ran while one was open for 4% -> 4% of each run, Pallas kernels for 44% -> 43%
where the time goes in v4:
time: 161 us
  Pallas kernels  69.2 us (43%)
  waiting for transfers between devices  42.9 us (27%)
  starting transfers between devices  34.2 us (21%)
  local copies, waits for them, and re-layouts  8.94 us (6%)
  other arithmetic  4.41 us (3%)
    pallas_call x12, Pallas kernels, call(): pl.pallas_call(kernel, out_shape=outs, in_specs=[pl.BlockSpec(memory_spac...  69.2 us
    ppermute x30, waiting for transfers between devices, swapped(): return lax.ppermute(block, 'dp', [(i, i ^ bit) for i in devices])  20.5 us
    ppermute x7, waiting for transfers between devices, ring_shifted(): lax.ppermute(block, 'dp', [(i, (i + 4) % count) for i in range(count)])  14.3 us
    ppermute x30, starting transfers between devices, swapped(): return lax.ppermute(block, 'dp', [(i, i ^ bit) for i in devices])  13.4 us
    ppermute x4, waiting for transfers between devices, on_device(): sends = lambda u: lax.ppermute(u, 'pipe', before)  7.88 us
    ppermute x7, starting transfers between devices, ring_shifted(): lax.ppermute(block, 'dp', [(i, (i + 4) % count) for i in range(count)])  7.68 us
    unnamed x62, local copies, waits for them, and re-layouts  7.45 us
    ppermute x4, starting transfers between devices, on_device(): sends = lambda u: lax.ppermute(u, 'pipe', before)  5.12 us
  transfers between devices with their start and end apart: 46, of which 18 were waited for; matrix products, arithmetic and copies ran while one was open for 4% of the time, Pallas kernels for 43%

profile of v4, /device:TPU:0, one launch (start us, length us, event | category | flops | bytes accessed | tf_op | source)
XLA Modules:
  0.0 160.8 jit_solution(16415593766740137689)
XLA Ops:
  0.6 3.1 %collective-permute-start = (bf16[96,1536]{1,0:T(8,128)(2,1)}, bf16[96,1536]{1,0:T(8,128)(2,1)S(1)}, u32[]{:S(2)}, u32[]{:S(2)}) collective-permute-start(bf16[96,1536]{1,0:T(8,128)(2,1)} %bitcast.51), channel_id=1, source_target_pairs={{0,8},{2,10},{4,12},{6,14},{8,16},{10,18},{12,20},{14,22},{16,24},... | collective-permute-start | bytes 884744 | tf_op jit(solution)/shard_map/ppermute | solution.py:35
  7.1 5.3 %modulate.1 = (bf16[256,1536]{1,0:T(8,128)(2,1)}, bf16[256,1536]{1,0:T(8,128)(2,1)}, f32[256,1536]{1,0:T(8,128)}, f32[256,1536]{1,0:T(8,128)}, bf16[256,128]{1,0:T(8,128)(2,1)}, /*index=5*/bf16[256,128]{1,0:T(8,128)(2,1)}) custom-call(s32[3]{0:T(128)} %pad_add_fusion.place_ref.refs_0_, s32[1,8]{1,0:T(1,128)} %frames_ref.3, s32[1,8]{1,0:T(1,128)} %sizes_ref.3, ...), custom_call_target="tpu_custom_call" | custom-call | bytes 4000000 | tf_op jit(solution)/shard_map/modulate/pallas_call | solution.py:568
  15.1 7.9 %attend.1 = (bf16[256,1536]{1,0:T(8,128)(2,1)}, bf16[256,128]{1,0:T(8,128)(2,1)}, f32[1,1536]{1,0:T(1,128)}, f32[1536,128]{1,0:T(8,128)}, f32[1536,128]{1,0:T(8,...) custom-call(s32[3]{0:T(128)} %pad_add_fusion.place_ref.refs_0_, s32[1,8]{1,0:T(1,128)} %frames_ref.3, s32[1,8]{1,0:T(1,128)} %sizes_ref.3, ...), custom_call_target="tpu_custom_call" | custom-call | bytes 6000000 | tf_op jit(solution)/shard_map/attend/pallas_call | solution.py:568
  23.1 1.6 %collective-permute-start.3 = (bf16[96,1536]{1,0:T(8,128)(2,1)S(1)}, bf16[96,1536]{1,0:T(8,128)(2,1)S(1)}, u32[]{:S(2)}, u32[]{:S(2)}) collective-permute-start(bf16[96,1536]{1,0:T(8,128)(2,1)S(1)} %collective-permute-done.1.refs_12_), channel_id=1, source_target_pairs={{0,8},{2,10},{4,12},{6,14},{8,16},{10,18},{12,20},{14,22},{16,24},... | collective-permute-start | bytes 884744 | tf_op jit(solution)/shard_map/ppermute | solution.py:35
  27.2 6.1 %backward0.1 = (bf16[256,1152]{1,0:T(8,128)(2,1)}, f32[1152,128]{1,0:T(8,128)}, f32[1,1536]{1,0:T(1,128)}, f32[256,128]{1,0:T(8,128)}) custom-call(s32[3]{0:T(128)} %pad_add_fusion.place_ref.refs_0_, bf16[256,128]{1,0:T(8,128)(2,1)} %get-tuple-element.83.low_grad_ref.refs_1_, bf16[256,128]{1,0:T(8,128)(2,1)} %get-tuple-element.80.refs_2_, ...), custom_call_target="tpu_custom_call" | custom-call | bytes 5000000 | tf_op jit(solution)/shard_map/backward0/pallas_call | solution.py:568
  36.3 6.3 %backward1.1 = (bf16[256,1152]{1,0:T(8,128)(2,1)}, f32[1152,128]{1,0:T(8,128)}, f32[1,1536]{1,0:T(1,128)}, f32[256,128]{1,0:T(8,128)}) custom-call(s32[3]{0:T(128)} %pad_add_fusion.place_ref.refs_0_, bf16[256,128]{1,0:T(8,128)(2,1)} %get-tuple-element.83.low_grad_ref.refs_1_, bf16[256,128]{1,0:T(8,128)(2,1)} %get-tuple-element.80.refs_2_, ...), custom_call_target="tpu_custom_call" | custom-call | bytes 5000000 | tf_op jit(solution)/shard_map/backward1/pallas_call | solution.py:568
  47.1 6.1 %backward2.1 = (bf16[256,1152]{1,0:T(8,128)(2,1)}, f32[1152,128]{1,0:T(8,128)}, f32[1,1536]{1,0:T(1,128)}, f32[256,128]{1,0:T(8,128)}) custom-call(s32[3]{0:T(128)} %pad_add_fusion.place_ref.refs_0_, bf16[256,128]{1,0:T(8,128)(2,1)} %get-tuple-element.83.low_grad_ref.refs_1_, bf16[256,128]{1,0:T(8,128)(2,1)} %get-tuple-element.80.refs_2_, ...), custom_call_target="tpu_custom_call" | custom-call | bytes 5000000 | tf_op jit(solution)/shard_map/backward2/pallas_call | solution.py:568
  54.1 6.1 %backward3.1 = (bf16[256,1152]{1,0:T(8,128)(2,1)}, f32[1152,128]{1,0:T(8,128)}, f32[1,1536]{1,0:T(1,128)}, f32[256,128]{1,0:T(8,128)}) custom-call(s32[3]{0:T(128)} %pad_add_fusion.place_ref.refs_0_, bf16[256,128]{1,0:T(8,128)(2,1)} %get-tuple-element.83.low_grad_ref.refs_1_, bf16[256,128]{1,0:T(8,128)(2,1)} %get-tuple-element.80.refs_2_, ...), custom_call_target="tpu_custom_call" | custom-call | bytes 5000000 | tf_op jit(solution)/shard_map/backward3/pallas_call | solution.py:568
  60.3 5.2 %adapt.1 = (bf16[256,128]{1,0:T(8,128)(2,1)}, bf16[8,576,128]{2,1,0:T(8,128)(2,1)}, f32[8,576,128]{2,1,0:T(8,128)}) custom-call(s32[3]{0:T(128)} %pad_add_fusion.place_ref.refs_0_, bf16[256,1536]{1,0:T(8,128)(2,1)} %get-tuple-element.103.refs_1_, f32[256,128]{1,0:T(8,128)} %get-tuple-element.112.refs_2_, f32[1536,128]{1,0:T(8,128)} %get-tuple-element.113.refs_3_, ...), custom_call_target="tpu_custom_call" | custom-call | bytes 4000000 | tf_op jit(solution)/shard_map/adapt/pallas_call | solution.py:568
  72.9 5.6 %project0.1 = (bf16[256,384]{1,0:T(8,128)(2,1)}, f32[3,1536]{1,0:T(4,128)}) custom-call(s32[3]{0:T(128)} %pad_add_fusion.place_ref.refs_0_, bf16[256,128]{1,0:T(8,128)(2,1)} %get-tuple-element.119.refs_1_, f32[3,1536]{1,0:T(4,128)} %concatenate.3.refs_2_, bf16[256,1152]{1,0:T(8,128)(2,1)} %get-tuple-element.123.refs_3_, ...), custom_call_target="tpu_custom_call" | custom-call | bytes 5000000 | tf_op jit(solution)/shard_map/project0/pallas_call | solution.py:568
  78.6 10.2 %collective-permute-done.22.refs_11_ = bf16[96,4608]{1,0:T(8,128)(2,1)} collective-permute-done((bf16[96,4608]{1,0:T(8,128)(2,1)}, bf16[96,4608]{1,0:T(8,128)(2,1)}, u32[]{:S(2)}, u32[]{:S(2)}) %collective-permute-start.22) | collective-permute-done | bytes 884768 | tf_op jit(solution)/shard_map/ppermute | solution.py:30
  89.2 2.2 %collective-permute-done.27.refs_10_ = bf16[96,4608]{1,0:T(8,128)(2,1)} collective-permute-done((bf16[96,4608]{1,0:T(8,128)(2,1)}, bf16[96,4608]{1,0:T(8,128)(2,1)}, u32[]{:S(2)}, u32[]{:S(2)}) %collective-permute-start.27) | collective-permute-done | bytes 884768 | tf_op jit(solution)/shard_map/ppermute | solution.py:35
  93.8 1.9 %convert_add_fusion = f32[8,576,128]{2,1,0:T(8,128)S(1)} fusion(f32[8,576,128]{2,1,0:T(8,128)} %get-tuple-element.134, bf16[8,576,128]{2,1,0:T(8,128)(2,1)S(1)} %collective-permute-done.24), kind=kLoop, calls=%fused_computation | loop fusion | flops 1179648 | bytes 5898240 | tf_op jit(solution)/shard_map/add | solution.py:762
  95.7 2.5 %collective-permute-done.20.refs_3_ = bf16[256,384]{1,0:T(8,128)(2,1)} collective-permute-done((bf16[256,384]{1,0:T(8,128)(2,1)}, bf16[256,384]{1,0:T(8,128)(2,1)}, u32[]{:S(2)}, u32[]{:S(2)}) %collective-permute-start.20) | collective-permute-done | bytes 196640 | tf_op jit(solution)/shard_map/ppermute | solution.py:748
  98.3 5.6 %project1.1 = (bf16[256,384]{1,0:T(8,128)(2,1)}, f32[3,1536]{1,0:T(4,128)}) custom-call(s32[3]{0:T(128)} %pad_add_fusion.place_ref.refs_0_, bf16[256,128]{1,0:T(8,128)(2,1)} %get-tuple-element.119.refs_1_, f32[3,1536]{1,0:T(4,128)} %get-tuple-element.138.refs_2_, bf16[256,1152]{1,0:T(8,128)(2,1)} %get-tuple-element.123.refs_3_, ...), custom_call_target="tpu_custom_call" | custom-call | bytes 5000000 | tf_op jit(solution)/shard_map/project1/pallas_call | solution.py:568
  103.9 7.5 %collective-permute-done.28.refs_11_ = bf16[96,4608]{1,0:T(8,128)(2,1)} collective-permute-done((bf16[96,4608]{1,0:T(8,128)(2,1)}, bf16[96,4608]{1,0:T(8,128)(2,1)}, u32[]{:S(2)}, u32[]{:S(2)}) %collective-permute-start.28) | collective-permute-done | bytes 884768 | tf_op jit(solution)/shard_map/ppermute | solution.py:30
  113.4 1.7 %collective-permute-done.32.refs_10_ = bf16[96,4608]{1,0:T(8,128)(2,1)} collective-permute-done((bf16[96,4608]{1,0:T(8,128)(2,1)}, bf16[96,4608]{1,0:T(8,128)(2,1)}, u32[]{:S(2)}, u32[]{:S(2)}) %collective-permute-start.32) | collective-permute-done | bytes 884768 | tf_op jit(solution)/shard_map/ppermute | solution.py:35
  115.6 5.4 %collective-permute-done.26.refs_4_ = bf16[256,384]{1,0:T(8,128)(2,1)S(1)} collective-permute-done((bf16[256,384]{1,0:T(8,128)(2,1)}, bf16[256,384]{1,0:T(8,128)(2,1)S(1)}, u32[]{:S(2)}, u32[]{:S(2)}) %collective-permute-start.26) | collective-permute-done | bytes 196640 | tf_op jit(solution)/shard_map/ppermute | solution.py:748
  122.2 5.7 %project2.1 = (bf16[256,384]{1,0:T(8,128)(2,1)}, f32[3,1536]{1,0:T(4,128)}) custom-call(s32[3]{0:T(128)} %pad_add_fusion.place_ref.refs_0_, bf16[256,128]{1,0:T(8,128)(2,1)} %get-tuple-element.119.refs_1_, f32[3,1536]{1,0:T(4,128)} %get-tuple-element.143.refs_2_, bf16[256,1152]{1,0:T(8,128)(2,1)} %get-tuple-element.123.refs_3_, ...), custom_call_target="tpu_custom_call" | custom-call | bytes 5000000 | tf_op jit(solution)/shard_map/project2/pallas_call | solution.py:568
  127.9 7.6 %collective-permute-done.33.refs_11_ = bf16[96,4608]{1,0:T(8,128)(2,1)} collective-permute-done((bf16[96,4608]{1,0:T(8,128)(2,1)}, bf16[96,4608]{1,0:T(8,128)(2,1)}, u32[]{:S(2)}, u32[]{:S(2)}) %collective-permute-start.33) | collective-permute-done | bytes 884768 | tf_op jit(solution)/shard_map/ppermute | solution.py:35
  138.5 5.7 %project3.1 = (bf16[256,384]{1,0:T(8,128)(2,1)}, f32[3,1536]{1,0:T(4,128)}) custom-call(s32[3]{0:T(128)} %pad_add_fusion.place_ref.refs_0_, bf16[256,128]{1,0:T(8,128)(2,1)} %get-tuple-element.119.refs_1_, f32[3,1536]{1,0:T(4,128)} %get-tuple-element.145.refs_2_, bf16[256,1152]{1,0:T(8,128)(2,1)} %get-tuple-element.123.refs_3_, ...), custom_call_target="tpu_custom_call" | custom-call | bytes 5000000 | tf_op jit(solution)/shard_map/project3/pallas_call | solution.py:568
  149.0 1.7 %collective-permute-start.40 = (f32[3,1536]{1,0:T(4,128)S(1)}, f32[3,1536]{1,0:T(4,128)S(1)}, u32[]{:S(2)}, u32[]{:S(2)}) collective-permute-start(f32[3,1536]{1,0:T(4,128)S(1)} %add_add_fusion), channel_id=1, source_target_pairs={{0,8},{2,10},{4,12},{6,14},{8,16},{10,18},{12,20},{14,22},{16,24},... | collective-permute-start | bytes 55304 | tf_op jit(solution)/shard_map/ppermute | solution.py:596
  151.7 2.2 %collective-permute-start.42 = (f32[3,1536]{1,0:T(4,128)S(1)}, f32[3,1536]{1,0:T(4,128)S(1)}, u32[]{:S(2)}, u32[]{:S(2)}) collective-permute-start(f32[3,1536]{1,0:T(4,128)S(1)} %add_add_fusion), channel_id=1, source_target_pairs={{0,24},{2,26},{4,28},{6,30},{8,0},{10,2},{12,4},{14,6},{16,8},{18,... | collective-permute-start | bytes 55304 | tf_op jit(solution)/shard_map/ppermute | solution.py:596
  154.6 3.6 %finish.1 = bf16[256,1536]{1,0:T(8,128)(2,1)} custom-call(s32[3]{0:T(128)} %pad_add_fusion.place_ref.refs_0_, bf16[256,1536]{1,0:T(8,128)(2,1)} %copy-done.8, bf16[256,1536]{1,0:T(8,128)(2,1)} %collective-permute-done.11.refs_2_, bf16[256,384]{1,0:T(8,128)(2,1)} %collective-permute-done.20.refs_3_, bf16[256,384]{1,0:T(8,128)(2,1)} %copy-done.25, ...), custom_call_target="tpu_custom_call" | custom-call | bytes 4000000 | tf_op jit(solution)/shard_map/finish/pallas_call | solution.py:568
  (154 shorter events, 43.0 us)
Async XLA Ops:
  0.6 12.3 %collective-permute-start = (bf16[96,1536]{1,0:T(8,128)(2,1)}, bf16[96,1536]{1,0:T(8,128)(2,1)S(1)}, u32[]{:S(2)}, u32[]{:S(2)}) collective-permute-start(bf16[96,1536]{1,0:T(8,128)(2,1)} %bitcast.51), channel_id=1, source_target_pairs={{0,8},{2,10},{4,12},{6,14},{8,16},{10,18},{12,20},{14,22},{16,24},... | collective-permute-start | bytes 884744 | tf_op jit(solution)/shard_map/ppermute | solution.py:35
  3.7 10.9 %collective-permute-start.2 = (bf16[96,1536]{1,0:T(8,128)(2,1)}, bf16[96,1536]{1,0:T(8,128)(2,1)S(1)}, u32[]{:S(2)}, u32[]{:S(2)}) collective-permute-start(bf16[96,1536]{1,0:T(8,128)(2,1)} %bitcast.52), channel_id=1, source_target_pairs={{0,4},{2,6},{4,0},{6,2},{8,12},{10,14},{12,8},{14,10},{16,20},{18,... | collective-permute-start | bytes 884744 | tf_op jit(solution)/shard_map/ppermute | solution.py:30
  13.0 10.1 %collective-permute-start.1 = (bf16[96,1536]{1,0:T(8,128)(2,1)S(1)}, bf16[96,1536]{1,0:T(8,128)(2,1)S(1)}, u32[]{:S(2)}, u32[]{:S(2)}) collective-permute-start(bf16[96,1536]{1,0:T(8,128)(2,1)S(1)} %collective-permute-done.refs_12_), channel_id=1, source_target_pairs={{0,8},{2,10},{4,12},{6,14},{8,16},{10,18},{12,20},{14,22},{16,24},... | collective-permute-start | bytes 884744 | tf_op jit(solution)/shard_map/ppermute | solution.py:35
  14.1 10.6 %collective-permute-start.5 = (bf16[96,1536]{1,0:T(8,128)(2,1)S(1)}, bf16[96,1536]{1,0:T(8,128)(2,1)S(1)}, u32[]{:S(2)}, u32[]{:S(2)}) collective-permute-start(bf16[96,1536]{1,0:T(8,128)(2,1)S(1)} %collective-permute-done.refs_12_), channel_id=1, source_target_pairs={{0,4},{2,6},{4,0},{6,2},{8,12},{10,14},{12,8},{14,10},{16,20},{18,... | collective-permute-start | bytes 884744 | tf_op jit(solution)/shard_map/ppermute | solution.py:30
  14.6 11.7 %collective-permute-start.6 = (bf16[96,1536]{1,0:T(8,128)(2,1)S(1)}, bf16[96,1536]{1,0:T(8,128)(2,1)S(1)}, u32[]{:S(2)}, u32[]{:S(2)}) collective-permute-start(bf16[96,1536]{1,0:T(8,128)(2,1)S(1)} %collective-permute-done.2.refs_13_), channel_id=1, source_target_pairs={{0,2},{2,0},{4,6},{6,4},{8,10},{10,8},{12,14},{14,12},{16,18},{18,... | collective-permute-start | bytes 884744 | tf_op jit(solution)/shard_map/ppermute | solution.py:30
  14.6 11.8 %collective-permute-start.7 = (bf16[96,1536]{1,0:T(8,128)(2,1)S(1)}, bf16[96,1536]{1,0:T(8,128)(2,1)S(1)}, u32[]{:S(2)}, u32[]{:S(2)}) collective-permute-start(bf16[96,1536]{1,0:T(8,128)(2,1)S(1)} %bitcast.54), channel_id=1, source_target_pairs={{0,2},{2,0},{4,6},{6,4},{8,10},{10,8},{12,14},{14,12},{16,18},{18,... | collective-permute-start | bytes 884744 | tf_op jit(solution)/shard_map/ppermute | solution.py:30
  23.1 10.9 %collective-permute-start.3 = (bf16[96,1536]{1,0:T(8,128)(2,1)S(1)}, bf16[96,1536]{1,0:T(8,128)(2,1)S(1)}, u32[]{:S(2)}, u32[]{:S(2)}) collective-permute-start(bf16[96,1536]{1,0:T(8,128)(2,1)S(1)} %collective-permute-done.1.refs_12_), channel_id=1, source_target_pairs={{0,8},{2,10},{4,12},{6,14},{8,16},{10,18},{12,20},{14,22},{16,24},... | collective-permute-start | bytes 884744 | tf_op jit(solution)/shard_map/ppermute | solution.py:35
  24.7 10.7 %collective-permute-start.8 = (bf16[96,1536]{1,0:T(8,128)(2,1)S(1)}, bf16[96,1536]{1,0:T(8,128)(2,1)S(1)}, u32[]{:S(2)}, u32[]{:S(2)}) collective-permute-start(bf16[96,1536]{1,0:T(8,128)(2,1)S(1)} %collective-permute-done.refs_12_), channel_id=1, source_target_pairs={{0,2},{2,0},{4,6},{6,4},{8,10},{10,8},{12,14},{14,12},{16,18},{18,... | collective-permute-start | bytes 884744 | tf_op jit(solution)/shard_map/ppermute | solution.py:30
  24.7 10.7 %collective-permute-start.4 = (bf16[96,1536]{1,0:T(8,128)(2,1)S(1)}, bf16[96,1536]{1,0:T(8,128)(2,1)S(1)}, u32[]{:S(2)}, u32[]{:S(2)}) collective-permute-start(bf16[96,1536]{1,0:T(8,128)(2,1)S(1)} %collective-permute-done.1.refs_12_), channel_id=1, source_target_pairs={{0,4},{2,6},{4,0},{6,2},{8,12},{10,14},{12,8},{14,10},{16,20},{18,... | collective-permute-start | bytes 884744 | tf_op jit(solution)/shard_map/ppermute | solution.py:30
  42.8 22.7 %collective-permute-start.13 = (bf16[96,4608]{1,0:T(8,128)(2,1)S(1)}, bf16[96,4608]{1,0:T(8,128)(2,1)S(1)}, u32[]{:S(2)}, u32[]{:S(2)}) collective-permute-start(bf16[96,4608]{1,0:T(8,128)(2,1)S(1)} %bitcast.45), channel_id=1, source_target_pairs={{0,4},{2,6},{4,0},{6,2},{8,12},{10,14},{12,8},{14,10},{16,20},{18,... | collective-permute-start | bytes 2654216 | tf_op jit(solution)/shard_map/ppermute | solution.py:30
  44.1 23.5 %collective-permute-start.21 = (bf16[96,4608]{1,0:T(8,128)(2,1)S(1)}, bf16[96,4608]{1,0:T(8,128)(2,1)}, u32[]{:S(2)}, u32[]{:S(2)}) collective-permute-start(bf16[96,4608]{1,0:T(8,128)(2,1)S(1)} %bitcast.46), channel_id=1, source_target_pairs={{0,8},{2,10},{4,12},{6,14},{8,16},{10,18},{12,20},{14,22},{16,24},... | collective-permute-start | bytes 2654216 | tf_op jit(solution)/shard_map/ppermute | solution.py:35
  45.6 23.3 %collective-permute-start.10 = (bf16[256,1536]{1,0:T(8,128)(2,1)S(1)}, bf16[256,1536]{1,0:T(8,128)(2,1)S(1)}, u32[]{:S(2)}, u32[]{:S(2)}) collective-permute-start(bf16[256,1536]{1,0:T(8,128)(2,1)S(1)} %bitcast.49), channel_id=1, source_target_pairs={{1,0},{0,1},{3,2},{2,3},{5,4},{4,5},{7,6},{6,7},{9,8},{8,9},{11,10... | collective-permute-start | bytes 2359304 | tf_op jit(solution)/shard_map/ppermute | solution.py:704
  67.6 21.1 %collective-permute-start.22 = (bf16[96,4608]{1,0:T(8,128)(2,1)}, bf16[96,4608]{1,0:T(8,128)(2,1)}, u32[]{:S(2)}, u32[]{:S(2)}) collective-permute-start(bf16[96,4608]{1,0:T(8,128)(2,1)} %collective-permute-done.21.refs_10_), channel_id=1, source_target_pairs={{0,4},{2,6},{4,0},{6,2},{8,12},{10,14},{12,8},{14,10},{16,20},{18,... | collective-permute-start | bytes 2654216 | tf_op jit(solution)/shard_map/ppermute | solution.py:30
  68.8 22.6 %collective-permute-start.27 = (bf16[96,4608]{1,0:T(8,128)(2,1)}, bf16[96,4608]{1,0:T(8,128)(2,1)}, u32[]{:S(2)}, u32[]{:S(2)}) collective-permute-start(bf16[96,4608]{1,0:T(8,128)(2,1)} %collective-permute-done.21.refs_10_), channel_id=1, source_target_pairs={{0,8},{2,10},{4,12},{6,14},{8,16},{10,18},{12,20},{14,22},{16,24},... | collective-permute-start | bytes 2654216 | tf_op jit(solution)/shard_map/ppermute | solution.py:35
  69.7 22.5 %collective-permute-start.24 = (bf16[8,576,128]{2,1,0:T(8,128)(2,1)}, bf16[8,576,128]{2,1,0:T(8,128)(2,1)S(1)}, u32[]{:S(2)}, u32[]{:S(2)}) collective-permute-start(bf16[8,576,128]{2,1,0:T(8,128)(2,1)} %get-tuple-element.135), channel_id=1, source_target_pairs={{0,2},{2,0},{4,6},{6,4},{8,10},{10,8},{12,14},{14,12},{16,18},{18,... | collective-permute-start | bytes 3538952 | tf_op jit(solution)/shard_map/ppermute | solution.py:30
  69.7 24.0 %collective-permute-start.11 = (bf16[256,1536]{1,0:T(8,128)(2,1)S(1)}, bf16[256,1536]{1,0:T(8,128)(2,1)}, u32[]{:S(2)}, u32[]{:S(2)}) collective-permute-start(bf16[256,1536]{1,0:T(8,128)(2,1)S(1)} %bitcast.39), channel_id=1, source_target_pairs={{1,0},{0,1},{3,2},{2,3},{5,4},{4,5},{7,6},{6,7},{9,8},{8,9},{11,10... | collective-permute-start | bytes 2359304 | tf_op jit(solution)/shard_map/ppermute | solution.py:705
  91.4 19.9 %collective-permute-start.28 = (bf16[96,4608]{1,0:T(8,128)(2,1)}, bf16[96,4608]{1,0:T(8,128)(2,1)}, u32[]{:S(2)}, u32[]{:S(2)}) collective-permute-start(bf16[96,4608]{1,0:T(8,128)(2,1)} %collective-permute-done.27.refs_10_), channel_id=1, source_target_pairs={{0,4},{2,6},{4,0},{6,2},{8,12},{10,14},{12,8},{14,10},{16,20},{18,... | collective-permute-start | bytes 2654216 | tf_op jit(solution)/shard_map/ppermute | solution.py:30
  93.8 21.3 %collective-permute-start.32 = (bf16[96,4608]{1,0:T(8,128)(2,1)}, bf16[96,4608]{1,0:T(8,128)(2,1)}, u32[]{:S(2)}, u32[]{:S(2)}) collective-permute-start(bf16[96,4608]{1,0:T(8,128)(2,1)} %collective-permute-done.27.refs_10_), channel_id=1, source_target_pairs={{0,8},{2,10},{4,12},{6,14},{8,16},{10,18},{12,20},{14,22},{16,24},... | collective-permute-start | bytes 2654216 | tf_op jit(solution)/shard_map/ppermute | solution.py:35
  111.9 23.7 %collective-permute-start.33 = (bf16[96,4608]{1,0:T(8,128)(2,1)}, bf16[96,4608]{1,0:T(8,128)(2,1)}, u32[]{:S(2)}, u32[]{:S(2)}) collective-permute-start(bf16[96,4608]{1,0:T(8,128)(2,1)} %collective-permute-done.28.refs_11_), channel_id=1, source_target_pairs={{0,8},{2,10},{4,12},{6,14},{8,16},{10,18},{12,20},{14,22},{16,24},... | collective-permute-start | bytes 2654216 | tf_op jit(solution)/shard_map/ppermute | solution.py:35
  112.9 22.7 %collective-permute-start.43 = (bf16[4,576,128]{2,1,0:T(8,128)(2,1)S(1)}, bf16[4,576,128]{2,1,0:T(8,128)(2,1)}, u32[]{:S(2)}, u32[]{:S(2)}) collective-permute-start(bf16[4,576,128]{2,1,0:T(8,128)(2,1)S(1)} %fusion), channel_id=1, source_target_pairs={{0,4},{2,6},{4,0},{6,2},{8,12},{10,14},{12,8},{14,10},{16,20},{18,... | collective-permute-start | bytes 1769480 | tf_op jit(solution)/shard_map/ppermute | solution.py:30
  121.0 17.5 %collective-permute-start.34 = (bf16[96,4608]{1,0:T(8,128)(2,1)}, bf16[96,4608]{1,0:T(8,128)(2,1)}, u32[]{:S(2)}, u32[]{:S(2)}) collective-permute-start(bf16[96,4608]{1,0:T(8,128)(2,1)} %collective-permute-done.32.refs_10_), channel_id=1, source_target_pairs={{0,2},{2,0},{4,6},{6,4},{8,10},{10,8},{12,14},{14,12},{16,18},{18,... | collective-permute-start | bytes 2654216 | tf_op jit(solution)/shard_map/ppermute | solution.py:30
  136.9 14.8 %collective-permute-start.31 = (bf16[256,384]{1,0:T(8,128)(2,1)}, bf16[256,384]{1,0:T(8,128)(2,1)S(1)}, u32[]{:S(2)}, u32[]{:S(2)}) collective-permute-start(bf16[256,384]{1,0:T(8,128)(2,1)} %get-tuple-element.144), channel_id=1, source_target_pairs={{1,0},{0,1},{3,2},{2,3},{5,4},{4,5},{7,6},{6,7},{9,8},{8,9},{11,10... | collective-permute-start | bytes 589832 | tf_op jit(solution)/shard_map/ppermute | solution.py:748
  147.9 11.3 %collective-permute-start.45 = (bf16[1,576,128]{2,1,0:T(8,128)(2,1)S(1)}, bf16[1,576,128]{2,1,0:T(8,128)(2,1)S(1)}, u32[]{:S(2)}, u32[]{:S(2)}) collective-permute-start(bf16[1,576,128]{2,1,0:T(8,128)(2,1)S(1)} %dynamic-slice_convert_fusion.1), channel_id=1, source_target_pairs={{0,16},{2,18},{4,20},{6,22},{8,24},{10,26},{12,28},{14,30},{16,0},... | collective-permute-start | bytes 442376 | tf_op jit(solution)/shard_map/ppermute | solution.py:30
  149.0 10.1 %collective-permute-start.40 = (f32[3,1536]{1,0:T(4,128)S(1)}, f32[3,1536]{1,0:T(4,128)S(1)}, u32[]{:S(2)}, u32[]{:S(2)}) collective-permute-start(f32[3,1536]{1,0:T(4,128)S(1)} %add_add_fusion), channel_id=1, source_target_pairs={{0,8},{2,10},{4,12},{6,14},{8,16},{10,18},{12,20},{14,22},{16,24},... | collective-permute-start | bytes 55304 | tf_op jit(solution)/shard_map/ppermute | solution.py:596
  (52 other events, 305.1 us)

commit v5 on v4

--- a/solution.py
+++ b/solution.py
@@ -749,7 +749,6 @@
     event = low_grad_in
     qkv_r.append(ring_shifted(gate(qkv_r[1], event)))
     qkv_x.append(across(gate(qkv_r[1], event)))
-    qkv_rc.append(beside(gate(qkv_r[1], event)))
     qkv_xc.append(beside(gate(qkv_x[0], event)))
     arrived = beside(sent)
     layers = [[[qkv_r[0]], [qkv_x[0]], [qkv_rc[0]], [qkv_xc[0]]]]
@@ -757,13 +756,14 @@
     u0, table = project(0, qkv_xc[0], next_input)
     qkv_r.append(ring_shifted(gate(qkv_r[2], u0)))
     qkv_x.append(across(gate(qkv_r[2], u0)))
-    qkv_rc.append(beside(gate(qkv_r[2], u0)))
+    qkv_rc.append(beside(gate(qkv_r[1], u0)))
     qkv_xc.append(beside(gate(qkv_x[1], u0)))
     kept, sent = halved(kept + gate(arrived, u0).astype(F32), 2)
     received = [sends(u0)]
     layers.append([[qkv_r[1]], [qkv_x[1]], [qkv_rc[1]], [qkv_xc[1]]])
     u1, table = project(1, qkv_xc[1], sent, received[0], next_cot)
     rest = [ring_shifted(gate(qkv_x[2], u1))]
+    qkv_rc.append(beside(gate(qkv_r[2], u1)))
     qkv_rc.append(beside(gate(qkv_r[3], u1)))
     qkv_xc.append(beside(gate(qkv_x[2], u1)))
     arrived = across(gate(sent, u1))

time: 161 us -> 161 us (level)
  no operation moved by 1% of the time
where the time goes in v5:
time: 161 us
  Pallas kernels  69.2 us (43%)
  waiting for transfers between devices  42.9 us (27%)
  starting transfers between devices  34.2 us (21%)
  local copies, waits for them, and re-layouts  8.94 us (6%)
  other arithmetic  4.41 us (3%)
    pallas_call x12, Pallas kernels, call(): pl.pallas_call(kernel, out_shape=outs, in_specs=[pl.BlockSpec(memory_spac...  69.2 us
    ppermute x30, waiting for transfers between devices, swapped(): return lax.ppermute(block, 'dp', [(i, i ^ bit) for i in devices])  20.5 us
    ppermute x7, waiting for transfers between devices, ring_shifted(): lax.ppermute(block, 'dp', [(i, (i + 4) % count) for i in range(count)])  14.3 us
    ppermute x30, starting transfers between devices, swapped(): return lax.ppermute(block, 'dp', [(i, i ^ bit) for i in devices])  13.4 us
    ppermute x4, waiting for transfers between devices, on_device(): sends = lambda u: lax.ppermute(u, 'pipe', before)  7.88 us
    ppermute x7, starting transfers between devices, ring_shifted(): lax.ppermute(block, 'dp', [(i, (i + 4) % count) for i in range(count)])  7.68 us
    unnamed x62, local copies, waits for them, and re-layouts  7.45 us
    ppermute x4, starting transfers between devices, on_device(): sends = lambda u: lax.ppermute(u, 'pipe', before)  5.12 us
  transfers between devices with their start and end apart: 46, of which 18 were waited for; matrix products, arithmetic and copies ran while one was open for 4% of the time, Pallas kernels for 43%

profile of v5, /device:TPU:0, one launch (start us, length us, event | category | flops | bytes accessed | tf_op | source)
XLA Modules:
  0.0 160.8 jit_solution(16415593766740137689)
XLA Ops:
  0.6 3.1 %collective-permute-start = (bf16[96,1536]{1,0:T(8,128)(2,1)}, bf16[96,1536]{1,0:T(8,128)(2,1)S(1)}, u32[]{:S(2)}, u32[]{:S(2)}) collective-permute-start(bf16[96,1536]{1,0:T(8,128)(2,1)} %bitcast.51), channel_id=1, source_target_pairs={{0,8},{2,10},{4,12},{6,14},{8,16},{10,18},{12,20},{14,22},{16,24},... | collective-permute-start | bytes 884744 | tf_op jit(solution)/shard_map/ppermute | solution.py:35
  7.1 5.3 %modulate.1 = (bf16[256,1536]{1,0:T(8,128)(2,1)}, bf16[256,1536]{1,0:T(8,128)(2,1)}, f32[256,1536]{1,0:T(8,128)}, f32[256,1536]{1,0:T(8,128)}, bf16[256,128]{1,0:T(8,128)(2,1)}, /*index=5*/bf16[256,128]{1,0:T(8,128)(2,1)}) custom-call(s32[3]{0:T(128)} %pad_add_fusion.place_ref.refs_0_, s32[1,8]{1,0:T(1,128)} %frames_ref.3, s32[1,8]{1,0:T(1,128)} %sizes_ref.3, ...), custom_call_target="tpu_custom_call" | custom-call | bytes 4000000 | tf_op jit(solution)/shard_map/modulate/pallas_call | solution.py:568
  15.1 7.9 %attend.1 = (bf16[256,1536]{1,0:T(8,128)(2,1)}, bf16[256,128]{1,0:T(8,128)(2,1)}, f32[1,1536]{1,0:T(1,128)}, f32[1536,128]{1,0:T(8,128)}, f32[1536,128]{1,0:T(8,...) custom-call(s32[3]{0:T(128)} %pad_add_fusion.place_ref.refs_0_, s32[1,8]{1,0:T(1,128)} %frames_ref.3, s32[1,8]{1,0:T(1,128)} %sizes_ref.3, ...), custom_call_target="tpu_custom_call" | custom-call | bytes 6000000 | tf_op jit(solution)/shard_map/attend/pallas_call | solution.py:568
  23.1 1.6 %collective-permute-start.3 = (bf16[96,1536]{1,0:T(8,128)(2,1)S(1)}, bf16[96,1536]{1,0:T(8,128)(2,1)S(1)}, u32[]{:S(2)}, u32[]{:S(2)}) collective-permute-start(bf16[96,1536]{1,0:T(8,128)(2,1)S(1)} %collective-permute-done.1.refs_12_), channel_id=1, source_target_pairs={{0,8},{2,10},{4,12},{6,14},{8,16},{10,18},{12,20},{14,22},{16,24},... | collective-permute-start | bytes 884744 | tf_op jit(solution)/shard_map/ppermute | solution.py:35
  27.2 6.1 %backward0.1 = (bf16[256,1152]{1,0:T(8,128)(2,1)}, f32[1152,128]{1,0:T(8,128)}, f32[1,1536]{1,0:T(1,128)}, f32[256,128]{1,0:T(8,128)}) custom-call(s32[3]{0:T(128)} %pad_add_fusion.place_ref.refs_0_, bf16[256,128]{1,0:T(8,128)(2,1)} %get-tuple-element.85.low_grad_ref.refs_1_, bf16[256,128]{1,0:T(8,128)(2,1)} %get-tuple-element.82.refs_2_, ...), custom_call_target="tpu_custom_call" | custom-call | bytes 5000000 | tf_op jit(solution)/shard_map/backward0/pallas_call | solution.py:568
  36.3 6.3 %backward1.1 = (bf16[256,1152]{1,0:T(8,128)(2,1)}, f32[1152,128]{1,0:T(8,128)}, f32[1,1536]{1,0:T(1,128)}, f32[256,128]{1,0:T(8,128)}) custom-call(s32[3]{0:T(128)} %pad_add_fusion.place_ref.refs_0_, bf16[256,128]{1,0:T(8,128)(2,1)} %get-tuple-element.85.low_grad_ref.refs_1_, bf16[256,128]{1,0:T(8,128)(2,1)} %get-tuple-element.82.refs_2_, ...), custom_call_target="tpu_custom_call" | custom-call | bytes 5000000 | tf_op jit(solution)/shard_map/backward1/pallas_call | solution.py:568
  47.1 6.1 %backward2.1 = (bf16[256,1152]{1,0:T(8,128)(2,1)}, f32[1152,128]{1,0:T(8,128)}, f32[1,1536]{1,0:T(1,128)}, f32[256,128]{1,0:T(8,128)}) custom-call(s32[3]{0:T(128)} %pad_add_fusion.place_ref.refs_0_, bf16[256,128]{1,0:T(8,128)(2,1)} %get-tuple-element.85.low_grad_ref.refs_1_, bf16[256,128]{1,0:T(8,128)(2,1)} %get-tuple-element.82.refs_2_, ...), custom_call_target="tpu_custom_call" | custom-call | bytes 5000000 | tf_op jit(solution)/shard_map/backward2/pallas_call | solution.py:568
  54.1 6.1 %backward3.1 = (bf16[256,1152]{1,0:T(8,128)(2,1)}, f32[1152,128]{1,0:T(8,128)}, f32[1,1536]{1,0:T(1,128)}, f32[256,128]{1,0:T(8,128)}) custom-call(s32[3]{0:T(128)} %pad_add_fusion.place_ref.refs_0_, bf16[256,128]{1,0:T(8,128)(2,1)} %get-tuple-element.85.low_grad_ref.refs_1_, bf16[256,128]{1,0:T(8,128)(2,1)} %get-tuple-element.82.refs_2_, ...), custom_call_target="tpu_custom_call" | custom-call | bytes 5000000 | tf_op jit(solution)/shard_map/backward3/pallas_call | solution.py:568
  60.3 5.2 %adapt.1 = (bf16[256,128]{1,0:T(8,128)(2,1)}, bf16[8,576,128]{2,1,0:T(8,128)(2,1)}, f32[8,576,128]{2,1,0:T(8,128)}) custom-call(s32[3]{0:T(128)} %pad_add_fusion.place_ref.refs_0_, bf16[256,1536]{1,0:T(8,128)(2,1)} %get-tuple-element.105.refs_1_, f32[256,128]{1,0:T(8,128)} %get-tuple-element.114.refs_2_, f32[1536,128]{1,0:T(8,128)} %get-tuple-element.115.refs_3_, ...), custom_call_target="tpu_custom_call" | custom-call | bytes 4000000 | tf_op jit(solution)/shard_map/adapt/pallas_call | solution.py:568
  72.9 5.6 %project0.1 = (bf16[256,384]{1,0:T(8,128)(2,1)}, f32[3,1536]{1,0:T(4,128)}) custom-call(s32[3]{0:T(128)} %pad_add_fusion.place_ref.refs_0_, bf16[256,128]{1,0:T(8,128)(2,1)} %get-tuple-element.121.refs_1_, f32[3,1536]{1,0:T(4,128)} %concatenate.3.refs_2_, bf16[256,1152]{1,0:T(8,128)(2,1)} %get-tuple-element.125.refs_3_, ...), custom_call_target="tpu_custom_call" | custom-call | bytes 5000000 | tf_op jit(solution)/shard_map/project0/pallas_call | solution.py:568
  78.6 10.2 %collective-permute-done.22.refs_11_ = bf16[96,4608]{1,0:T(8,128)(2,1)} collective-permute-done((bf16[96,4608]{1,0:T(8,128)(2,1)}, bf16[96,4608]{1,0:T(8,128)(2,1)}, u32[]{:S(2)}, u32[]{:S(2)}) %collective-permute-start.22) | collective-permute-done | bytes 884768 | tf_op jit(solution)/shard_map/ppermute | solution.py:30
  89.2 2.2 %collective-permute-done.27.refs_10_ = bf16[96,4608]{1,0:T(8,128)(2,1)} collective-permute-done((bf16[96,4608]{1,0:T(8,128)(2,1)}, bf16[96,4608]{1,0:T(8,128)(2,1)}, u32[]{:S(2)}, u32[]{:S(2)}) %collective-permute-start.27) | collective-permute-done | bytes 884768 | tf_op jit(solution)/shard_map/ppermute | solution.py:35
  93.8 1.9 %convert_add_fusion = f32[8,576,128]{2,1,0:T(8,128)S(1)} fusion(f32[8,576,128]{2,1,0:T(8,128)} %get-tuple-element.136, bf16[8,576,128]{2,1,0:T(8,128)(2,1)S(1)} %collective-permute-done.24), kind=kLoop, calls=%fused_computation | loop fusion | flops 1179648 | bytes 5898240 | tf_op jit(solution)/shard_map/add | solution.py:761
  95.7 2.5 %collective-permute-done.20.refs_3_ = bf16[256,384]{1,0:T(8,128)(2,1)} collective-permute-done((bf16[256,384]{1,0:T(8,128)(2,1)}, bf16[256,384]{1,0:T(8,128)(2,1)}, u32[]{:S(2)}, u32[]{:S(2)}) %collective-permute-start.20) | collective-permute-done | bytes 196640 | tf_op jit(solution)/shard_map/ppermute | solution.py:748
  98.3 5.6 %project1.1 = (bf16[256,384]{1,0:T(8,128)(2,1)}, f32[3,1536]{1,0:T(4,128)}) custom-call(s32[3]{0:T(128)} %pad_add_fusion.place_ref.refs_0_, bf16[256,128]{1,0:T(8,128)(2,1)} %get-tuple-element.121.refs_1_, f32[3,1536]{1,0:T(4,128)} %get-tuple-element.140.refs_2_, bf16[256,1152]{1,0:T(8,128)(2,1)} %get-tuple-element.125.refs_3_, ...), custom_call_target="tpu_custom_call" | custom-call | bytes 5000000 | tf_op jit(solution)/shard_map/project1/pallas_call | solution.py:568
  103.9 7.5 %collective-permute-done.28.refs_11_ = bf16[96,4608]{1,0:T(8,128)(2,1)} collective-permute-done((bf16[96,4608]{1,0:T(8,128)(2,1)}, bf16[96,4608]{1,0:T(8,128)(2,1)}, u32[]{:S(2)}, u32[]{:S(2)}) %collective-permute-start.28) | collective-permute-done | bytes 884768 | tf_op jit(solution)/shard_map/ppermute | solution.py:30
  113.4 1.7 %collective-permute-done.32.refs_10_ = bf16[96,4608]{1,0:T(8,128)(2,1)} collective-permute-done((bf16[96,4608]{1,0:T(8,128)(2,1)}, bf16[96,4608]{1,0:T(8,128)(2,1)}, u32[]{:S(2)}, u32[]{:S(2)}) %collective-permute-start.32) | collective-permute-done | bytes 884768 | tf_op jit(solution)/shard_map/ppermute | solution.py:35
  115.6 5.4 %collective-permute-done.26.refs_4_ = bf16[256,384]{1,0:T(8,128)(2,1)S(1)} collective-permute-done((bf16[256,384]{1,0:T(8,128)(2,1)}, bf16[256,384]{1,0:T(8,128)(2,1)S(1)}, u32[]{:S(2)}, u32[]{:S(2)}) %collective-permute-start.26) | collective-permute-done | bytes 196640 | tf_op jit(solution)/shard_map/ppermute | solution.py:748
  122.2 5.7 %project2.1 = (bf16[256,384]{1,0:T(8,128)(2,1)}, f32[3,1536]{1,0:T(4,128)}) custom-call(s32[3]{0:T(128)} %pad_add_fusion.place_ref.refs_0_, bf16[256,128]{1,0:T(8,128)(2,1)} %get-tuple-element.121.refs_1_, f32[3,1536]{1,0:T(4,128)} %get-tuple-element.146.refs_2_, bf16[256,1152]{1,0:T(8,128)(2,1)} %get-tuple-element.125.refs_3_, ...), custom_call_target="tpu_custom_call" | custom-call | bytes 5000000 | tf_op jit(solution)/shard_map/project2/pallas_call | solution.py:568
  127.9 7.6 %collective-permute-done.33.refs_11_ = bf16[96,4608]{1,0:T(8,128)(2,1)} collective-permute-done((bf16[96,4608]{1,0:T(8,128)(2,1)}, bf16[96,4608]{1,0:T(8,128)(2,1)}, u32[]{:S(2)}, u32[]{:S(2)}) %collective-permute-start.33) | collective-permute-done | bytes 884768 | tf_op jit(solution)/shard_map/ppermute | solution.py:35
  138.5 5.7 %project3.1 = (bf16[256,384]{1,0:T(8,128)(2,1)}, f32[3,1536]{1,0:T(4,128)}) custom-call(s32[3]{0:T(128)} %pad_add_fusion.place_ref.refs_0_, bf16[256,128]{1,0:T(8,128)(2,1)} %get-tuple-element.121.refs_1_, f32[3,1536]{1,0:T(4,128)} %get-tuple-element.149.refs_2_, bf16[256,1152]{1,0:T(8,128)(2,1)} %get-tuple-element.125.refs_3_, ...), custom_call_target="tpu_custom_call" | custom-call | bytes 5000000 | tf_op jit(solution)/shard_map/project3/pallas_call | solution.py:568
  149.0 1.7 %collective-permute-start.40 = (f32[3,1536]{1,0:T(4,128)S(1)}, f32[3,1536]{1,0:T(4,128)S(1)}, u32[]{:S(2)}, u32[]{:S(2)}) collective-permute-start(f32[3,1536]{1,0:T(4,128)S(1)} %add_add_fusion), channel_id=1, source_target_pairs={{0,8},{2,10},{4,12},{6,14},{8,16},{10,18},{12,20},{14,22},{16,24},... | collective-permute-start | bytes 55304 | tf_op jit(solution)/shard_map/ppermute | solution.py:596
  151.7 2.2 %collective-permute-start.42 = (f32[3,1536]{1,0:T(4,128)S(1)}, f32[3,1536]{1,0:T(4,128)S(1)}, u32[]{:S(2)}, u32[]{:S(2)}) collective-permute-start(f32[3,1536]{1,0:T(4,128)S(1)} %add_add_fusion), channel_id=1, source_target_pairs={{0,24},{2,26},{4,28},{6,30},{8,0},{10,2},{12,4},{14,6},{16,8},{18,... | collective-permute-start | bytes 55304 | tf_op jit(solution)/shard_map/ppermute | solution.py:596
  154.6 3.6 %finish.1 = bf16[256,1536]{1,0:T(8,128)(2,1)} custom-call(s32[3]{0:T(128)} %pad_add_fusion.place_ref.refs_0_, bf16[256,1536]{1,0:T(8,128)(2,1)} %copy-done.8, bf16[256,1536]{1,0:T(8,128)(2,1)} %collective-permute-done.11.refs_2_, bf16[256,384]{1,0:T(8,128)(2,1)} %collective-permute-done.20.refs_3_, bf16[256,384]{1,0:T(8,128)(2,1)} %copy-done.25, ...), custom_call_target="tpu_custom_call" | custom-call | bytes 4000000 | tf_op jit(solution)/shard_map/finish/pallas_call | solution.py:568
  (154 shorter events, 43.0 us)
Async XLA Ops:
  0.6 12.3 %collective-permute-start = (bf16[96,1536]{1,0:T(8,128)(2,1)}, bf16[96,1536]{1,0:T(8,128)(2,1)S(1)}, u32[]{:S(2)}, u32[]{:S(2)}) collective-permute-start(bf16[96,1536]{1,0:T(8,128)(2,1)} %bitcast.51), channel_id=1, source_target_pairs={{0,8},{2,10},{4,12},{6,14},{8,16},{10,18},{12,20},{14,22},{16,24},... | collective-permute-start | bytes 884744 | tf_op jit(solution)/shard_map/ppermute | solution.py:35
  3.7 10.9 %collective-permute-start.2 = (bf16[96,1536]{1,0:T(8,128)(2,1)}, bf16[96,1536]{1,0:T(8,128)(2,1)S(1)}, u32[]{:S(2)}, u32[]{:S(2)}) collective-permute-start(bf16[96,1536]{1,0:T(8,128)(2,1)} %bitcast.52), channel_id=1, source_target_pairs={{0,4},{2,6},{4,0},{6,2},{8,12},{10,14},{12,8},{14,10},{16,20},{18,... | collective-permute-start | bytes 884744 | tf_op jit(solution)/shard_map/ppermute | solution.py:30
  13.0 10.1 %collective-permute-start.1 = (bf16[96,1536]{1,0:T(8,128)(2,1)S(1)}, bf16[96,1536]{1,0:T(8,128)(2,1)S(1)}, u32[]{:S(2)}, u32[]{:S(2)}) collective-permute-start(bf16[96,1536]{1,0:T(8,128)(2,1)S(1)} %collective-permute-done.refs_12_), channel_id=1, source_target_pairs={{0,8},{2,10},{4,12},{6,14},{8,16},{10,18},{12,20},{14,22},{16,24},... | collective-permute-start | bytes 884744 | tf_op jit(solution)/shard_map/ppermute | solution.py:35
  14.1 10.6 %collective-permute-start.5 = (bf16[96,1536]{1,0:T(8,128)(2,1)S(1)}, bf16[96,1536]{1,0:T(8,128)(2,1)S(1)}, u32[]{:S(2)}, u32[]{:S(2)}) collective-permute-start(bf16[96,1536]{1,0:T(8,128)(2,1)S(1)} %collective-permute-done.refs_12_), channel_id=1, source_target_pairs={{0,4},{2,6},{4,0},{6,2},{8,12},{10,14},{12,8},{14,10},{16,20},{18,... | collective-permute-start | bytes 884744 | tf_op jit(solution)/shard_map/ppermute | solution.py:30
  14.6 11.7 %collective-permute-start.6 = (bf16[96,1536]{1,0:T(8,128)(2,1)S(1)}, bf16[96,1536]{1,0:T(8,128)(2,1)S(1)}, u32[]{:S(2)}, u32[]{:S(2)}) collective-permute-start(bf16[96,1536]{1,0:T(8,128)(2,1)S(1)} %collective-permute-done.2.refs_13_), channel_id=1, source_target_pairs={{0,2},{2,0},{4,6},{6,4},{8,10},{10,8},{12,14},{14,12},{16,18},{18,... | collective-permute-start | bytes 884744 | tf_op jit(solution)/shard_map/ppermute | solution.py:30
  14.6 11.8 %collective-permute-start.7 = (bf16[96,1536]{1,0:T(8,128)(2,1)S(1)}, bf16[96,1536]{1,0:T(8,128)(2,1)S(1)}, u32[]{:S(2)}, u32[]{:S(2)}) collective-permute-start(bf16[96,1536]{1,0:T(8,128)(2,1)S(1)} %bitcast.54), channel_id=1, source_target_pairs={{0,2},{2,0},{4,6},{6,4},{8,10},{10,8},{12,14},{14,12},{16,18},{18,... | collective-permute-start | bytes 884744 | tf_op jit(solution)/shard_map/ppermute | solution.py:30
  23.1 10.9 %collective-permute-start.3 = (bf16[96,1536]{1,0:T(8,128)(2,1)S(1)}, bf16[96,1536]{1,0:T(8,128)(2,1)S(1)}, u32[]{:S(2)}, u32[]{:S(2)}) collective-permute-start(bf16[96,1536]{1,0:T(8,128)(2,1)S(1)} %collective-permute-done.1.refs_12_), channel_id=1, source_target_pairs={{0,8},{2,10},{4,12},{6,14},{8,16},{10,18},{12,20},{14,22},{16,24},... | collective-permute-start | bytes 884744 | tf_op jit(solution)/shard_map/ppermute | solution.py:35
  24.7 10.7 %collective-permute-start.8 = (bf16[96,1536]{1,0:T(8,128)(2,1)S(1)}, bf16[96,1536]{1,0:T(8,128)(2,1)S(1)}, u32[]{:S(2)}, u32[]{:S(2)}) collective-permute-start(bf16[96,1536]{1,0:T(8,128)(2,1)S(1)} %collective-permute-done.refs_12_), channel_id=1, source_target_pairs={{0,2},{2,0},{4,6},{6,4},{8,10},{10,8},{12,14},{14,12},{16,18},{18,... | collective-permute-start | bytes 884744 | tf_op jit(solution)/shard_map/ppermute | solution.py:30
  24.7 10.7 %collective-permute-start.4 = (bf16[96,1536]{1,0:T(8,128)(2,1)S(1)}, bf16[96,1536]{1,0:T(8,128)(2,1)S(1)}, u32[]{:S(2)}, u32[]{:S(2)}) collective-permute-start(bf16[96,1536]{1,0:T(8,128)(2,1)S(1)} %collective-permute-done.1.refs_12_), channel_id=1, source_target_pairs={{0,4},{2,6},{4,0},{6,2},{8,12},{10,14},{12,8},{14,10},{16,20},{18,... | collective-permute-start | bytes 884744 | tf_op jit(solution)/shard_map/ppermute | solution.py:30
  42.8 22.7 %collective-permute-start.13 = (bf16[96,4608]{1,0:T(8,128)(2,1)S(1)}, bf16[96,4608]{1,0:T(8,128)(2,1)S(1)}, u32[]{:S(2)}, u32[]{:S(2)}) collective-permute-start(bf16[96,4608]{1,0:T(8,128)(2,1)S(1)} %bitcast.45), channel_id=1, source_target_pairs={{0,4},{2,6},{4,0},{6,2},{8,12},{10,14},{12,8},{14,10},{16,20},{18,... | collective-permute-start | bytes 2654216 | tf_op jit(solution)/shard_map/ppermute | solution.py:30
  44.1 23.5 %collective-permute-start.21 = (bf16[96,4608]{1,0:T(8,128)(2,1)S(1)}, bf16[96,4608]{1,0:T(8,128)(2,1)}, u32[]{:S(2)}, u32[]{:S(2)}) collective-permute-start(bf16[96,4608]{1,0:T(8,128)(2,1)S(1)} %bitcast.46), channel_id=1, source_target_pairs={{0,8},{2,10},{4,12},{6,14},{8,16},{10,18},{12,20},{14,22},{16,24},... | collective-permute-start | bytes 2654216 | tf_op jit(solution)/shard_map/ppermute | solution.py:35
  45.6 23.3 %collective-permute-start.10 = (bf16[256,1536]{1,0:T(8,128)(2,1)S(1)}, bf16[256,1536]{1,0:T(8,128)(2,1)S(1)}, u32[]{:S(2)}, u32[]{:S(2)}) collective-permute-start(bf16[256,1536]{1,0:T(8,128)(2,1)S(1)} %bitcast.49), channel_id=1, source_target_pairs={{1,0},{0,1},{3,2},{2,3},{5,4},{4,5},{7,6},{6,7},{9,8},{8,9},{11,10... | collective-permute-start | bytes 2359304 | tf_op jit(solution)/shard_map/ppermute | solution.py:704
  67.6 21.1 %collective-permute-start.22 = (bf16[96,4608]{1,0:T(8,128)(2,1)}, bf16[96,4608]{1,0:T(8,128)(2,1)}, u32[]{:S(2)}, u32[]{:S(2)}) collective-permute-start(bf16[96,4608]{1,0:T(8,128)(2,1)} %collective-permute-done.21.refs_10_), channel_id=1, source_target_pairs={{0,4},{2,6},{4,0},{6,2},{8,12},{10,14},{12,8},{14,10},{16,20},{18,... | collective-permute-start | bytes 2654216 | tf_op jit(solution)/shard_map/ppermute | solution.py:30
  68.8 22.6 %collective-permute-start.27 = (bf16[96,4608]{1,0:T(8,128)(2,1)}, bf16[96,4608]{1,0:T(8,128)(2,1)}, u32[]{:S(2)}, u32[]{:S(2)}) collective-permute-start(bf16[96,4608]{1,0:T(8,128)(2,1)} %collective-permute-done.21.refs_10_), channel_id=1, source_target_pairs={{0,8},{2,10},{4,12},{6,14},{8,16},{10,18},{12,20},{14,22},{16,24},... | collective-permute-start | bytes 2654216 | tf_op jit(solution)/shard_map/ppermute | solution.py:35
  69.7 22.5 %collective-permute-start.24 = (bf16[8,576,128]{2,1,0:T(8,128)(2,1)}, bf16[8,576,128]{2,1,0:T(8,128)(2,1)S(1)}, u32[]{:S(2)}, u32[]{:S(2)}) collective-permute-start(bf16[8,576,128]{2,1,0:T(8,128)(2,1)} %get-tuple-element.137), channel_id=1, source_target_pairs={{0,2},{2,0},{4,6},{6,4},{8,10},{10,8},{12,14},{14,12},{16,18},{18,... | collective-permute-start | bytes 3538952 | tf_op jit(solution)/shard_map/ppermute | solution.py:30
  69.7 24.0 %collective-permute-start.11 = (bf16[256,1536]{1,0:T(8,128)(2,1)S(1)}, bf16[256,1536]{1,0:T(8,128)(2,1)}, u32[]{:S(2)}, u32[]{:S(2)}) collective-permute-start(bf16[256,1536]{1,0:T(8,128)(2,1)S(1)} %bitcast.39), channel_id=1, source_target_pairs={{1,0},{0,1},{3,2},{2,3},{5,4},{4,5},{7,6},{6,7},{9,8},{8,9},{11,10... | collective-permute-start | bytes 2359304 | tf_op jit(solution)/shard_map/ppermute | solution.py:705
  91.4 19.9 %collective-permute-start.28 = (bf16[96,4608]{1,0:T(8,128)(2,1)}, bf16[96,4608]{1,0:T(8,128)(2,1)}, u32[]{:S(2)}, u32[]{:S(2)}) collective-permute-start(bf16[96,4608]{1,0:T(8,128)(2,1)} %collective-permute-done.27.refs_10_), channel_id=1, source_target_pairs={{0,4},{2,6},{4,0},{6,2},{8,12},{10,14},{12,8},{14,10},{16,20},{18,... | collective-permute-start | bytes 2654216 | tf_op jit(solution)/shard_map/ppermute | solution.py:30
  93.8 21.3 %collective-permute-start.32 = (bf16[96,4608]{1,0:T(8,128)(2,1)}, bf16[96,4608]{1,0:T(8,128)(2,1)}, u32[]{:S(2)}, u32[]{:S(2)}) collective-permute-start(bf16[96,4608]{1,0:T(8,128)(2,1)} %collective-permute-done.27.refs_10_), channel_id=1, source_target_pairs={{0,8},{2,10},{4,12},{6,14},{8,16},{10,18},{12,20},{14,22},{16,24},... | collective-permute-start | bytes 2654216 | tf_op jit(solution)/shard_map/ppermute | solution.py:35
  111.9 23.7 %collective-permute-start.33 = (bf16[96,4608]{1,0:T(8,128)(2,1)}, bf16[96,4608]{1,0:T(8,128)(2,1)}, u32[]{:S(2)}, u32[]{:S(2)}) collective-permute-start(bf16[96,4608]{1,0:T(8,128)(2,1)} %collective-permute-done.28.refs_11_), channel_id=1, source_target_pairs={{0,8},{2,10},{4,12},{6,14},{8,16},{10,18},{12,20},{14,22},{16,24},... | collective-permute-start | bytes 2654216 | tf_op jit(solution)/shard_map/ppermute | solution.py:35
  112.9 22.7 %collective-permute-start.43 = (bf16[4,576,128]{2,1,0:T(8,128)(2,1)S(1)}, bf16[4,576,128]{2,1,0:T(8,128)(2,1)}, u32[]{:S(2)}, u32[]{:S(2)}) collective-permute-start(bf16[4,576,128]{2,1,0:T(8,128)(2,1)S(1)} %fusion), channel_id=1, source_target_pairs={{0,4},{2,6},{4,0},{6,2},{8,12},{10,14},{12,8},{14,10},{16,20},{18,... | collective-permute-start | bytes 1769480 | tf_op jit(solution)/shard_map/ppermute | solution.py:30
  121.0 17.5 %collective-permute-start.34 = (bf16[96,4608]{1,0:T(8,128)(2,1)}, bf16[96,4608]{1,0:T(8,128)(2,1)}, u32[]{:S(2)}, u32[]{:S(2)}) collective-permute-start(bf16[96,4608]{1,0:T(8,128)(2,1)} %collective-permute-done.32.refs_10_), channel_id=1, source_target_pairs={{0,2},{2,0},{4,6},{6,4},{8,10},{10,8},{12,14},{14,12},{16,18},{18,... | collective-permute-start | bytes 2654216 | tf_op jit(solution)/shard_map/ppermute | solution.py:30
  136.9 14.8 %collective-permute-start.31 = (bf16[256,384]{1,0:T(8,128)(2,1)}, bf16[256,384]{1,0:T(8,128)(2,1)S(1)}, u32[]{:S(2)}, u32[]{:S(2)}) collective-permute-start(bf16[256,384]{1,0:T(8,128)(2,1)} %get-tuple-element.148), channel_id=1, source_target_pairs={{1,0},{0,1},{3,2},{2,3},{5,4},{4,5},{7,6},{6,7},{9,8},{8,9},{11,10... | collective-permute-start | bytes 589832 | tf_op jit(solution)/shard_map/ppermute | solution.py:748
  147.9 11.3 %collective-permute-start.45 = (bf16[1,576,128]{2,1,0:T(8,128)(2,1)S(1)}, bf16[1,576,128]{2,1,0:T(8,128)(2,1)S(1)}, u32[]{:S(2)}, u32[]{:S(2)}) collective-permute-start(bf16[1,576,128]{2,1,0:T(8,128)(2,1)S(1)} %dynamic-slice_convert_fusion.1), channel_id=1, source_target_pairs={{0,16},{2,18},{4,20},{6,22},{8,24},{10,26},{12,28},{14,30},{16,0},... | collective-permute-start | bytes 442376 | tf_op jit(solution)/shard_map/ppermute | solution.py:30
  149.0 10.1 %collective-permute-start.40 = (f32[3,1536]{1,0:T(4,128)S(1)}, f32[3,1536]{1,0:T(4,128)S(1)}, u32[]{:S(2)}, u32[]{:S(2)}) collective-permute-start(f32[3,1536]{1,0:T(4,128)S(1)} %add_add_fusion), channel_id=1, source_target_pairs={{0,8},{2,10},{4,12},{6,14},{8,16},{10,18},{12,20},{14,22},{16,24},... | collective-permute-start | bytes 55304 | tf_op jit(solution)/shard_map/ppermute | solution.py:596
  (52 other events, 305.1 us)
